TPU v7x, 256 devices: a whole 4x4x8 slice. The times are simulated.
256 devices in a mesh: gx: 16 (over y, x), gy: 16 (over z, core).
Axes of the slice: x: 4, y: 4, z: 8, core: 2. Of those that a mesh axis runs over, the one named last changes fastest.
Arguments:
- thermal_anomaly: float32 [75, 128, 2048], P(None, 'gy', 'gx'), may hold values from -6 to 6
- saltiness_anomaly: float32 [75, 128, 2048], P(None, 'gy', 'gx'), may hold values from -6 to 6
- east_face_speed: float32 [75, 128, 2048], P(None, 'gy', 'gx'), may hold values from -3 to 3
- north_face_speed: float32 [75, 128, 2048], P(None, 'gy', 'gx'), may hold values from -3 to 3
- sea_elevation: float32 [128, 2048], P('gy', 'gx'), may hold values from -2 to 2
- water_land_flag: int32 [128, 2048], P('gy', 'gx'), may hold values 0 or 1
- bottom_layer_index: int32 [128, 2048], P('gy', 'gx'), may hold values from 18 to 75
Outputs:
- temperature_next: float32 [75, 128, 2048], P(None, 'gy', 'gx')
- salinity_next: float32 [75, 128, 2048], P(None, 'gy', 'gx')
- east_velocity_next: float32 [75, 128, 2048], P(None, 'gy', 'gx')
- north_velocity_next: float32 [75, 128, 2048], P(None, 'gy', 'gx')
- surface_next: float32 [128, 2048], P('gy', 'gx')
Inputs may be any that keep to these rules, and one draw needn't show every extreme that they name: `water_land_flag`: 1 marks an ocean column, 0 land. `bottom_layer_index`: levels of a column counted from the top; only used where water_land_flag is 1.
All inputs are finite; a program needn't handle non-finite values. No bound on the sum of `water_land_flag` on one device may be relied on, other than what follows from the above.
Results may differ from a plain program's by a relative error of at most 0.00002.
Values sent between devices are 32-bit elements; how exact they have to be, the bound alone decides.
A program may use at most 64 MiB of HBM per device.

v0:
```python
import functools

import jax
import jax.numpy as jnp
from jax import lax
from jax.experimental import pallas as pl
from jax.experimental.pallas import tpu as pltpu
from jax.sharding import PartitionSpec as P

MESH = pl.DeviceIdType.MESH
K = 75
NC = 5
LC = K // NC
SUBSTEPS = 8
ROWS = 8
LANES = 128

DT = 0.4
NU = 0.025
KAPPA = 0.01
DTT = 0.2
GRAVITY = 4.0
DB = DT / SUBSTEPS

AROUND = [(dx, dy) for dy in (-1, 0, 1) for dx in (-1, 0, 1) if (dx, dy) != (0, 0)]
CORNERS = [(dx, dy) for dx, dy in AROUND if dx != 0 and dy != 0]


class Wires:
    def __init__(self, send, recv, gx, gy, nx, ny):
        self.send, self.recv = send, recv
        self.gx, self.gy, self.nx, self.ny = gx, gy, nx, ny
        self.used = 0

    def slots(self, count=1):
        first = self.used
        self.used += count
        return first

    def device(self, dx, dy):
        return (lax.rem(self.gx + dx + self.nx, self.nx), lax.rem(self.gy + dy + self.ny, self.ny))

    def copy(self, src, dst, slot, dx, dy):
        return pltpu.make_async_remote_copy(
            src_ref=src,
            dst_ref=dst,
            send_sem=self.send.at[slot],
            recv_sem=self.recv.at[slot],
            device_id=self.device(dx, dy),
            device_id_type=MESH,
        )


N_WIRES = 128


def kernel(
    nx,
    ny,
    t_in,
    s_in,
    u_in,
    v_in,
    h_in,
    flag_in,
    bottom_in,
    t_out,
    s_out,
    u_out,
    v_out,
    h_out,
    X,
    D2,
    flag_v,
    bottom_v,
    CU,
    CV,
    CC,
    PC,
    pack,
    PE,
    PW,
    F2,
    DV,
    U1B,
    V1X,
    pu1,
    PU1,
    AX,
    packa,
    QE,
    QW,
    UN,
    VN,
    TN,
    SN,
    HN,
    load_sem,
    send_sem,
    recv_sem,
    out_sem,
):
    gx, gy = lax.axis_index("gx"), lax.axis_index("gy")
    wires = Wires(send_sem, recv_sem, gx, gy, nx, ny)
    sent = []

    loads = [
        pltpu.make_async_copy(h_in, D2.at[1, 1, pl.ds(8, 8), :], load_sem.at[4]),
        pltpu.make_async_copy(flag_in, flag_v, load_sem.at[5]),
        pltpu.make_async_copy(bottom_in, bottom_v, load_sem.at[6]),
        pltpu.make_async_copy(u_in, X.at[0, :, pl.ds(8, 8), :], load_sem.at[0]),
        pltpu.make_async_copy(v_in, X.at[1, :, pl.ds(8, 8), :], load_sem.at[1]),
        pltpu.make_async_copy(t_in, X.at[2, :, pl.ds(8, 8), :], load_sem.at[2]),
        pltpu.make_async_copy(s_in, X.at[3, :, pl.ds(8, 8), :], load_sem.at[3]),
    ]
    for load in loads:
        load.start()

    barrier = pltpu.get_barrier_semaphore()
    for dx, dy in AROUND:
        pl.semaphore_signal(barrier, inc=1, device_id=wires.device(dx, dy), device_id_type=MESH)

    lane = lax.broadcasted_iota(jnp.int32, (ROWS, LANES), 1)
    lane4 = lax.rem(lane, 4)
    lane_group = lax.div(lane, 4).astype(jnp.float32)
    row = lax.broadcasted_iota(jnp.int32, (ROWS, LANES), 0)
    first, last = lane == 0, lane == LANES - 1
    low2, at1, at2 = lane4 < 2, lane4 == 1, lane4 == 2
    has_south, has_north = gy > 0, gy < ny - 1

    def roll(x, shift):
        return pltpu.roll(x, shift % LANES, 1)

    def east(x, halo):
        return roll(jnp.where(first, halo, x), LANES - 1)

    def west(x, halo):
        return roll(jnp.where(last, halo, x), 1)

    def unpacked(packed, i):
        return roll(packed, LANES - 2 - 4 * i)

    @pl.when(jnp.logical_not(has_south))
    def _():
        AX[:, :, 6:8, :] = jnp.zeros((2, K, 2, LANES), jnp.float32)

    @pl.when(jnp.logical_not(has_north))
    def _():
        AX[:, :, 16:18, :] = jnp.zeros((2, K, 2, LANES), jnp.float32)

    for load in loads[:3]:
        load.wait()
    D2[0, 1, 8:16, :] = (flag_v[...] * bottom_v[...]).astype(jnp.float32)

    pl.semaphore_wait(barrier, len(AROUND))

    def spread(src, dst_of):
        copies = []
        for dx, dy in AROUND:
            copy = wires.copy(src, dst_of(1 - dx, 8 * (1 - dy)), wires.slots(), dx, dy)
            copy.start()
            copies.append(copy)
        sent.extend(copies)
        return copies

    got_d2 = spread(
        D2.at[:, 1, pl.ds(8, 8), :], lambda tile, r: D2.at[:, tile, pl.ds(r, 8), :]
    )

    for load in loads[3:]:
        load.wait()
    uv_slot = wires.slots(2 * NC)
    ts_slot = wires.slots(2 * NC)

    def uv_copy(c, up):
        src, dst, dy = (14, 6, 1) if up else (8, 16, -1)
        levels = pl.ds(c * LC, LC)
        return wires.copy(
            X.at[pl.ds(0, 2), levels, pl.ds(src, 2), :],
            X.at[pl.ds(0, 2), levels, pl.ds(dst, 2), :],
            uv_slot + 2 * c + int(up),
            0,
            dy,
        )

    def ts_copy(c, up):
        src, dst, dy = (15, 7, 1) if up else (8, 16, -1)
        levels = pl.ds(c * LC, LC)
        return wires.copy(
            X.at[pl.ds(2, 2), levels, pl.ds(src, 1), :],
            X.at[pl.ds(2, 2), levels, pl.ds(dst, 1), :],
            ts_slot + 2 * c + int(up),
            0,
            dy,
        )

    @pl.loop(0, NC)
    def _(c):
        for up in (True, False):
            uv_copy(c, up).start()
            ts_copy(c, up).start()

    @pl.loop(0, NC)
    def _(c):
        for f in range(4):
            held = jnp.zeros((ROWS, LANES), jnp.float32)
            for i in range(LC):
                edge = roll(X[f, c * LC + i, 8:16, :], 4 * i + 2)
                held = jnp.where(lane_group == i, edge, held)
            pack[f, c] = held

    got_packs = []

    def side_packs(src, to_east, to_west, corners):
        copies = [
            wires.copy(src, to_east, wires.slots(), 1, 0),
            wires.copy(src, to_west, wires.slots(), -1, 0),
        ]
        for dx, dy, corner_src, corner_dst in corners:
            copies.append(wires.copy(corner_src, corner_dst, wires.slots(), dx, dy))
        for copy in copies:
            copy.start()
        sent.extend(copies)
        return copies

    def corner_copies(src, west_side, east_side):
        out = []
        for dx, dy in CORNERS:
            side = west_side if dx > 0 else east_side
            r_src, r_dst = (7, 0) if dy > 0 else (0, 9)
            out.append(
                (dx, dy, src.at[:, :, pl.ds(r_src, 1), :], side.at[:, :, pl.ds(r_dst, 1), :])
            )
        return out

    uv_pack = pack.at[pl.ds(0, 2)]
    got_packs = side_packs(
        pack,
        PW.at[:, :, pl.ds(1, 8), :],
        PE.at[:, :, pl.ds(1, 8), :],
        corner_copies(uv_pack, PW.at[pl.ds(0, 2)], PE.at[pl.ds(0, 2)]),
    )

    for copy in got_d2:
        copy.wait_recv()
    row24 = lax.broadcasted_iota(jnp.int32, (24, LANES), 0)
    lane24 = lax.broadcasted_iota(jnp.int32, (24, LANES), 1)
    first24, last24 = lane24 == 0, lane24 == LANES - 1
    inside = jnp.logical_and(
        jnp.logical_or(row24 >= 8, has_south), jnp.logical_or(row24 < 16, has_north)
    )

    def ring_east(c, h):
        return (
            roll(jnp.where(first24, h, c), LANES - 1),
            roll(jnp.where(first24, c, h), LANES - 1),
        )

    def ring_west(c, h):
        return (
            roll(jnp.where(last24, h, c), 1),
            roll(jnp.where(last24, c, h), 1),
        )

    def north24(x):
        return pltpu.roll(x, 23, 0)

    def south24(x):
        return pltpu.roll(x, 1, 0)

    def sides(ref, f):
        return ref[f, 1], jnp.where(lane24 < 64, ref[f, 2], ref[f, 0])

    col = [jnp.where(inside, x, 0.0) for x in sides(D2, 0)]
    ocean = [x > 0.0 for x in col]
    level0 = [jnp.where(o, x, 0.0) for o, x in zip(ocean, sides(D2, 1))]
    cu = [jnp.minimum(a, b) for a, b in zip(col, ring_east(*col))]
    cv = [jnp.minimum(a, north24(a)) for a in col]

    def depth(c):
        return c * (0.5 / K + c * (0.5 / (K * K)))

    CC[...] = col[0]
    CU[...] = cu[0]
    CV[...] = cv[0]

    def four(x):
        edge = [jnp.broadcast_to(x[:, l : l + 1], x.shape) for l in (126, 127, 0, 1)]
        l4 = lax.rem(lax.broadcasted_iota(jnp.int32, x.shape, 1), 4)
        return jnp.where(l4 < 2, jnp.where(l4 == 0, edge[0], edge[1]), jnp.where(l4 == 2, edge[2], edge[3]))

    PC[0] = four(col[1])
    PC[1] = four(cu[1])
    PC[2] = four(cv[1])
    col_own4 = four(col[0][8:16])

    def start_sums(c, carry):
        su, sv = carry
        base = (c * LC).astype(jnp.float32)
        cu0, cv0 = CU[8:16, :] - base, CV[8:16, :] - base
        for i in range(LC):
            dz = 0.5 / K + (base + (i + 0.5)) * (1.0 / (K * K))
            su = su + jnp.where(cu0 > i, X[0, c * LC + i, 8:16, :], 0.0) * dz
            sv = sv + jnp.where(cv0 > i, X[1, c * LC + i, 8:16, :], 0.0) * dz
        return su, sv

    zero = jnp.zeros((ROWS, LANES), jnp.float32)
    start_u, start_v = lax.fori_loop(0, NC, start_sums, (zero, zero))
    F2[0, 1, 8:16, :] = start_u
    F2[1, 1, 8:16, :] = start_v
    got_start = spread(
        F2.at[pl.ds(0, 2), 1, pl.ds(8, 8), :],
        lambda tile, r: F2.at[pl.ds(0, 2), tile, pl.ds(r, 8), :],
    )

    for copy in got_packs:
        copy.wait_recv()
    at_wall = jnp.where(
        jnp.logical_or(
            jnp.logical_and(row == 0, jnp.logical_not(has_south)),
            jnp.logical_and(row == ROWS - 1, jnp.logical_not(has_north)),
        ),
        19.0,
        20.0,
    )
    latitude = (row + gy * ROWS).astype(jnp.float32)
    f4 = (0.25 * DT) * (0.2 + 0.3 * (latitude + 0.5) / (ROWS * ny))
    centre_uv = 1.0 - (DT * NU) * at_wall
    centre_ts = 1.0 - KAPPA * at_wall

    v1_slot = wires.slots(NC)

    def v1_copy(c):
        levels = pl.ds(c * LC, LC)
        return wires.copy(
            V1X.at[levels, pl.ds(15, 1), :], V1X.at[levels, pl.ds(7, 1), :], v1_slot + c, 0, 1
        )

    def edge_terms(a, y):
        return (
            2.0 * y
            - 8.0 * a
            + jnp.where(at2, roll(a, LANES - 1), roll(a, 1))
        )

    def spread_terms(a, y, halo_a, halo_q):
        z = 2.0 * y - 8.0 * a
        return east(z + east(a, halo_a), halo_q) + west(z + west(a, halo_a), halo_q)

    def weight(t, s, dz):
        return (0.8 * s - t * (0.2 + 0.05 * t)) * dz

    def momentum(c, carry):
        cum_e, cum_n, sum_u, sum_v = carry
        for up in (True, False):
            uv_copy(c, up).wait_recv()
            ts_copy(c, up).wait_recv()
        base = (c * LC).astype(jnp.float32)
        packed_level = lane_group + base
        dz_packed = DT * (0.5 / K + (packed_level + 0.5) * (1.0 / (K * K)))

        def halo(f, depths, r):
            raw = jnp.where(low2, PW[f, c, r : r + 8, :], PE[f, c, r : r + 8, :])
            return jnp.where(packed_level < PC[depths, r + 7 : r + 15, :], raw, 0.0)

        us, uc, un = [halo(0, 1, r) for r in range(3)]
        vs, vc, vn = [halo(1, 2, r) for r in range(3)]
        pack_uq = edge_terms(uc, un + us)
        pack_vq = edge_terms(vc, vn + vs)
        pack_cross = jnp.where(at1, uc + un, vc + vs)
        pack_w = weight(halo(2, 0, 1), halo(3, 0, 1), dz_packed)

        cu5 = [CU[r : r + 8, :] - base for r in range(6, 11)]
        cv5 = [CV[r : r + 8, :] - base for r in range(6, 11)]
        cc0, ccn = CC[8:16, :] - base, CC[9:17, :] - base
        held = zero
        for i in range(LC):
            k = c * LC + i
            dz = 0.5 / K + (base + (i + 0.5)) * (1.0 / (K * K))
            uss, us, u, un, unn = [
                jnp.where(cu5[r] > i, X[0, k, r + 6 : r + 14, :], 0.0) for r in range(5)
            ]
            vss, vs, v, vn, vnn = [
                jnp.where(cv5[r] > i, X[1, k, r + 6 : r + 14, :], 0.0) for r in range(5)
            ]
            w = weight(
                jnp.where(cc0 > i, X[2, k, 8:16, :], 0.0),
                jnp.where(cc0 > i, X[3, k, 8:16, :], 0.0),
                DT * dz,
            )
            wn = weight(
                jnp.where(ccn > i, X[2, k, 9:17, :], 0.0),
                jnp.where(ccn > i, X[3, k, 9:17, :], 0.0),
                DT * dz,
            )
            step_e = east(w, unpacked(pack_w, i)) - w
            step_n = wn - w
            cum_e = cum_e + step_e
            cum_n = cum_n + step_n
            cross = unpacked(pack_cross, i)
            uu = u + un
            vv = v + vs
            uu = uu + west(uu, cross)
            vv = vv + east(vv, cross)
            yu, yv = un + us, vn + vs
            far_u = unn + uss + spread_terms(u, yu, unpacked(uc, i), unpacked(pack_uq, i))
            far_v = vnn + vss + spread_terms(v, yv, unpacked(vc, i), unpacked(pack_vq, i))
            u1 = centre_uv * u + (8.0 * DT * NU) * yu + f4 * vv - (cum_e - 0.5 * step_e) - (DT * NU) * far_u
            v1 = centre_uv * v + (8.0 * DT * NU) * yv - f4 * uu - (cum_n - 0.5 * step_n) - (DT * NU) * far_v
            u1 = jnp.where(cu5[2] > i, u1, 0.0)
            v1 = jnp.where(cv5[2] > i, v1, 0.0)
            sum_u = sum_u + u1 * dz
            sum_v = sum_v + v1 * dz
            U1B[k] = u1
            V1X[k, 8:16, :] = v1
            held = jnp.where(lane_group == i, roll(u1, 4 * i + 2), held)
        pu1[c] = held
        v1_copy(c).start()
        return cum_e, cum_n, sum_u, sum_v

    _, _, total_u, total_v = lax.fori_loop(0, NC, momentum, (zero, zero, zero, zero))

    F2[2, 1, 8:16, :] = total_u
    F2[3, 1, 8:16, :] = total_v
    got_total = spread(
        F2.at[pl.ds(2, 2), 1, pl.ds(8, 8), :],
        lambda tile, r: F2.at[pl.ds(2, 2), tile, pl.ds(r, 8), :],
    )
    pu1_copy = wires.copy(pu1, PU1, wires.slots(), 1, 0)
    pu1_copy.start()
    sent.append(pu1_copy)
    for copy in got_start + got_total:
        copy.wait_recv()

    def both(op, *pairs):
        return [op(*xs) for xs in zip(*pairs)]

    u0, v0, u_all, v_all = [list(sides(F2, f)) for f in range(4)]
    open_u = [(x > 0.0).astype(jnp.float32) for x in cu]
    open_v = [(x > 0.0).astype(jnp.float32) for x in cv]
    depth_u = both(depth, cu)
    depth_v = both(depth, cv)
    pull_u = both(lambda o, d: o * d * (DB * GRAVITY), open_u, depth_u)
    pull_v = both(lambda o, d: o * d * (DB * GRAVITY), open_v, depth_v)
    push_u = both(lambda o, a, b: o * ((a - b) * (DB / DT)), open_u, u_all, u0)
    push_v = both(lambda o, a, b: o * ((a - b) * (DB / DT)), open_v, v_all, v0)
    trans_u = both(lambda o, a: o * a, open_u, u0)
    trans_v = both(lambda o, a: o * a, open_v, v0)
    ease = both(lambda o: jnp.where(o, DB, 0.0), ocean)
    level = level0
    run_u = [jnp.zeros((24, LANES), jnp.float32)] * 2
    run_v = run_u
    for _ in range(SUBSTEPS):
        trans_u = both(
            lambda t, p, q, e, h: t + (p - q * (e - h)), trans_u, push_u, pull_u, ring_east(*level), level
        )
        trans_v = both(
            lambda t, p, q, h: t + (p - q * (north24(h) - h)), trans_v, push_v, pull_v, level
        )
        level = both(
            lambda h, e, u, w, v: h - e * ((u - w) + (v - south24(v))),
            level,
            ease,
            trans_u,
            ring_west(*trans_u),
            trans_v,
        )
        run_u = both(jnp.add, run_u, trans_u)
        run_v = both(jnp.add, run_v, trans_v)

    HN[...] = level[0][8:16]
    h_copy = pltpu.make_async_copy(HN, h_out, out_sem.at[4])
    h_copy.start()
    shift_u = both(
        lambda r, a, d, o: (r * (1.0 / SUBSTEPS) - a) / (d + (1.0 - o)), run_u, u_all, depth_u, open_u
    )
    shift_v = (run_v[0] * (1.0 / SUBSTEPS) - v_all[0]) / (depth_v[0] + (1.0 - open_v[0]))
    DV[...] = shift_v
    du = shift_u[0][8:16]
    dv = shift_v[8:16]
    dvs = DV[7:15, :]
    du_west = jnp.broadcast_to(shift_u[1][8:16, LANES - 1 : LANES], (ROWS, LANES))

    a_slot = wires.slots(2 * NC)

    def a_copy(c, up):
        src, dst, dy = (14, 6, 1) if up else (8, 16, -1)
        levels = pl.ds(c * LC, LC)
        return wires.copy(
            AX.at[:, levels, pl.ds(src, 2), :],
            AX.at[:, levels, pl.ds(dst, 2), :],
            a_slot + 2 * c + int(up),
            0,
            dy,
        )

    pu1_copy.wait_recv()

    @pl.loop(0, NC)
    def _(c):
        v1_copy(c).wait_recv()
        base = (c * LC).astype(jnp.float32)
        packed_level = lane_group + base

        u_edge = jnp.where(packed_level < PC[1, 8:16, :], PU1[c] + du_west, 0.0) * (0.5 * DTT)
        edges = []
        for f in (2, 3):
            raw = jnp.where(low2, PW[f, c, 1:9, :], PE[f, c, 1:9, :])
            c_halo = jnp.where(packed_level < PC[0, 8:16, :], raw, 0.0)
            c_own = jnp.where(packed_level < col_own4, pack[f, c], 0.0)
            flux = u_edge * (c_halo + roll(c_own, LANES - 1))
            edges.append(jnp.where(at1, flux, c_halo))

        ccs, cc0, ccn = [CC[r : r + 8, :] - base for r in (7, 8, 9)]
        cu0 = CU[8:16, :] - base
        cvs, cv0 = CV[7:15, :] - base, CV[8:16, :] - base
        held = [zero, zero]
        for i in range(LC):
            k = c * LC + i
            u = jnp.where(cu0 > i, U1B[k] + du, 0.0)
            v = jnp.where(cv0 > i, V1X[k, 8:16, :] + dv, 0.0)
            vs = jnp.where(cvs > i, V1X[k, 7:15, :] + dvs, 0.0) * (0.5 * DTT)
            UN[k] = u
            VN[k] = v
            u = u * (0.5 * DTT)
            v = v * (0.5 * DTT)
            for f in range(2):
                here = jnp.where(cc0 > i, X[2 + f, k, 8:16, :], 0.0)
                north = jnp.where(ccn > i, X[2 + f, k, 9:17, :], 0.0)
                south = jnp.where(ccs > i, X[2 + f, k, 7:15, :], 0.0)
                edge = unpacked(edges[f], i)
                flux_e = u * (here + east(here, edge))
                a = here - (
                    (flux_e - west(flux_e, edge)) + (v * (here + north) - vs * (here + south))
                )
                a = jnp.where(cc0 > i, a, 0.0)
                AX[f, k, 8:16, :] = a
                held[f] = jnp.where(lane_group == i, roll(a, 4 * i + 2), held[f])
        packa[0, c] = held[0]
        packa[1, c] = held[1]

        @pl.when(has_north)
        def _():
            a_copy(c, True).start()

        @pl.when(has_south)
        def _():
            a_copy(c, False).start()

    u_copy = pltpu.make_async_copy(UN, u_out, out_sem.at[0])
    v_copy = pltpu.make_async_copy(VN, v_out, out_sem.at[1])
    got_a = side_packs(
        packa,
        QW.at[:, :, pl.ds(1, 8), :],
        QE.at[:, :, pl.ds(1, 8), :],
        corner_copies(packa, QW, QE),
    )
    u_copy.start()
    v_copy.start()
    for copy in got_a:
        copy.wait_recv()

    south_row = jnp.logical_and(row == 0, jnp.logical_not(has_south))
    north_row = jnp.logical_and(row == ROWS - 1, jnp.logical_not(has_north))

    @pl.loop(0, NC)
    def _(c):
        @pl.when(has_south)
        def _():
            a_copy(c, True).wait_recv()

        @pl.when(has_north)
        def _():
            a_copy(c, False).wait_recv()

        base = (c * LC).astype(jnp.float32)
        cc0 = CC[8:16, :] - base
        near, beyond = [], []
        for f in range(2):
            s, m, n = [
                jnp.where(low2, QW[f, c, r : r + 8, :], QE[f, c, r : r + 8, :]) for r in range(3)
            ]
            y = jnp.where(north_row, 0.0, n) + jnp.where(south_row, 0.0, s)
            near.append(m)
            beyond.append(edge_terms(m, y))
        for i in range(LC):
            k = c * LC + i
            for f, out in ((0, TN), (1, SN)):
                ss, s, a, n, nn = [AX[f, k, r + 6 : r + 14, :] for r in range(5)]
                y = n + s
                far = nn + ss + spread_terms(a, y, unpacked(near[f], i), unpacked(beyond[f], i))
                mixed = centre_ts * a + (8.0 * KAPPA) * y - KAPPA * far
                out[k] = jnp.where(cc0 > i, mixed, 0.0)

    t_copy = pltpu.make_async_copy(TN, t_out, out_sem.at[2])
    s_copy = pltpu.make_async_copy(SN, s_out, out_sem.at[3])
    t_copy.start()
    s_copy.start()

    for copy in sent:
        copy.wait_send()

    @pl.loop(0, NC)
    def _(c):
        v1_copy(c).wait_send()
        for up in (True, False):
            uv_copy(c, up).wait_send()
            ts_copy(c, up).wait_send()

        @pl.when(has_north)
        def _():
            a_copy(c, True).wait_send()

        @pl.when(has_south)
        def _():
            a_copy(c, False).wait_send()

    for copy in (h_copy, u_copy, v_copy, t_copy, s_copy):
        copy.wait()


def per_device(nx, ny, *args):
    tile3 = jax.ShapeDtypeStruct((K, ROWS, LANES), jnp.float32)
    tile2 = jax.ShapeDtypeStruct((ROWS, LANES), jnp.float32)

    def vmem(*shape, dtype=jnp.float32):
        return pltpu.VMEM(shape, dtype)

    return pl.pallas_call(
        functools.partial(kernel, nx, ny),
        out_shape=(tile3, tile3, tile3, tile3, tile2),
        in_specs=[pl.BlockSpec(memory_space=pl.ANY)] * 7,
        out_specs=[pl.BlockSpec(memory_space=pl.ANY)] * 5,
        scratch_shapes=[
            vmem(4, K, 24, LANES),
            vmem(2, 3, 24, LANES),
            vmem(ROWS, LANES, dtype=jnp.int32),
            vmem(ROWS, LANES, dtype=jnp.int32),
            vmem(24, LANES),
            vmem(24, LANES),
            vmem(24, LANES),
            vmem(3, 24, LANES),
            vmem(4, NC, ROWS, LANES),
            vmem(4, NC, 16, LANES),
            vmem(4, NC, 16, LANES),
            vmem(4, 3, 24, LANES),
            vmem(24, LANES),
            vmem(K, ROWS, LANES),
            vmem(K, 16, LANES),
            vmem(NC, ROWS, LANES),
            vmem(NC, ROWS, LANES),
            vmem(2, K, 24, LANES),
            vmem(2, NC, ROWS, LANES),
            vmem(2, NC, 16, LANES),
            vmem(2, NC, 16, LANES),
            vmem(K, ROWS, LANES),
            vmem(K, ROWS, LANES),
            vmem(K, ROWS, LANES),
            vmem(K, ROWS, LANES),
            vmem(ROWS, LANES),
            pltpu.SemaphoreType.DMA((7,)),
            pltpu.SemaphoreType.DMA((N_WIRES,)),
            pltpu.SemaphoreType.DMA((N_WIRES,)),
            pltpu.SemaphoreType.DMA((5,)),
        ],
        compiler_params=pltpu.CompilerParams(
            collective_id=0, has_side_effects=True, vmem_limit_bytes=48 * 1024 * 1024
        ),
    )(*args)


def solution(mesh):
    placed = (P(None, "gy", "gx"),) * 4 + (P("gy", "gx"),) * 3
    return jax.shard_map(
        functools.partial(per_device, mesh.shape["gx"], mesh.shape["gy"]),
        mesh=mesh,
        in_specs=placed,
        out_specs=(P(None, "gy", "gx"),) * 4 + (P("gy", "gx"),),
        check_vma=False,
    )
```

profile of v0, /device:TPU:1, one launch (start us, length us, event | category | flops | bytes accessed | tf_op | source)
XLA Modules:
  0.0 51.4 jit_solution(17666456754187259990)
XLA Ops:
  0.6 0.0 copy-start
  0.6 1.0 %copy-done = f32[75,8,128]{2,1,0:T(8,128)S(1)} copy-done((f32[75,8,128]{2,1,0:T(8,128)S(1)}, f32[75,8,128]{2,1,0:T(8,128)}, u32[]{:S(2)}) %copy-start) | copy-done | bytes 307224
  1.6 0.0 copy-start.1
  1.6 1.0 %copy-done.1 = f32[75,8,128]{2,1,0:T(8,128)S(1)} copy-done((f32[75,8,128]{2,1,0:T(8,128)S(1)}, f32[75,8,128]{2,1,0:T(8,128)}, u32[]{:S(2)}) %copy-start.1) | copy-done | bytes 307224
  2.6 0.0 copy-start.2
  2.6 1.0 %copy-done.2 = f32[75,8,128]{2,1,0:T(8,128)S(1)} copy-done((f32[75,8,128]{2,1,0:T(8,128)S(1)}, f32[75,8,128]{2,1,0:T(8,128)}, u32[]{:S(2)}) %copy-start.2) | copy-done | bytes 307224
  3.5 0.0 copy-start.3
  3.5 1.0 %copy-done.3 = f32[75,8,128]{2,1,0:T(8,128)S(1)} copy-done((f32[75,8,128]{2,1,0:T(8,128)S(1)}, f32[75,8,128]{2,1,0:T(8,128)}, u32[]{:S(2)}) %copy-start.3) | copy-done | bytes 307224
  4.5 0.0 copy-start.4
  4.5 0.7 %copy-done.4 = f32[8,128]{1,0:T(8,128)S(1)} copy-done((f32[8,128]{1,0:T(8,128)S(1)}, f32[8,128]{1,0:T(8,128)}, u32[]{:S(2)}) %copy-start.4) | copy-done | bytes 4120
  5.2 0.0 copy-start.5
  5.2 0.7 %copy-done.5 = s32[8,128]{1,0:T(8,128)S(1)} copy-done((s32[8,128]{1,0:T(8,128)S(1)}, s32[8,128]{1,0:T(8,128)}, u32[]{:S(2)}) %copy-start.5) | copy-done | bytes 4120
  5.9 0.0 copy-start.6
  5.9 0.7 %copy-done.6 = s32[8,128]{1,0:T(8,128)S(1)} copy-done((s32[8,128]{1,0:T(8,128)S(1)}, s32[8,128]{1,0:T(8,128)}, u32[]{:S(2)}) %copy-start.6) | copy-done | bytes 4120
  6.6 41.4 %shard_map.110 = (f32[75,8,128]{2,1,0:T(8,128)S(1)}, f32[75,8,128]{2,1,0:T(8,128)S(1)}, f32[75,8,128]{2,1,0:T(8,128)S(1)}, f32[75,8,128]{2,1,0:T(8,128)S(1)}, f32[8,128]{1,0:T(8,128)S(1)}) custom-call(f32[75,8,128]{2,1,0:T(8,128)S(1)} %copy-done, f32[75,8,128]{2,1,0:T(8,128)S(1)} %copy-done.1, f32[75,8,128]{2,1,0:T(8,128)S(1)} %copy-done.2, ...), custom_call_target="tpu_custom_call" | custom-call | tf_op jit(solution)/shard_map/pallas_call | solution.py:629
  47.9 0.7 %copy.17 = f32[75,8,128]{2,1,0:T(8,128)} copy(f32[75,8,128]{2,1,0:T(8,128)S(1)} %get-tuple-element.10) | data formatting | bytes 614400
  48.7 0.7 %copy.18 = f32[75,8,128]{2,1,0:T(8,128)} copy(f32[75,8,128]{2,1,0:T(8,128)S(1)} %get-tuple-element.11) | data formatting | bytes 614400
  49.4 0.7 %copy.19 = f32[75,8,128]{2,1,0:T(8,128)} copy(f32[75,8,128]{2,1,0:T(8,128)S(1)} %get-tuple-element.12) | data formatting | bytes 614400
  50.1 0.7 %copy.20 = f32[75,8,128]{2,1,0:T(8,128)} copy(f32[75,8,128]{2,1,0:T(8,128)S(1)} %get-tuple-element.13) | data formatting | bytes 614400
  50.8 0.6 %copy.21 = f32[8,128]{1,0:T(8,128)} copy(f32[8,128]{1,0:T(8,128)S(1)} %get-tuple-element.14) | data formatting | bytes 8192
Async XLA Ops:
  0.6 1.0 %copy-start = (f32[75,8,128]{2,1,0:T(8,128)S(1)}, f32[75,8,128]{2,1,0:T(8,128)}, u32[]{:S(2)}) copy-start(f32[75,8,128]{2,1,0:T(8,128)} %t_in.1) | copy-start | bytes 921604
  1.6 1.0 %copy-start.1 = (f32[75,8,128]{2,1,0:T(8,128)S(1)}, f32[75,8,128]{2,1,0:T(8,128)}, u32[]{:S(2)}) copy-start(f32[75,8,128]{2,1,0:T(8,128)} %s_in.1) | copy-start | bytes 921604
  2.6 1.0 %copy-start.2 = (f32[75,8,128]{2,1,0:T(8,128)S(1)}, f32[75,8,128]{2,1,0:T(8,128)}, u32[]{:S(2)}) copy-start(f32[75,8,128]{2,1,0:T(8,128)} %u_in.1) | copy-start | bytes 921604
  3.5 1.0 %copy-start.3 = (f32[75,8,128]{2,1,0:T(8,128)S(1)}, f32[75,8,128]{2,1,0:T(8,128)}, u32[]{:S(2)}) copy-start(f32[75,8,128]{2,1,0:T(8,128)} %v_in.1) | copy-start | bytes 921604
  4.5 0.7 %copy-start.4 = (f32[8,128]{1,0:T(8,128)S(1)}, f32[8,128]{1,0:T(8,128)}, u32[]{:S(2)}) copy-start(f32[8,128]{1,0:T(8,128)} %h_in.1) | copy-start | bytes 12292
  5.2 0.7 %copy-start.5 = (s32[8,128]{1,0:T(8,128)S(1)}, s32[8,128]{1,0:T(8,128)}, u32[]{:S(2)}) copy-start(s32[8,128]{1,0:T(8,128)} %flag_in.1) | copy-start | bytes 12292
  5.9 0.7 %copy-start.6 = (s32[8,128]{1,0:T(8,128)S(1)}, s32[8,128]{1,0:T(8,128)}, u32[]{:S(2)}) copy-start(s32[8,128]{1,0:T(8,128)} %bottom_in.1) | copy-start | bytes 12292
where the time goes:
time: 51.7 us; the launch traced here: 51.4 us
  Pallas kernels  41.4 us (80%)
  local copies, waits for them, and re-layouts  9.38 us (18%)
  between operations  0.66 us (1%)
    pallas_call x1, Pallas kernels, per_device(): pl.pallas_call(functools.partial(kernel, nx, ny), out_shape=(tile3, tile3...  41.4 us
    unnamed x19, local copies, waits for them, and re-layouts  9.38 us

commit v1 on v0

--- a/solution.py
+++ b/solution.py
@@ -64,11 +64,11 @@
     h_in,
     flag_in,
     bottom_in,
-    t_out,
-    s_out,
-    u_out,
-    v_out,
-    h_out,
+    TN,
+    SN,
+    UN,
+    VN,
+    HN,
     X,
     D2,
     flag_v,
@@ -90,15 +90,9 @@
     packa,
     QE,
     QW,
-    UN,
-    VN,
-    TN,
-    SN,
-    HN,
     load_sem,
     send_sem,
     recv_sem,
-    out_sem,
 ):
     gx, gy = lax.axis_index("gx"), lax.axis_index("gy")
     wires = Wires(send_sem, recv_sem, gx, gy, nx, ny)
@@ -469,8 +463,6 @@
         run_v = both(jnp.add, run_v, trans_v)
 
     HN[...] = level[0][8:16]
-    h_copy = pltpu.make_async_copy(HN, h_out, out_sem.at[4])
-    h_copy.start()
     shift_u = both(
         lambda r, a, d, o: (r * (1.0 / SUBSTEPS) - a) / (d + (1.0 - o)), run_u, u_all, depth_u, open_u
     )
@@ -547,16 +539,12 @@
         def _():
             a_copy(c, False).start()
 
-    u_copy = pltpu.make_async_copy(UN, u_out, out_sem.at[0])
-    v_copy = pltpu.make_async_copy(VN, v_out, out_sem.at[1])
     got_a = side_packs(
         packa,
         QW.at[:, :, pl.ds(1, 8), :],
         QE.at[:, :, pl.ds(1, 8), :],
         corner_copies(packa, QW, QE),
     )
-    u_copy.start()
-    v_copy.start()
     for copy in got_a:
         copy.wait_recv()
 
@@ -592,11 +580,6 @@
                 mixed = centre_ts * a + (8.0 * KAPPA) * y - KAPPA * far
                 out[k] = jnp.where(cc0 > i, mixed, 0.0)
 
-    t_copy = pltpu.make_async_copy(TN, t_out, out_sem.at[2])
-    s_copy = pltpu.make_async_copy(SN, s_out, out_sem.at[3])
-    t_copy.start()
-    s_copy.start()
-
     for copy in sent:
         copy.wait_send()
 
@@ -615,9 +598,6 @@
         def _():
             a_copy(c, False).wait_send()
 
-    for copy in (h_copy, u_copy, v_copy, t_copy, s_copy):
-        copy.wait()
-
 
 def per_device(nx, ny, *args):
     tile3 = jax.ShapeDtypeStruct((K, ROWS, LANES), jnp.float32)
@@ -626,11 +606,12 @@
     def vmem(*shape, dtype=jnp.float32):
         return pltpu.VMEM(shape, dtype)
 
-    return pl.pallas_call(
+    args = [pltpu.with_memory_space_constraint(x, pltpu.HBM) for x in args]
+    held = pl.pallas_call(
         functools.partial(kernel, nx, ny),
-        out_shape=(tile3, tile3, tile3, tile3, tile2),
-        in_specs=[pl.BlockSpec(memory_space=pl.ANY)] * 7,
-        out_specs=[pl.BlockSpec(memory_space=pl.ANY)] * 5,
+        out_shape=tuple(pltpu.VMEM(x.shape, x.dtype) for x in (tile3, tile3, tile3, tile3, tile2)),
+        in_specs=[pl.BlockSpec(memory_space=pltpu.HBM)] * 7,
+        out_specs=[pl.BlockSpec(memory_space=pltpu.VMEM)] * 5,
         scratch_shapes=[
             vmem(4, K, 24, LANES),
             vmem(2, 3, 24, LANES),
@@ -653,20 +634,30 @@
             vmem(2, NC, ROWS, LANES),
             vmem(2, NC, 16, LANES),
             vmem(2, NC, 16, LANES),
-            vmem(K, ROWS, LANES),
-            vmem(K, ROWS, LANES),
-            vmem(K, ROWS, LANES),
-            vmem(K, ROWS, LANES),
-            vmem(ROWS, LANES),
             pltpu.SemaphoreType.DMA((7,)),
             pltpu.SemaphoreType.DMA((N_WIRES,)),
             pltpu.SemaphoreType.DMA((N_WIRES,)),
-            pltpu.SemaphoreType.DMA((5,)),
         ],
         compiler_params=pltpu.CompilerParams(
-            collective_id=0, has_side_effects=True, vmem_limit_bytes=48 * 1024 * 1024
+            collective_id=0, has_side_effects=True, vmem_limit_bytes=24 * 1024 * 1024
         ),
     )(*args)
+    return pl.pallas_call(
+        write_out,
+        out_shape=(tile3, tile3, tile3, tile3, tile2),
+        in_specs=[pl.BlockSpec(memory_space=pltpu.VMEM)] * 5,
+        out_specs=[pl.BlockSpec(memory_space=pltpu.HBM)] * 5,
+        scratch_shapes=[pltpu.SemaphoreType.DMA((5,))],
+        compiler_params=pltpu.CompilerParams(vmem_limit_bytes=8 * 1024 * 1024),
+    )(*held)
+
+
+def write_out(*refs):
+    copies = [pltpu.make_async_copy(refs[i], refs[5 + i], refs[10].at[i]) for i in range(5)]
+    for copy in copies:
+        copy.start()
+    for copy in copies:
+        copy.wait()
 
 
 def solution(mesh):

time: 51.7 us -> 42.9 us (0.83)
  local copies, waits for them, and re-layouts: 9.38 us -> 0 us
  Pallas kernels: 41.4 us -> 42.2 us
    unnamed x19 -> x0, local copies, waits for them, and re-layouts: 9.38 us -> none
    pallas_call x1 -> x2, Pallas kernels: 41.4 us -> 42.2 us  [the longest x1 41.1 us: per_device(): pl.pallas_call(functools.partial(kernel, nx, ny), out_shape=tuple((pltpu....]
where the time goes in v1:
time: 42.9 us; the launch traced here: 42.8 us
  Pallas kernels  42.2 us (98%)
  between operations  0.64 us (1%)
    pallas_call x1, Pallas kernels, per_device(): pl.pallas_call(functools.partial(kernel, nx, ny), out_shape=tuple((pltpu....  41.1 us
    pallas_call x1, Pallas kernels, per_device(): pl.pallas_call(write_out, out_shape=(tile3, tile3, tile3, tile3, tile2),...  1.07 us

profile of v1, /device:TPU:1, one launch (start us, length us, event | category | flops | bytes accessed | tf_op | source)
XLA Modules:
  0.0 42.8 jit_solution(2908012572353150887)
XLA Ops:
  0.6 41.1 %shard_map.110 = (f32[75,8,128]{2,1,0:T(8,128)S(1)}, f32[75,8,128]{2,1,0:T(8,128)S(1)}, f32[75,8,128]{2,1,0:T(8,128)S(1)}, f32[75,8,128]{2,1,0:T(8,128)S(1)}, f32[8,128]{1,0:T(8,128)S(1)}) custom-call(f32[75,8,128]{2,1,0:T(8,128)} %t_in.1, f32[75,8,128]{2,1,0:T(8,128)} %s_in.1, f32[75,8,128]{2,1,0:T(8,128)} %u_in.1, f32[75,8,128]{2,1,0:T(8,128)} %v_in.1, ...), custom_call_target="tpu_custom_call" | custom-call | tf_op jit(solution)/shard_map/pallas_call | solution.py:610
  41.8 1.1 %shard_map.111 = (f32[75,8,128]{2,1,0:T(8,128)}, f32[75,8,128]{2,1,0:T(8,128)}, f32[75,8,128]{2,1,0:T(8,128)}, f32[75,8,128]{2,1,0:T(8,128)}, f32[8,128]{1,0:T(8,128)}) custom-call(f32[75,8,128]{2,1,0:T(8,128)S(1)} %get-tuple-element.10.refs_0_, f32[75,8,128]{2,1,0:T(8,128)S(1)} %get-tuple-element.11.refs_1_, f32[75,8,128]{2,1,0:T(8,128)S(1)} %get-tuple-element.12.refs_2_, ...), custom_call_target="tpu_custom_call" | custom-call | tf_op jit(solution)/shard_map/pallas_call | solution.py:645

commit v2 on v0

v2 whole, which is shorter than its diff:
```python
import functools

import jax
import jax.numpy as jnp
from jax import lax
from jax.experimental import pallas as pl
from jax.experimental.pallas import tpu as pltpu
from jax.sharding import PartitionSpec as P

MESH = pl.DeviceIdType.MESH
K = 75
NC = 5
LC = K // NC
SUBSTEPS = 8
ROWS = 8
LANES = 128

DT = 0.4
NU = 0.025
KAPPA = 0.01
DTT = 0.2
GRAVITY = 4.0
DB = DT / SUBSTEPS

AROUND = [(dx, dy) for dy in (-1, 0, 1) for dx in (-1, 0, 1) if (dx, dy) != (0, 0)]
(G_2D, G_UV, G_W, G_SIDE, G_CORNER, G_POLE, G_TS, G_SUM, G_SIDE1, G_CORNER1, G_V1, G_UP, G_DOWN, G_UP1, G_DOWN1) = range(15)
GROUPS = 15


def kernel(
    nx,
    ny,
    t_in,
    s_in,
    u_in,
    v_in,
    h_in,
    flag_in,
    bottom_in,
    TN,
    SN,
    UN,
    VN,
    HN,
    X,
    WX,
    D2,
    flag_v,
    bottom_v,
    CC,
    CU,
    CV,
    SC,
    SU,
    SV,
    pack,
    PE,
    PW,
    F2,
    DV,
    DP,
    U1B,
    V1X,
    pack1,
    P1E,
    P1W,
    AX,
    AD,
    load_sem,
    send_sem,
    recv_sem,
):
    gx, gy = lax.axis_index("gx"), lax.axis_index("gy")

    def device(dx, dy):
        return (lax.rem(gx + dx + nx, nx), lax.rem(gy + dy + ny, ny))

    def send(group, src, dst, dx, dy):
        pltpu.make_async_remote_copy(
            src_ref=src,
            dst_ref=dst,
            send_sem=send_sem.at[group],
            recv_sem=recv_sem.at[group],
            device_id=device(dx, dy),
            device_id_type=MESH,
        ).start()

    def received(group, size):
        pltpu.make_async_copy(size, size, recv_sem.at[group]).wait()

    def left(group, size):
        pltpu.make_async_copy(size, size, send_sem.at[group]).wait()

    loads = [
        pltpu.make_async_copy(flag_in, flag_v, load_sem.at[5]),
        pltpu.make_async_copy(bottom_in, bottom_v, load_sem.at[6]),
        pltpu.make_async_copy(h_in, D2.at[1, 1, pl.ds(8, 8), :], load_sem.at[4]),
        pltpu.make_async_copy(u_in, X.at[0, :, pl.ds(8, 8), :], load_sem.at[0]),
        pltpu.make_async_copy(v_in, X.at[1, :, pl.ds(8, 8), :], load_sem.at[1]),
        pltpu.make_async_copy(t_in, X.at[2, :, pl.ds(8, 8), :], load_sem.at[2]),
        pltpu.make_async_copy(s_in, X.at[3, :, pl.ds(8, 8), :], load_sem.at[3]),
    ]
    for load in loads:
        load.start()

    barrier = pltpu.get_barrier_semaphore()
    for dx, dy in AROUND:
        pl.semaphore_signal(barrier, inc=1, device_id=device(dx, dy), device_id_type=MESH)

    lane = lax.broadcasted_iota(jnp.int32, (ROWS, LANES), 1)
    lane8 = lax.rem(lane, 8)
    slot = lax.div(lane, 8).astype(jnp.float32)
    row = lax.broadcasted_iota(jnp.int32, (ROWS, LANES), 0)
    first, last = lane == 0, lane == LANES - 1
    edge4 = jnp.logical_or(lane < 2, lane >= LANES - 2)
    western, at3, at4 = lane8 < 4, lane8 == 3, lane8 == 4
    has_south, has_north = gy > 0, gy < ny - 1
    zero = jnp.zeros((ROWS, LANES), jnp.float32)

    def roll(x, shift):
        return pltpu.roll(x, shift % LANES, 1)

    def packed(x, i):
        return roll(x, 8 * i + 4)

    def unpacked(x, i):
        return roll(x, LANES - 4 - 8 * i)

    def in_slots(x, lanes):
        l8 = lax.rem(lax.broadcasted_iota(jnp.int32, x.shape, 1), 8)
        out = None
        for l in lanes:
            column = jnp.broadcast_to(x[:, l : l + 1], x.shape)
            out = column if out is None else jnp.where(l8 == (l + 4) % LANES, column, out)
        return out

    @pl.when(jnp.logical_not(has_south))
    def _():
        AD[:, :, 0:1, :] = jnp.zeros((2, NC, 1, LANES), jnp.float32)

        @pl.loop(0, K)
        def _(k):
            for f in range(2):
                AX[f, k, 6:8, :] = jnp.zeros((2, LANES), jnp.float32)

    @pl.when(jnp.logical_not(has_north))
    def _():
        AD[:, :, 9:10, :] = jnp.zeros((2, NC, 1, LANES), jnp.float32)

        @pl.loop(0, K)
        def _(k):
            for f in range(2):
                AX[f, k, 16:18, :] = jnp.zeros((2, LANES), jnp.float32)

    for load in loads[:3]:
        load.wait()
    own = (flag_v[...] * bottom_v[...]).astype(jnp.float32)
    D2[0, 1, 8:16, :] = own
    D2[2, 1, 8:16, :] = in_slots(own, (124, 125, 126, 127, 0, 1, 2, 3))

    pl.semaphore_wait(barrier, len(AROUND))

    for dx, dy in AROUND:
        send(
            G_2D,
            D2.at[:, 1, pl.ds(8, 8), :],
            D2.at[:, 1 - dx, pl.ds(8 * (1 - dy), 8), :],
            dx,
            dy,
        )

    def rows(group, fields, count, dy):
        src, dst = (16 - count, 8 - count) if dy > 0 else (8, 16)
        send(
            group,
            X.at[fields, :, pl.ds(src, count), :],
            X.at[fields, :, pl.ds(dst, count), :],
            0,
            dy,
        )

    for load in loads[3:]:
        load.wait()
    for dy in (1, -1):
        rows(G_UV, pl.ds(0, 2), 2, dy)

    def weight(t, s, dz):
        return (0.8 * s - t * (0.2 + 0.05 * t)) * dz

    def thickness(base, i):
        return 0.5 / K + (base + (i + 0.5)) * (1.0 / (K * K))

    @pl.loop(0, NC)
    def _(c):
        base = (c * LC).astype(jnp.float32)
        depth = D2[0, 1, 8:16, :] - base
        held = [zero] * 5
        for i in range(LC):
            k = c * LC + i
            u, v, t, s = [X[f, k, 8:16, :] for f in range(4)]
            w = jnp.where(depth > i, weight(t, s, DT * thickness(base, i)), 0.0)
            WX[k, 0:8, :] = w
            for n, x in enumerate((u, v, w, t, s)):
                held[n] = jnp.where(slot == i, packed(x, i), held[n])
        for n in range(5):
            pack[n, c, 1:9, :] = held[n]

    for dx in (1, -1):
        side = PW if dx > 0 else PE
        send(G_SIDE, pack.at[:, :, pl.ds(1, 8), :], side.at[:, :, pl.ds(1, 8), :], dx, 0)
    for dx in (1, -1):
        for dy in (1, -1):
            side = PW if dx > 0 else PE
            src, dst = (8, 0) if dy > 0 else (1, 9)
            send(
                G_CORNER, pack.at[:, :, pl.ds(src, 1), :], side.at[:, :, pl.ds(dst, 1), :], dx, dy
            )
    for dy in (1, -1):
        src, dst = (8, 0) if dy > 0 else (1, 9)
        uv = pl.ds(0, 2)
        send(G_POLE, pack.at[uv, :, pl.ds(src, 1), :], pack.at[uv, :, pl.ds(dst, 1), :], 0, dy)
    send(G_W, WX.at[:, pl.ds(0, 1), :], WX.at[:, pl.ds(8, 1), :], 0, -1)
    for dy in (1, -1):
        rows(G_TS, pl.ds(2, 2), 1, dy)

    size_2d = X.at[0, pl.ds(0, 24), pl.ds(0, 8), :]
    size_uv = X.at[pl.ds(0, 2), :, pl.ds(0, 4), :]
    size_w = X.at[0, :, pl.ds(0, 1), :]
    size_side = PE.at[:, :, pl.ds(0, 16), :]
    size_corner = PE.at[:, :, pl.ds(0, 4), :]
    size_pole = PE.at[pl.ds(0, 2), :, pl.ds(0, 2), :]
    size_ts = X.at[pl.ds(0, 2), :, pl.ds(0, 2), :]
    size_sum = X.at[0, pl.ds(0, 32), pl.ds(0, 8), :]
    size_side1 = P1E.at[:, :, pl.ds(0, 16), :]
    size_corner1 = P1E.at[0, :, pl.ds(0, 2), :]
    size_v1 = V1X.at[:, pl.ds(0, 1), :]
    size_a = X.at[pl.ds(0, 2), :, pl.ds(0, 2), :]
    size_ad = AD.at[:, :, pl.ds(0, 1), :]

    received(G_2D, size_2d)
    row24 = lax.broadcasted_iota(jnp.int32, (24, LANES), 0)
    lane24 = lax.broadcasted_iota(jnp.int32, (24, LANES), 1)
    slot24 = lax.rem(lane24, 8)
    first24, last24 = lane24 == 0, lane24 == LANES - 1
    inside = jnp.logical_and(
        jnp.logical_or(row24 >= 8, has_south), jnp.logical_or(row24 < 16, has_north)
    )

    def ring_east(c, h, seam=first24):
        return (
            roll(jnp.where(seam, h, c), LANES - 1),
            roll(jnp.where(seam, c, h), LANES - 1),
        )

    def ring_west(c, h):
        return (
            roll(jnp.where(last24, h, c), 1),
            roll(jnp.where(last24, c, h), 1),
        )

    def north24(x):
        return pltpu.roll(x, 23, 0)

    def south24(x):
        return pltpu.roll(x, 1, 0)

    def sides(ref, f):
        return ref[f, 1], jnp.where(lane24 < 64, ref[f, 2], ref[f, 0])

    col = [jnp.where(inside, x, 0.0) for x in sides(D2, 0)]
    ocean = [x > 0.0 for x in col]
    cu = [jnp.minimum(a, b) for a, b in zip(col, ring_east(*col))]
    cv = [jnp.minimum(a, north24(a)) for a in col]
    CC[...] = col[0]
    CU[...] = cu[0]
    CV[...] = cv[0]
    edge_col = [
        jnp.where(inside, x, 0.0)
        for x in (jnp.where(slot24 < 4, D2[2, 0], D2[2, 2]), D2[2, 1])
    ]
    edge_cu = [jnp.minimum(a, b) for a, b in zip(edge_col, ring_east(*edge_col, slot24 == 4))]
    for n in range(2):
        SC[n] = edge_col[n]
        SU[n] = edge_cu[n]
        SV[n] = jnp.minimum(edge_col[n], north24(edge_col[n]))

    at_wall = jnp.where(
        jnp.logical_or(
            jnp.logical_and(row == 0, jnp.logical_not(has_south)),
            jnp.logical_and(row == ROWS - 1, jnp.logical_not(has_north)),
        ),
        19.0,
        20.0,
    )
    latitude = (row + gy * ROWS).astype(jnp.float32)
    f4 = (0.25 * DT) * (0.2 + 0.3 * (latitude + 0.5) / (ROWS * ny))
    centre_uv = 1.0 - (DT * NU) * at_wall
    centre_ts = 1.0 - KAPPA * at_wall

    received(G_UV, size_uv)
    left(G_UV, size_uv)

    @pl.loop(0, NC)
    def _(c):
        base = (c * LC).astype(jnp.float32)
        for f, depths in ((0, CU), (1, CV)):
            low, high = depths[6:14, :] - base, depths[10:18, :] - base
            for i in range(LC):
                k = c * LC + i
                a = jnp.where(low > i, X[f, k, 6:14, :], 0.0)
                b = jnp.where(high > i, X[f, k, 10:18, :], 0.0)
                X[f, k, 6:14, :] = a
                X[f, k, 10:18, :] = b

    received(G_W, size_w)
    received(G_SIDE, size_side)
    received(G_CORNER, size_corner)
    received(G_POLE, size_pole)

    def edge_far(d, y):
        z = 2.0 * y - 8.0 * d
        return jnp.where(western, roll(d, -2), roll(d, 2)) + jnp.where(
            at3, roll(z, -1), jnp.where(at4, roll(z, 1), 0.0)
        )

    def far(a, y, yy):
        z = 2.0 * y - 8.0 * a
        return yy + roll(z + roll(a, -1), -1) + roll(z + roll(a, 1), 1)

    def momentum(c, carry):
        cum_e, cum_n, edge_cum, sum_u0, sum_v0, sum_u, sum_v = carry
        base = (c * LC).astype(jnp.float32)
        level = slot + base

        def excess(f, depths, r):
            beyond = jnp.where(western, PW[f, c, r : r + 8, :], PE[f, c, r : r + 8, :])
            beyond = jnp.where(level < depths[0, r + 7 : r + 15, :], beyond, 0.0)
            return beyond - jnp.where(
                level < depths[1, r + 7 : r + 15, :], pack[f, c, r : r + 8, :], 0.0
            )

        du_s, du, du_n = [excess(0, SU, r) for r in range(3)]
        dv_s, dv, dv_n = [excess(1, SV, r) for r in range(3)]
        dw = jnp.where(western, PW[2, c, 1:9, :], PE[2, c, 1:9, :]) - pack[2, c, 1:9, :]
        dw = jnp.where(at3, roll(dw, -1), 0.0)
        run = dw
        for shift in (8, 16, 32, 64):
            run = run + jnp.where(lane >= shift, roll(run, shift), 0.0)
        run = run + edge_cum
        edge_cum = jnp.broadcast_to(run[:, 8 * LC - 5 : 8 * LC - 4], run.shape)
        edge_u = (
            jnp.where(at3, f4 * roll(dv + dv_s, -1) - run + 0.5 * dw, 0.0)
            - (DT * NU) * edge_far(du, du_n + du_s)
        )
        edge_v = (
            jnp.where(at4, -f4 * roll(du + du_n, 1), 0.0)
            - (DT * NU) * edge_far(dv, dv_n + dv_s)
        )

        cu0, cv0 = CU[8:16, :] - base, CV[8:16, :] - base
        held_u = held_v = zero
        for i in range(LC):
            k = c * LC + i
            dz = thickness(base, i)
            uss, us, u, un, unn = [X[0, k, r : r + 8, :] for r in range(6, 11)]
            vss, vs, v, vn, vnn = [X[1, k, r : r + 8, :] for r in range(6, 11)]
            w, wn = WX[k, 0:8, :], WX[k, 1:9, :]
            step_e = roll(w, -1) - w
            step_n = wn - w
            cum_e = cum_e + step_e
            cum_n = cum_n + step_n
            uu = u + un
            vv = v + vs
            uu = uu + roll(uu, 1)
            vv = vv + roll(vv, -1)
            yu, yv = un + us, vn + vs
            u1 = (
                centre_uv * u
                + f4 * vv
                - (cum_e - 0.5 * step_e)
                - (DT * NU) * (far(u, yu, unn + uss) - 8.0 * yu)
                + jnp.where(edge4, unpacked(edge_u, i), 0.0)
            )
            v1 = (
                centre_uv * v
                - f4 * uu
                - (cum_n - 0.5 * step_n)
                - (DT * NU) * (far(v, yv, vnn + vss) - 8.0 * yv)
                + jnp.where(edge4, unpacked(edge_v, i), 0.0)
            )
            u1 = jnp.where(cu0 > i, u1, 0.0)
            v1 = jnp.where(cv0 > i, v1, 0.0)
            sum_u0 = sum_u0 + u * dz
            sum_v0 = sum_v0 + v * dz
            sum_u = sum_u + u1 * dz
            sum_v = sum_v + v1 * dz
            U1B[k] = u1
            V1X[k, 8:16, :] = v1
            held_u = jnp.where(slot == i, packed(u1, i), held_u)
            held_v = jnp.where(slot == i, packed(v1, i), held_v)
        pack1[0, c] = held_u
        pack1[1, c] = held_v
        return cum_e, cum_n, edge_cum, sum_u0, sum_v0, sum_u, sum_v

    sums = lax.fori_loop(0, NC, momentum, (zero,) * 7)[3:]

    for n in range(4):
        F2[n, 1, 8:16, :] = sums[n]
    for dx, dy in AROUND:
        send(
            G_SUM,
            F2.at[:, 1, pl.ds(8, 8), :],
            F2.at[:, 1 - dx, pl.ds(8 * (1 - dy), 8), :],
            dx,
            dy,
        )
    for dx in (1, -1):
        side = P1W if dx > 0 else P1E
        send(G_SIDE1, pack1, side.at[:, :, pl.ds(1, 8), :], dx, 0)
        send(G_CORNER1, pack1.at[1, :, pl.ds(7, 1), :], side.at[1, :, pl.ds(0, 1), :], dx, 1)
    send(G_V1, V1X.at[:, pl.ds(15, 1), :], V1X.at[:, pl.ds(7, 1), :], 0, 1)

    left(G_2D, size_2d)
    left(G_W, size_w)
    left(G_SIDE, size_side)
    left(G_CORNER, size_corner)
    left(G_POLE, size_pole)
    left(G_TS, size_ts)
    received(G_TS, size_ts)

    @pl.loop(0, NC)
    def _(c):
        base = (c * LC).astype(jnp.float32)
        low, high = CC[7:15, :] - base, CC[9:17, :] - base
        for f in (2, 3):
            for i in range(LC):
                k = c * LC + i
                a = jnp.where(low > i, X[f, k, 7:15, :], 0.0)
                b = jnp.where(high > i, X[f, k, 9:17, :], 0.0)
                X[f, k, 7:15, :] = a
                X[f, k, 9:17, :] = b

    def both(op, *pairs):
        return [op(*xs) for xs in zip(*pairs)]

    def depth_of(c):
        return c * (0.5 / K + c * (0.5 / (K * K)))

    open_u = [(x > 0.0).astype(jnp.float32) for x in cu]
    open_v = [(x > 0.0).astype(jnp.float32) for x in cv]
    depth_u = both(depth_of, cu)
    depth_v = both(depth_of, cv)
    pull_u = both(lambda o, d: o * d * (DB * GRAVITY), open_u, depth_u)
    pull_v = both(lambda o, d: o * d * (DB * GRAVITY), open_v, depth_v)
    ease = both(lambda o: jnp.where(o, DB, 0.0), ocean)
    level = [jnp.where(o, x, 0.0) for o, x in zip(ocean, sides(D2, 1))]

    received(G_SUM, size_sum)
    u0, v0, u_all, v_all = [list(sides(F2, f)) for f in range(4)]
    push_u = both(lambda o, a, b: o * ((a - b) * (DB / DT)), open_u, u_all, u0)
    push_v = both(lambda o, a, b: o * ((a - b) * (DB / DT)), open_v, v_all, v0)
    trans_u = both(lambda o, a: o * a, open_u, u0)
    trans_v = both(lambda o, a: o * a, open_v, v0)
    run_u = [jnp.zeros((24, LANES), jnp.float32)] * 2
    run_v = run_u

    def substep(_, state):
        level, trans_u, trans_v, run_u, run_v = state
        trans_u = both(
            lambda t, p, q, e, h: t + (p - q * (e - h)),
            trans_u,
            push_u,
            pull_u,
            ring_east(*level),
            level,
        )
        trans_v = both(
            lambda t, p, q, h: t + (p - q * (north24(h) - h)), trans_v, push_v, pull_v, level
        )
        level = both(
            lambda h, e, u, w, v: h - e * ((u - w) + (v - south24(v))),
            level,
            ease,
            trans_u,
            ring_west(*trans_u),
            trans_v,
        )
        return level, trans_u, trans_v, both(jnp.add, run_u, trans_u), both(jnp.add, run_v, trans_v)

    state = level, trans_u, trans_v, run_u, run_v
    for n in range(SUBSTEPS):
        state = substep(n, state)
    level, _, _, run_u, run_v = state

    HN[...] = level[0][8:16]

    def shift(r, a, d, o):
        return (r * (1.0 / SUBSTEPS) - a) / (d + (1.0 - o))

    shift_u = both(shift, run_u, u_all, depth_u, open_u)
    shift_v = both(shift, run_v, v_all, depth_v, open_v)
    DV[0] = shift_v[0]
    DV[1] = shift_v[1]
    du, dv, dvs = shift_u[0][8:16], shift_v[0][8:16], DV[0, 7:15, :]
    DP[0] = in_slots(shift_u[1][8:16], (125, 126, 127, 0, 1))
    DP[1] = in_slots(DV[1, 8:16, :], (126, 127, 0, 1))
    DP[2] = in_slots(DV[1, 7:15, :], (126, 127, 0, 1))
    DP[3] = jnp.broadcast_to(du[:, LANES - 1 :], du.shape)

    received(G_SIDE1, size_side1)
    received(G_CORNER1, size_corner1)
    received(G_V1, size_v1)
    half = 0.5 * DTT

    @pl.loop(0, NC)
    def _(c):
        base = (c * LC).astype(jnp.float32)
        level = slot + base

        def beyond(west, east, f, r):
            return jnp.where(western, west[f, c, r : r + 8, :], east[f, c, r : r + 8, :])

        edge_u = jnp.where(level < SU[0, 8:16, :], beyond(P1W, P1E, 0, 1) + DP[0], 0.0) * half
        edge_v = jnp.where(level < SV[0, 8:16, :], beyond(P1W, P1E, 1, 1) + DP[1], 0.0) * half
        edge_vs = jnp.where(level < SV[0, 7:15, :], beyond(P1W, P1E, 1, 0) + DP[2], 0.0) * half
        last_u = jnp.where(level < SU[1, 8:16, :], pack1[0, c] + DP[3], 0.0) * half
        edges, outer = [], []
        for f in (3, 4):
            south, here, north = [
                jnp.where(level < SC[0, r + 7 : r + 15, :], beyond(PW, PE, f, r), 0.0)
                for r in range(3)
            ]
            inner = jnp.where(level < SC[1, 8:16, :], pack[f, c, 1:9, :], 0.0)
            flux = edge_u * (here + roll(jnp.where(at4, inner, here), -1))
            flux_last = last_u * (inner + roll(here, -1))
            flux_west = roll(jnp.where(at3, flux_last, flux), 1)
            a = here - ((flux - flux_west) + (edge_v * (here + north) - edge_vs * (south + here)))
            outer.append(jnp.where(level < SC[0, 8:16, :], a, 0.0))
            edges.append(jnp.where(at3, flux, here))

        cc0, cu0, cv0 = CC[8:16, :] - base, CU[8:16, :] - base, CV[8:16, :] - base
        cvs = CV[7:15, :] - base
        held = [zero, zero]
        for i in range(LC):
            k = c * LC + i
            u = jnp.where(cu0 > i, U1B[k] + du, 0.0)
            v = jnp.where(cv0 > i, V1X[k, 8:16, :] + dv, 0.0)
            vs = jnp.where(cvs > i, V1X[k, 7:15, :] + dvs, 0.0) * half
            UN[k] = u
            VN[k] = v
            u = u * half
            v = v * half
            for f in range(2):
                south, here, north = [X[2 + f, k, r : r + 8, :] for r in (7, 8, 9)]
                edge = unpacked(edges[f], i)
                flux = u * (here + roll(jnp.where(first, edge, here), -1))
                a = here - (
                    (flux - roll(jnp.where(last, edge, flux), 1))
                    + (v * (here + north) - vs * (south + here))
                )
                a = jnp.where(cc0 > i, a, 0.0)
                AX[f, k, 8:16, :] = a
                held[f] = jnp.where(slot == i, packed(a, i), held[f])
        for f in range(2):
            AD[f, c, 1:9, :] = outer[f] - held[f]

    @pl.when(has_north)
    def _():
        send(G_UP, AX.at[:, :, pl.ds(14, 2), :], AX.at[:, :, pl.ds(6, 2), :], 0, 1)
        send(G_UP1, AD.at[:, :, pl.ds(8, 1), :], AD.at[:, :, pl.ds(0, 1), :], 0, 1)

    @pl.when(has_south)
    def _():
        send(G_DOWN, AX.at[:, :, pl.ds(8, 2), :], AX.at[:, :, pl.ds(16, 2), :], 0, -1)
        send(G_DOWN1, AD.at[:, :, pl.ds(1, 1), :], AD.at[:, :, pl.ds(9, 1), :], 0, -1)

    left(G_SUM, size_sum)
    left(G_SIDE1, size_side1)
    left(G_CORNER1, size_corner1)
    left(G_V1, size_v1)

    @pl.when(has_south)
    def _():
        received(G_UP, size_a)
        received(G_UP1, size_ad)

    @pl.when(has_north)
    def _():
        received(G_DOWN, size_a)
        received(G_DOWN1, size_ad)

    @pl.loop(0, NC)
    def _(c):
        base = (c * LC).astype(jnp.float32)
        cc0 = CC[8:16, :] - base
        edges = []
        for f in range(2):
            south, here, north = [AD[f, c, r : r + 8, :] for r in range(3)]
            edges.append(KAPPA * edge_far(here, south + north))
        for i in range(LC):
            k = c * LC + i
            for f, out in ((0, TN), (1, SN)):
                ss, s, a, n, nn = [AX[f, k, r : r + 8, :] for r in range(6, 11)]
                y = n + s
                mixed = (
                    centre_ts * a
                    - KAPPA * (far(a, y, nn + ss) - 8.0 * y)
                    - jnp.where(edge4, unpacked(edges[f], i), 0.0)
                )
                out[k] = jnp.where(cc0 > i, mixed, 0.0)

    @pl.when(has_north)
    def _():
        left(G_UP, size_a)
        left(G_UP1, size_ad)

    @pl.when(has_south)
    def _():
        left(G_DOWN, size_a)
        left(G_DOWN1, size_ad)


def write_out(*refs):
    copies = [pltpu.make_async_copy(refs[i], refs[5 + i], refs[10].at[i]) for i in range(5)]
    for copy in copies:
        copy.start()
    for copy in copies:
        copy.wait()


def per_device(nx, ny, *args):
    tile3 = jax.ShapeDtypeStruct((K, ROWS, LANES), jnp.float32)
    tile2 = jax.ShapeDtypeStruct((ROWS, LANES), jnp.float32)
    outs = (tile3, tile3, tile3, tile3, tile2)

    def vmem(*shape, dtype=jnp.float32):
        return pltpu.VMEM(shape, dtype)

    args = [pltpu.with_memory_space_constraint(x, pltpu.HBM) for x in args]
    held = pl.pallas_call(
        functools.partial(kernel, nx, ny),
        out_shape=tuple(pltpu.VMEM(x.shape, x.dtype) for x in outs),
        in_specs=[pl.BlockSpec(memory_space=pltpu.HBM)] * 7,
        out_specs=[pl.BlockSpec(memory_space=pltpu.VMEM)] * 5,
        scratch_shapes=[
            vmem(4, K, 24, LANES),
            vmem(K, 16, LANES),
            vmem(3, 3, 24, LANES),
            vmem(ROWS, LANES, dtype=jnp.int32),
            vmem(ROWS, LANES, dtype=jnp.int32),
            vmem(24, LANES),
            vmem(24, LANES),
            vmem(24, LANES),
            vmem(2, 24, LANES),
            vmem(2, 24, LANES),
            vmem(2, 24, LANES),
            vmem(5, NC, 16, LANES),
            vmem(5, NC, 16, LANES),
            vmem(5, NC, 16, LANES),
            vmem(4, 3, 24, LANES),
            vmem(2, 24, LANES),
            vmem(4, ROWS, LANES),
            vmem(K, ROWS, LANES),
            vmem(K, 16, LANES),
            vmem(2, NC, ROWS, LANES),
            vmem(2, NC, 16, LANES),
            vmem(2, NC, 16, LANES),
            vmem(2, K, 24, LANES),
            vmem(2, NC, 16, LANES),
            pltpu.SemaphoreType.DMA((7,)),
            pltpu.SemaphoreType.DMA((GROUPS,)),
            pltpu.SemaphoreType.DMA((GROUPS,)),
        ],
        compiler_params=pltpu.CompilerParams(
            collective_id=0, has_side_effects=True, vmem_limit_bytes=24 * 1024 * 1024
        ),
    )(*args)
    return pl.pallas_call(
        write_out,
        out_shape=outs,
        in_specs=[pl.BlockSpec(memory_space=pltpu.VMEM)] * 5,
        out_specs=[pl.BlockSpec(memory_space=pltpu.HBM)] * 5,
        scratch_shapes=[pltpu.SemaphoreType.DMA((5,))],
        compiler_params=pltpu.CompilerParams(vmem_limit_bytes=8 * 1024 * 1024),
    )(*held)


def solution(mesh):
    placed = (P(None, "gy", "gx"),) * 4 + (P("gy", "gx"),) * 3
    return jax.shard_map(
        functools.partial(per_device, mesh.shape["gx"], mesh.shape["gy"]),
        mesh=mesh,
        in_specs=placed,
        out_specs=(P(None, "gy", "gx"),) * 4 + (P("gy", "gx"),),
        check_vma=False,
    )
```

time: 51.7 us -> 37.9 us (0.73)
  local copies, waits for them, and re-layouts: 9.38 us -> 0 us
  Pallas kernels: 41.4 us -> 37.1 us
    unnamed x19 -> x0, local copies, waits for them, and re-layouts: 9.38 us -> none
    pallas_call x1 -> x2, Pallas kernels: 41.4 us -> 37.1 us  [the longest x1 36.1 us: per_device(): pl.pallas_call(functools.partial(kernel, nx, ny), out_shape=tuple((pltpu....]
where the time goes in v2:
time: 37.9 us; the launch traced here: 37.8 us
  Pallas kernels  37.1 us (98%)
  between operations  0.64 us (2%)
    pallas_call x1, Pallas kernels, per_device(): pl.pallas_call(functools.partial(kernel, nx, ny), out_shape=tuple((pltpu....  36.1 us
    pallas_call x1, Pallas kernels, per_device(): pl.pallas_call(write_out, out_shape=outs, in_specs=[pl.BlockSpec(memory_s...  1.07 us

profile of v2, /device:TPU:1, one launch (start us, length us, event | category | flops | bytes accessed | tf_op | source)
XLA Modules:
  0.0 37.8 jit_solution(3636468982568402092)
XLA Ops:
  0.6 36.1 %shard_map.110 = (f32[75,8,128]{2,1,0:T(8,128)S(1)}, f32[75,8,128]{2,1,0:T(8,128)S(1)}, f32[75,8,128]{2,1,0:T(8,128)S(1)}, f32[75,8,128]{2,1,0:T(8,128)S(1)}, f32[8,128]{1,0:T(8,128)S(1)}) custom-call(f32[75,8,128]{2,1,0:T(8,128)} %t_in.1, f32[75,8,128]{2,1,0:T(8,128)} %s_in.1, f32[75,8,128]{2,1,0:T(8,128)} %u_in.1, f32[75,8,128]{2,1,0:T(8,128)} %v_in.1, ...), custom_call_target="tpu_custom_call" | custom-call | tf_op jit(solution)/shard_map/pallas_call | solution.py:640
  36.7 1.1 %shard_map.111 = (f32[75,8,128]{2,1,0:T(8,128)}, f32[75,8,128]{2,1,0:T(8,128)}, f32[75,8,128]{2,1,0:T(8,128)}, f32[75,8,128]{2,1,0:T(8,128)}, f32[8,128]{1,0:T(8,128)}) custom-call(f32[75,8,128]{2,1,0:T(8,128)S(1)} %get-tuple-element.10.refs_0_, f32[75,8,128]{2,1,0:T(8,128)S(1)} %get-tuple-element.11.refs_1_, f32[75,8,128]{2,1,0:T(8,128)S(1)} %get-tuple-element.12.refs_2_, ...), custom_call_target="tpu_custom_call" | custom-call | tf_op jit(solution)/shard_map/pallas_call | solution.py:678

commit v3 on v2

--- a/solution.py
+++ b/solution.py
@@ -22,7 +22,7 @@
 GRAVITY = 4.0
 DB = DT / SUBSTEPS
 
-AROUND = [(dx, dy) for dy in (-1, 0, 1) for dx in (-1, 0, 1) if (dx, dy) != (0, 0)]
+AROUND = [(-1, -1), (1, -1), (-1, 1), (1, 1), (-1, 0), (1, 0), (0, -1), (0, 1)]
 (G_2D, G_UV, G_W, G_SIDE, G_CORNER, G_POLE, G_TS, G_SUM, G_SIDE1, G_CORNER1, G_V1, G_UP, G_DOWN, G_UP1, G_DOWN1) = range(15)
 GROUPS = 15
 
@@ -66,6 +66,13 @@
     P1W,
     AX,
     AD,
+    EU,
+    EV,
+    HC,
+    CE,
+    FW,
+    AO,
+    EM,
     load_sem,
     send_sem,
     recv_sem,
@@ -118,7 +125,7 @@
     zero = jnp.zeros((ROWS, LANES), jnp.float32)
 
     def roll(x, shift):
-        return pltpu.roll(x, shift % LANES, 1)
+        return pltpu.roll(x, shift % LANES, x.ndim - 1)
 
     def packed(x, i):
         return roll(x, 8 * i + 4)
@@ -157,17 +164,6 @@
     own = (flag_v[...] * bottom_v[...]).astype(jnp.float32)
     D2[0, 1, 8:16, :] = own
     D2[2, 1, 8:16, :] = in_slots(own, (124, 125, 126, 127, 0, 1, 2, 3))
-
-    pl.semaphore_wait(barrier, len(AROUND))
-
-    for dx, dy in AROUND:
-        send(
-            G_2D,
-            D2.at[:, 1, pl.ds(8, 8), :],
-            D2.at[:, 1 - dx, pl.ds(8 * (1 - dy), 8), :],
-            dx,
-            dy,
-        )
 
     def rows(group, fields, count, dy):
         src, dst = (16 - count, 8 - count) if dy > 0 else (8, 16)
@@ -181,9 +177,6 @@
 
     for load in loads[3:]:
         load.wait()
-    for dy in (1, -1):
-        rows(G_UV, pl.ds(0, 2), 2, dy)
-
     def weight(t, s, dz):
         return (0.8 * s - t * (0.2 + 0.05 * t)) * dz
 
@@ -205,9 +198,16 @@
         for n in range(5):
             pack[n, c, 1:9, :] = held[n]
 
-    for dx in (1, -1):
-        side = PW if dx > 0 else PE
-        send(G_SIDE, pack.at[:, :, pl.ds(1, 8), :], side.at[:, :, pl.ds(1, 8), :], dx, 0)
+    pl.semaphore_wait(barrier, len(AROUND))
+
+    for dx, dy in AROUND:
+        send(
+            G_2D,
+            D2.at[:, 1, pl.ds(8, 8), :],
+            D2.at[:, 1 - dx, pl.ds(8 * (1 - dy), 8), :],
+            dx,
+            dy,
+        )
     for dx in (1, -1):
         for dy in (1, -1):
             side = PW if dx > 0 else PE
@@ -215,6 +215,11 @@
             send(
                 G_CORNER, pack.at[:, :, pl.ds(src, 1), :], side.at[:, :, pl.ds(dst, 1), :], dx, dy
             )
+    for dx in (1, -1):
+        side = PW if dx > 0 else PE
+        send(G_SIDE, pack.at[:, :, pl.ds(1, 8), :], side.at[:, :, pl.ds(1, 8), :], dx, 0)
+    for dy in (1, -1):
+        rows(G_UV, pl.ds(0, 2), 2, dy)
     for dy in (1, -1):
         src, dst = (8, 0) if dy > 0 else (1, 9)
         uv = pl.ds(0, 2)
@@ -317,46 +322,56 @@
     received(G_CORNER, size_corner)
     received(G_POLE, size_pole)
 
-    def edge_far(d, y):
-        z = 2.0 * y - 8.0 * d
-        return jnp.where(western, roll(d, -2), roll(d, 2)) + jnp.where(
-            at3, roll(z, -1), jnp.where(at4, roll(z, 1), 0.0)
-        )
-
     def far(a, y, yy):
         z = 2.0 * y - 8.0 * a
         return yy + roll(z + roll(a, -1), -1) + roll(z + roll(a, 1), 1)
 
+    group = lax.broadcasted_iota(jnp.int32, (NC, ROWS, LANES), 0).astype(jnp.float32)
+    lanes = lax.broadcasted_iota(jnp.int32, (NC, ROWS, LANES), 2)
+    level = lax.div(lanes, 8).astype(jnp.float32) + group * LC
+    slots = lax.rem(lanes, 8)
+    westerns, at3s, at4s = slots < 4, slots == 3, slots == 4
+
+    def beyond(west, east, f, r):
+        return jnp.where(westerns, west[f, :, r : r + 8, :], east[f, :, r : r + 8, :])
+
+    def if_wet(depths, n, r, x):
+        return jnp.where(level < depths[n, r + 7 : r + 15, :][None], x, 0.0)
+
+    def excess(f, depths, r):
+        return if_wet(depths, 0, r, beyond(PW, PE, f, r)) - if_wet(
+            depths, 1, r, pack[f, :, r : r + 8, :]
+        )
+
+    def edge_far(d, y):
+        z = 2.0 * y - 8.0 * d
+        return jnp.where(westerns, roll(d, -2), roll(d, 2)) + jnp.where(
+            at3s, roll(z, -1), jnp.where(at4s, roll(z, 1), 0.0)
+        )
+
+    du_s, du, du_n = [excess(0, SU, r) for r in range(3)]
+    dv_s, dv, dv_n = [excess(1, SV, r) for r in range(3)]
+    dw = beyond(PW, PE, 2, 1) - pack[2, :, 1:9, :]
+    dw = jnp.where(at3s, roll(dw, -1), 0.0)
+    run = dw
+    for shift in (8, 16, 32, 64):
+        run = run + jnp.where(lanes >= shift, roll(run, shift), 0.0)
+    whole = jnp.broadcast_to(run[:, :, 8 * LC - 5 : 8 * LC - 4], run.shape)
+    above = [zero]
+    for c in range(NC - 1):
+        above.append(above[-1] + whole[c])
+    run = run + jnp.stack(above)
+    EU[...] = jnp.where(at3s, f4[None] * roll(dv + dv_s, -1) - run + 0.5 * dw, 0.0) - (
+        DT * NU
+    ) * edge_far(du, du_n + du_s)
+    EV[...] = jnp.where(at4s, -f4[None] * roll(du + du_n, 1), 0.0) - (DT * NU) * edge_far(
+        dv, dv_n + dv_s
+    )
+
     def momentum(c, carry):
-        cum_e, cum_n, edge_cum, sum_u0, sum_v0, sum_u, sum_v = carry
+        cum_e, cum_n, sum_u0, sum_v0, sum_u, sum_v = carry
         base = (c * LC).astype(jnp.float32)
-        level = slot + base
-
-        def excess(f, depths, r):
-            beyond = jnp.where(western, PW[f, c, r : r + 8, :], PE[f, c, r : r + 8, :])
-            beyond = jnp.where(level < depths[0, r + 7 : r + 15, :], beyond, 0.0)
-            return beyond - jnp.where(
-                level < depths[1, r + 7 : r + 15, :], pack[f, c, r : r + 8, :], 0.0
-            )
-
-        du_s, du, du_n = [excess(0, SU, r) for r in range(3)]
-        dv_s, dv, dv_n = [excess(1, SV, r) for r in range(3)]
-        dw = jnp.where(western, PW[2, c, 1:9, :], PE[2, c, 1:9, :]) - pack[2, c, 1:9, :]
-        dw = jnp.where(at3, roll(dw, -1), 0.0)
-        run = dw
-        for shift in (8, 16, 32, 64):
-            run = run + jnp.where(lane >= shift, roll(run, shift), 0.0)
-        run = run + edge_cum
-        edge_cum = jnp.broadcast_to(run[:, 8 * LC - 5 : 8 * LC - 4], run.shape)
-        edge_u = (
-            jnp.where(at3, f4 * roll(dv + dv_s, -1) - run + 0.5 * dw, 0.0)
-            - (DT * NU) * edge_far(du, du_n + du_s)
-        )
-        edge_v = (
-            jnp.where(at4, -f4 * roll(du + du_n, 1), 0.0)
-            - (DT * NU) * edge_far(dv, dv_n + dv_s)
-        )
-
+        edge_u, edge_v = EU[c], EV[c]
         cu0, cv0 = CU[8:16, :] - base, CV[8:16, :] - base
         held_u = held_v = zero
         for i in range(LC):
@@ -400,9 +415,9 @@
             held_v = jnp.where(slot == i, packed(v1, i), held_v)
         pack1[0, c] = held_u
         pack1[1, c] = held_v
-        return cum_e, cum_n, edge_cum, sum_u0, sum_v0, sum_u, sum_v
-
-    sums = lax.fori_loop(0, NC, momentum, (zero,) * 7)[3:]
+        return cum_e, cum_n, sum_u0, sum_v0, sum_u, sum_v
+
+    sums = lax.fori_loop(0, NC, momentum, (zero,) * 6)[2:]
 
     for n in range(4):
         F2[n, 1, 8:16, :] = sums[n]
@@ -428,17 +443,23 @@
     left(G_TS, size_ts)
     received(G_TS, size_ts)
 
+    for f in range(2):
+        HC[f] = if_wet(SC, 0, 1, beyond(PW, PE, 3 + f, 1))
+
     @pl.loop(0, NC)
     def _(c):
         base = (c * LC).astype(jnp.float32)
-        low, high = CC[7:15, :] - base, CC[9:17, :] - base
-        for f in (2, 3):
+        low, mid, high = [CC[r : r + 8, :] - base for r in (7, 8, 9)]
+        for f in range(2):
+            edge = HC[f, c]
             for i in range(LC):
                 k = c * LC + i
-                a = jnp.where(low > i, X[f, k, 7:15, :], 0.0)
-                b = jnp.where(high > i, X[f, k, 9:17, :], 0.0)
-                X[f, k, 7:15, :] = a
-                X[f, k, 9:17, :] = b
+                south = jnp.where(low > i, X[2 + f, k, 7:15, :], 0.0)
+                here = jnp.where(mid > i, X[2 + f, k, 8:16, :], 0.0)
+                north = jnp.where(high > i, X[2 + f, k, 9:17, :], 0.0)
+                X[2 + f, k, 7:15, :] = south
+                X[2 + f, k, 9:17, :] = north
+                CE[f, k] = here + roll(jnp.where(first, unpacked(edge, i), here), -1)
 
     def both(op, *pairs):
         return [op(*xs) for xs in zip(*pairs)]
@@ -452,8 +473,9 @@
     depth_v = both(depth_of, cv)
     pull_u = both(lambda o, d: o * d * (DB * GRAVITY), open_u, depth_u)
     pull_v = both(lambda o, d: o * d * (DB * GRAVITY), open_v, depth_v)
+    pull_w = ring_west(*pull_u)
     ease = both(lambda o: jnp.where(o, DB, 0.0), ocean)
-    level = [jnp.where(o, x, 0.0) for o, x in zip(ocean, sides(D2, 1))]
+    height = [jnp.where(o, x, 0.0) for o, x in zip(ocean, sides(D2, 1))]
 
     received(G_SUM, size_sum)
     u0, v0, u_all, v_all = [list(sides(F2, f)) for f in range(4)]
@@ -465,7 +487,11 @@
     run_v = run_u
 
     def substep(_, state):
-        level, trans_u, trans_v, run_u, run_v = state
+        level, trans_u, trans_w, trans_v, run_u, run_v = state
+        level_w = ring_west(*level)
+        trans_w = both(
+            lambda t, p, q, h, w: t + (p - q * (h - w)), trans_w, push_w, pull_w, level, level_w
+        )
         trans_u = both(
             lambda t, p, q, e, h: t + (p - q * (e - h)),
             trans_u,
@@ -482,17 +508,18 @@
             level,
             ease,
             trans_u,
-            ring_west(*trans_u),
+            trans_w,
             trans_v,
         )
-        return level, trans_u, trans_v, both(jnp.add, run_u, trans_u), both(jnp.add, run_v, trans_v)
-
-    state = level, trans_u, trans_v, run_u, run_v
+        return level, trans_u, trans_w, trans_v, both(jnp.add, run_u, trans_u), both(jnp.add, run_v, trans_v)
+
+    trans_w, push_w = ring_west(*trans_u), ring_west(*push_u)
+    state = height, trans_u, trans_w, trans_v, run_u, run_v
     for n in range(SUBSTEPS):
         state = substep(n, state)
-    level, _, _, run_u, run_v = state
-
-    HN[...] = level[0][8:16]
+    height, _, _, _, run_u, run_v = state
+
+    HN[...] = height[0][8:16]
 
     def shift(r, a, d, o):
         return (r * (1.0 / SUBSTEPS) - a) / (d + (1.0 - o))
@@ -512,32 +539,37 @@
     received(G_V1, size_v1)
     half = 0.5 * DTT
 
+    edge_u = if_wet(SU, 0, 1, beyond(P1W, P1E, 0, 1) + DP[0][None]) * half
+    edge_v = if_wet(SV, 0, 1, beyond(P1W, P1E, 1, 1) + DP[1][None]) * half
+    edge_vs = if_wet(SV, 0, 0, beyond(P1W, P1E, 1, 0) + DP[2][None]) * half
+    last_u = if_wet(SU, 1, 1, pack1[0] + DP[3][None]) * half
+    for f in range(2):
+        south = if_wet(SC, 0, 0, beyond(PW, PE, 3 + f, 0))
+        here = HC[f]
+        north = if_wet(SC, 0, 2, beyond(PW, PE, 3 + f, 2))
+        inner = if_wet(SC, 1, 1, pack[3 + f, :, 1:9, :])
+        flux = edge_u * (here + roll(jnp.where(at4s, inner, here), -1))
+        flux_last = last_u * (inner + roll(here, -1))
+        flux_west = roll(jnp.where(at3s, flux_last, flux), 1)
+        a = here - ((flux - flux_west) + (edge_v * (here + north) - edge_vs * (south + here)))
+        FW[f] = flux
+        AO[f] = if_wet(SC, 0, 1, a)
+
+    def send_rows(c, up):
+        src, dst, dy, group = (14, 6, 1, G_UP) if up else (8, 16, -1, G_DOWN)
+        levels = pl.ds(c * LC, LC)
+        send(
+            group,
+            AX.at[:, levels, pl.ds(src, 2), :],
+            AX.at[:, levels, pl.ds(dst, 2), :],
+            0,
+            dy,
+        )
+
     @pl.loop(0, NC)
     def _(c):
         base = (c * LC).astype(jnp.float32)
-        level = slot + base
-
-        def beyond(west, east, f, r):
-            return jnp.where(western, west[f, c, r : r + 8, :], east[f, c, r : r + 8, :])
-
-        edge_u = jnp.where(level < SU[0, 8:16, :], beyond(P1W, P1E, 0, 1) + DP[0], 0.0) * half
-        edge_v = jnp.where(level < SV[0, 8:16, :], beyond(P1W, P1E, 1, 1) + DP[1], 0.0) * half
-        edge_vs = jnp.where(level < SV[0, 7:15, :], beyond(P1W, P1E, 1, 0) + DP[2], 0.0) * half
-        last_u = jnp.where(level < SU[1, 8:16, :], pack1[0, c] + DP[3], 0.0) * half
-        edges, outer = [], []
-        for f in (3, 4):
-            south, here, north = [
-                jnp.where(level < SC[0, r + 7 : r + 15, :], beyond(PW, PE, f, r), 0.0)
-                for r in range(3)
-            ]
-            inner = jnp.where(level < SC[1, 8:16, :], pack[f, c, 1:9, :], 0.0)
-            flux = edge_u * (here + roll(jnp.where(at4, inner, here), -1))
-            flux_last = last_u * (inner + roll(here, -1))
-            flux_west = roll(jnp.where(at3, flux_last, flux), 1)
-            a = here - ((flux - flux_west) + (edge_v * (here + north) - edge_vs * (south + here)))
-            outer.append(jnp.where(level < SC[0, 8:16, :], a, 0.0))
-            edges.append(jnp.where(at3, flux, here))
-
+        edges = [FW[f, c] for f in range(2)]
         cc0, cu0, cv0 = CC[8:16, :] - base, CU[8:16, :] - base, CV[8:16, :] - base
         cvs = CV[7:15, :] - base
         held = [zero, zero]
@@ -553,7 +585,7 @@
             for f in range(2):
                 south, here, north = [X[2 + f, k, r : r + 8, :] for r in (7, 8, 9)]
                 edge = unpacked(edges[f], i)
-                flux = u * (here + roll(jnp.where(first, edge, here), -1))
+                flux = u * CE[f, k]
                 a = here - (
                     (flux - roll(jnp.where(last, edge, flux), 1))
                     + (v * (here + north) - vs * (south + here))
@@ -562,16 +594,22 @@
                 AX[f, k, 8:16, :] = a
                 held[f] = jnp.where(slot == i, packed(a, i), held[f])
         for f in range(2):
-            AD[f, c, 1:9, :] = outer[f] - held[f]
+            AD[f, c, 1:9, :] = AO[f, c] - held[f]
+
+        @pl.when(has_north)
+        def _():
+            send_rows(c, True)
+
+        @pl.when(has_south)
+        def _():
+            send_rows(c, False)
 
     @pl.when(has_north)
     def _():
-        send(G_UP, AX.at[:, :, pl.ds(14, 2), :], AX.at[:, :, pl.ds(6, 2), :], 0, 1)
         send(G_UP1, AD.at[:, :, pl.ds(8, 1), :], AD.at[:, :, pl.ds(0, 1), :], 0, 1)
 
     @pl.when(has_south)
     def _():
-        send(G_DOWN, AX.at[:, :, pl.ds(8, 2), :], AX.at[:, :, pl.ds(16, 2), :], 0, -1)
         send(G_DOWN1, AD.at[:, :, pl.ds(1, 1), :], AD.at[:, :, pl.ds(9, 1), :], 0, -1)
 
     left(G_SUM, size_sum)
@@ -589,14 +627,15 @@
         received(G_DOWN, size_a)
         received(G_DOWN1, size_ad)
 
+    for f in range(2):
+        south, here, north = [AD[f, :, r : r + 8, :] for r in range(3)]
+        EM[f] = KAPPA * edge_far(here, south + north)
+
     @pl.loop(0, NC)
     def _(c):
         base = (c * LC).astype(jnp.float32)
         cc0 = CC[8:16, :] - base
-        edges = []
-        for f in range(2):
-            south, here, north = [AD[f, c, r : r + 8, :] for r in range(3)]
-            edges.append(KAPPA * edge_far(here, south + north))
+        edges = [EM[f, c] for f in range(2)]
         for i in range(LC):
             k = c * LC + i
             for f, out in ((0, TN), (1, SN)):
@@ -667,6 +706,13 @@
             vmem(2, NC, 16, LANES),
             vmem(2, K, 24, LANES),
             vmem(2, NC, 16, LANES),
+            vmem(NC, ROWS, LANES),
+            vmem(NC, ROWS, LANES),
+            vmem(2, NC, ROWS, LANES),
+            vmem(2, K, ROWS, LANES),
+            vmem(2, NC, ROWS, LANES),
+            vmem(2, NC, ROWS, LANES),
+            vmem(2, NC, ROWS, LANES),
             pltpu.SemaphoreType.DMA((7,)),
             pltpu.SemaphoreType.DMA((GROUPS,)),
             pltpu.SemaphoreType.DMA((GROUPS,)),

time: 37.9 us -> 34.1 us (0.90)
  Pallas kernels: 37.1 us -> 33.3 us
    pallas_call x1, Pallas kernels: 36.1 us -> 32.3 us  [per_device(): pl.pallas_call(functools.partial(kernel, nx, ny), out_shape=tuple((pltpu....]
where the time goes in v3:
time: 34.1 us; the launch traced here: 34 us
  Pallas kernels  33.3 us (98%)
  between operations  0.64 us (2%)
    pallas_call x1, Pallas kernels, per_device(): pl.pallas_call(functools.partial(kernel, nx, ny), out_shape=tuple((pltpu....  32.3 us
    pallas_call x1, Pallas kernels, per_device(): pl.pallas_call(write_out, out_shape=outs, in_specs=[pl.BlockSpec(memory_s...  1.07 us

profile of v3, /device:TPU:1, one launch (start us, length us, event | category | flops | bytes accessed | tf_op | source)
XLA Modules:
  0.0 34.0 jit_solution(12231685817834271444)
XLA Ops:
  0.6 32.3 %shard_map.110 = (f32[75,8,128]{2,1,0:T(8,128)S(1)}, f32[75,8,128]{2,1,0:T(8,128)S(1)}, f32[75,8,128]{2,1,0:T(8,128)S(1)}, f32[75,8,128]{2,1,0:T(8,128)S(1)}, f32[8,128]{1,0:T(8,128)S(1)}) custom-call(f32[75,8,128]{2,1,0:T(8,128)} %t_in.1, f32[75,8,128]{2,1,0:T(8,128)} %s_in.1, f32[75,8,128]{2,1,0:T(8,128)} %u_in.1, f32[75,8,128]{2,1,0:T(8,128)} %v_in.1, ...), custom_call_target="tpu_custom_call" | custom-call | tf_op jit(solution)/shard_map/pallas_call | solution.py:679
  32.9 1.1 %shard_map.111 = (f32[75,8,128]{2,1,0:T(8,128)}, f32[75,8,128]{2,1,0:T(8,128)}, f32[75,8,128]{2,1,0:T(8,128)}, f32[75,8,128]{2,1,0:T(8,128)}, f32[8,128]{1,0:T(8,128)}) custom-call(f32[75,8,128]{2,1,0:T(8,128)S(1)} %get-tuple-element.10.refs_0_, f32[75,8,128]{2,1,0:T(8,128)S(1)} %get-tuple-element.11.refs_1_, f32[75,8,128]{2,1,0:T(8,128)S(1)} %get-tuple-element.12.refs_2_, ...), custom_call_target="tpu_custom_call" | custom-call | tf_op jit(solution)/shard_map/pallas_call | solution.py:724

commit v4 on v3

--- a/solution.py
+++ b/solution.py
@@ -11,6 +11,8 @@
 K = 75
 NC = 5
 LC = K // NC
+NM = 5
+LM = K // NM
 SUBSTEPS = 8
 ROWS = 8
 LANES = 128
@@ -23,8 +25,8 @@
 DB = DT / SUBSTEPS
 
 AROUND = [(-1, -1), (1, -1), (-1, 1), (1, 1), (-1, 0), (1, 0), (0, -1), (0, 1)]
-(G_2D, G_UV, G_W, G_SIDE, G_CORNER, G_POLE, G_TS, G_SUM, G_SIDE1, G_CORNER1, G_V1, G_UP, G_DOWN, G_UP1, G_DOWN1) = range(15)
-GROUPS = 15
+GROUPS = 7
+G_2D, G_A, G_TS, G_SUM, G_B, G_UP, G_DOWN = range(GROUPS)
 
 
 def kernel(
@@ -53,9 +55,14 @@
     SC,
     SU,
     SV,
+    SU4,
+    SV4,
     pack,
     PE,
     PW,
+    pack_ts,
+    TE,
+    TW,
     F2,
     DV,
     DP,
@@ -98,47 +105,43 @@
     def left(group, size):
         pltpu.make_async_copy(size, size, send_sem.at[group]).wait()
 
-    loads = [
-        pltpu.make_async_copy(flag_in, flag_v, load_sem.at[5]),
-        pltpu.make_async_copy(bottom_in, bottom_v, load_sem.at[6]),
-        pltpu.make_async_copy(h_in, D2.at[1, 1, pl.ds(8, 8), :], load_sem.at[4]),
-        pltpu.make_async_copy(u_in, X.at[0, :, pl.ds(8, 8), :], load_sem.at[0]),
-        pltpu.make_async_copy(v_in, X.at[1, :, pl.ds(8, 8), :], load_sem.at[1]),
-        pltpu.make_async_copy(t_in, X.at[2, :, pl.ds(8, 8), :], load_sem.at[2]),
-        pltpu.make_async_copy(s_in, X.at[3, :, pl.ds(8, 8), :], load_sem.at[3]),
-    ]
-    for load in loads:
-        load.start()
-
     barrier = pltpu.get_barrier_semaphore()
     for dx, dy in AROUND:
         pl.semaphore_signal(barrier, inc=1, device_id=device(dx, dy), device_id_type=MESH)
 
+    pltpu.make_async_copy(flag_in, flag_v, load_sem.at[0]).start()
+    pltpu.make_async_copy(bottom_in, bottom_v, load_sem.at[0]).start()
+    pltpu.make_async_copy(h_in, D2.at[1, 1, pl.ds(8, 8), :], load_sem.at[0]).start()
+    for f, source in enumerate((u_in, v_in, t_in, s_in)):
+        pltpu.make_async_copy(source, X.at[f, :, pl.ds(8, 8), :], load_sem.at[1]).start()
+
+    def loaded(sem, size):
+        pltpu.make_async_copy(size, size, load_sem.at[sem]).wait()
+
     lane = lax.broadcasted_iota(jnp.int32, (ROWS, LANES), 1)
-    lane8 = lax.rem(lane, 8)
     slot = lax.div(lane, 8).astype(jnp.float32)
     row = lax.broadcasted_iota(jnp.int32, (ROWS, LANES), 0)
     first, last = lane == 0, lane == LANES - 1
     edge4 = jnp.logical_or(lane < 2, lane >= LANES - 2)
-    western, at3, at4 = lane8 < 4, lane8 == 3, lane8 == 4
+    slot4 = lax.div(lane, 4).astype(jnp.float32)
     has_south, has_north = gy > 0, gy < ny - 1
     zero = jnp.zeros((ROWS, LANES), jnp.float32)
 
     def roll(x, shift):
         return pltpu.roll(x, shift % LANES, x.ndim - 1)
 
-    def packed(x, i):
-        return roll(x, 8 * i + 4)
-
-    def unpacked(x, i):
-        return roll(x, LANES - 4 - 8 * i)
-
-    def in_slots(x, lanes):
-        l8 = lax.rem(lax.broadcasted_iota(jnp.int32, x.shape, 1), 8)
+    def packed(x, i, width=8):
+        return roll(x, width * i + width // 2)
+
+    def unpacked(x, i, width=8):
+        return roll(x, LANES - width // 2 - width * i)
+
+    def in_slots(x, lanes, width=8):
+        at = lax.rem(lax.broadcasted_iota(jnp.int32, x.shape, 1), width)
         out = None
         for l in lanes:
             column = jnp.broadcast_to(x[:, l : l + 1], x.shape)
-            out = column if out is None else jnp.where(l8 == (l + 4) % LANES, column, out)
+            out = column if out is None else jnp.where(at == (l + width // 2) % LANES, column, out)
         return out
 
     @pl.when(jnp.logical_not(has_south))
@@ -159,8 +162,7 @@
             for f in range(2):
                 AX[f, k, 16:18, :] = jnp.zeros((2, LANES), jnp.float32)
 
-    for load in loads[:3]:
-        load.wait()
+    loaded(0, AX.at[0, pl.ds(0, 3), pl.ds(8, 8), :])
     own = (flag_v[...] * bottom_v[...]).astype(jnp.float32)
     D2[0, 1, 8:16, :] = own
     D2[2, 1, 8:16, :] = in_slots(own, (124, 125, 126, 127, 0, 1, 2, 3))
@@ -175,72 +177,93 @@
             dy,
         )
 
-    for load in loads[3:]:
-        load.wait()
+    loaded(1, X.at[:, :, pl.ds(8, 8), :])
     def weight(t, s, dz):
         return (0.8 * s - t * (0.2 + 0.05 * t)) * dz
 
     def thickness(base, i):
         return 0.5 / K + (base + (i + 0.5)) * (1.0 / (K * K))
 
-    @pl.loop(0, NC)
+    @pl.loop(0, NM)
     def _(c):
-        base = (c * LC).astype(jnp.float32)
+        base = (c * LM).astype(jnp.float32)
         depth = D2[0, 1, 8:16, :] - base
-        held = [zero] * 5
-        for i in range(LC):
-            k = c * LC + i
+        held = [zero] * 3
+        for i in range(LM):
+            k = c * LM + i
             u, v, t, s = [X[f, k, 8:16, :] for f in range(4)]
             w = jnp.where(depth > i, weight(t, s, DT * thickness(base, i)), 0.0)
             WX[k, 0:8, :] = w
-            for n, x in enumerate((u, v, w, t, s)):
-                held[n] = jnp.where(slot == i, packed(x, i), held[n])
-        for n in range(5):
+            for n, x in enumerate((u, v, w)):
+                held[n] = jnp.where(slot4 == i, packed(x, i, 4), held[n])
+        for n in range(3):
             pack[n, c, 1:9, :] = held[n]
 
     pl.semaphore_wait(barrier, len(AROUND))
 
-    for dx, dy in AROUND:
-        send(
-            G_2D,
-            D2.at[:, 1, pl.ds(8, 8), :],
-            D2.at[:, 1 - dx, pl.ds(8 * (1 - dy), 8), :],
-            dx,
-            dy,
-        )
-    for dx in (1, -1):
-        for dy in (1, -1):
-            side = PW if dx > 0 else PE
-            src, dst = (8, 0) if dy > 0 else (1, 9)
+    def corners(group, src, west, east, fields):
+        for dx in (1, -1):
+            for dy in (1, -1):
+                side = west if dx > 0 else east
+                r_src, r_dst = (8, 0) if dy > 0 else (1, 9)
+                send(
+                    group,
+                    src.at[fields, :, pl.ds(r_src, 1), :],
+                    side.at[fields, :, pl.ds(r_dst, 1), :],
+                    dx,
+                    dy,
+                )
+
+    def spread(group, ref, around):
+        for dx, dy in around:
             send(
-                G_CORNER, pack.at[:, :, pl.ds(src, 1), :], side.at[:, :, pl.ds(dst, 1), :], dx, dy
+                group,
+                ref.at[:, 1, pl.ds(8, 8), :],
+                ref.at[:, 1 - dx, pl.ds(8 * (1 - dy), 8), :],
+                dx,
+                dy,
             )
+
+    uv = pl.ds(0, 2)
+    spread(G_2D, D2, AROUND[:4])
+    corners(G_A, pack, PW, PE, uv)
+    spread(G_2D, D2, AROUND[4:6])
     for dx in (1, -1):
         side = PW if dx > 0 else PE
-        send(G_SIDE, pack.at[:, :, pl.ds(1, 8), :], side.at[:, :, pl.ds(1, 8), :], dx, 0)
+        send(G_A, pack.at[:, :, pl.ds(1, 8), :], side.at[:, :, pl.ds(1, 8), :], dx, 0)
+    spread(G_2D, D2, AROUND[6:])
     for dy in (1, -1):
-        rows(G_UV, pl.ds(0, 2), 2, dy)
+        rows(G_A, uv, 2, dy)
     for dy in (1, -1):
         src, dst = (8, 0) if dy > 0 else (1, 9)
-        uv = pl.ds(0, 2)
-        send(G_POLE, pack.at[uv, :, pl.ds(src, 1), :], pack.at[uv, :, pl.ds(dst, 1), :], 0, dy)
-    send(G_W, WX.at[:, pl.ds(0, 1), :], WX.at[:, pl.ds(8, 1), :], 0, -1)
+        send(G_A, pack.at[uv, :, pl.ds(src, 1), :], pack.at[uv, :, pl.ds(dst, 1), :], 0, dy)
+    send(G_A, WX.at[:, pl.ds(0, 1), :], WX.at[:, pl.ds(8, 1), :], 0, -1)
+
+    @pl.loop(0, NC)
+    def _(c):
+        held = [zero] * 2
+        for i in range(LC):
+            for f in range(2):
+                held[f] = jnp.where(slot == i, packed(X[2 + f, c * LC + i, 8:16, :], i), held[f])
+        for f in range(2):
+            pack_ts[f, c, 1:9, :] = held[f]
+
+    for dx in (1, -1):
+        side = TW if dx > 0 else TE
+        send(G_TS, pack_ts.at[:, :, pl.ds(1, 8), :], side.at[:, :, pl.ds(1, 8), :], dx, 0)
+    corners(G_TS, pack_ts, TW, TE, uv)
     for dy in (1, -1):
         rows(G_TS, pl.ds(2, 2), 1, dy)
 
-    size_2d = X.at[0, pl.ds(0, 24), pl.ds(0, 8), :]
-    size_uv = X.at[pl.ds(0, 2), :, pl.ds(0, 4), :]
-    size_w = X.at[0, :, pl.ds(0, 1), :]
-    size_side = PE.at[:, :, pl.ds(0, 16), :]
-    size_corner = PE.at[:, :, pl.ds(0, 4), :]
-    size_pole = PE.at[pl.ds(0, 2), :, pl.ds(0, 2), :]
-    size_ts = X.at[pl.ds(0, 2), :, pl.ds(0, 2), :]
-    size_sum = X.at[0, pl.ds(0, 32), pl.ds(0, 8), :]
-    size_side1 = P1E.at[:, :, pl.ds(0, 16), :]
-    size_corner1 = P1E.at[0, :, pl.ds(0, 2), :]
-    size_v1 = V1X.at[:, pl.ds(0, 1), :]
-    size_a = X.at[pl.ds(0, 2), :, pl.ds(0, 2), :]
-    size_ad = AD.at[:, :, pl.ds(0, 1), :]
+    def size(levels, count):
+        return X.at[0, pl.ds(0, levels), pl.ds(0, count), :]
+
+    size_2d = size(24, 8)
+    size_a = size(K, 13)
+    size_ts = size(50, 10)
+    size_sum = size(32, 8)
+    size_b = size(49, 5)
+    size_c = size(62, 5)
 
     received(G_2D, size_2d)
     row24 = lax.broadcasted_iota(jnp.int32, (24, LANES), 0)
@@ -285,6 +308,8 @@
     ]
     edge_cu = [jnp.minimum(a, b) for a, b in zip(edge_col, ring_east(*edge_col, slot24 == 4))]
     for n in range(2):
+        SU4[n] = in_slots(cu[1 - n], (126, 127, 0, 1), 4)
+        SV4[n] = in_slots(cv[1 - n], (126, 127, 0, 1), 4)
         SC[n] = edge_col[n]
         SU[n] = edge_cu[n]
         SV[n] = jnp.minimum(edge_col[n], north24(edge_col[n]))
@@ -302,8 +327,8 @@
     centre_uv = 1.0 - (DT * NU) * at_wall
     centre_ts = 1.0 - KAPPA * at_wall
 
-    received(G_UV, size_uv)
-    left(G_UV, size_uv)
+    received(G_A, size_a)
+    left(G_A, size_a)
 
     @pl.loop(0, NC)
     def _(c):
@@ -317,91 +342,96 @@
                 X[f, k, 6:14, :] = a
                 X[f, k, 10:18, :] = b
 
-    received(G_W, size_w)
-    received(G_SIDE, size_side)
-    received(G_CORNER, size_corner)
-    received(G_POLE, size_pole)
-
     def far(a, y, yy):
         z = 2.0 * y - 8.0 * a
         return yy + roll(z + roll(a, -1), -1) + roll(z + roll(a, 1), 1)
 
-    group = lax.broadcasted_iota(jnp.int32, (NC, ROWS, LANES), 0).astype(jnp.float32)
-    lanes = lax.broadcasted_iota(jnp.int32, (NC, ROWS, LANES), 2)
-    level = lax.div(lanes, 8).astype(jnp.float32) + group * LC
-    slots = lax.rem(lanes, 8)
-    westerns, at3s, at4s = slots < 4, slots == 3, slots == 4
-
-    def beyond(west, east, f, r):
-        return jnp.where(westerns, west[f, :, r : r + 8, :], east[f, :, r : r + 8, :])
-
-    def if_wet(depths, n, r, x):
-        return jnp.where(level < depths[n, r + 7 : r + 15, :][None], x, 0.0)
+    class Slots:
+        def __init__(self, count, width):
+            shape = (count, ROWS, LANES)
+            self.lanes = lax.broadcasted_iota(jnp.int32, shape, 2)
+            self.place = lax.rem(self.lanes, width)
+            tile = lax.broadcasted_iota(jnp.int32, shape, 0)
+            self.level = (lax.div(self.lanes, width) + tile * (K // count)).astype(jnp.float32)
+            self.west, self.east = self.place == width // 2 - 1, self.place == width // 2
+            self.western = self.place < width // 2
+
+        def beyond(self, west, east, f, r):
+            return jnp.where(self.western, west[f, :, r : r + 8, :], east[f, :, r : r + 8, :])
+
+        def if_wet(self, depths, n, r, x):
+            return jnp.where(self.level < depths[n, r + 7 : r + 15, :][None], x, 0.0)
+
+        def far(self, d, y):
+            z = 2.0 * y - 8.0 * d
+            return jnp.where(self.western, roll(d, -2), roll(d, 2)) + jnp.where(
+                self.west, roll(z, -1), jnp.where(self.east, roll(z, 1), 0.0)
+            )
+
+    by4, by8 = Slots(NM, 4), Slots(NC, 8)
 
     def excess(f, depths, r):
-        return if_wet(depths, 0, r, beyond(PW, PE, f, r)) - if_wet(
+        return by4.if_wet(depths, 0, r, by4.beyond(PW, PE, f, r)) - by4.if_wet(
             depths, 1, r, pack[f, :, r : r + 8, :]
         )
 
-    def edge_far(d, y):
-        z = 2.0 * y - 8.0 * d
-        return jnp.where(westerns, roll(d, -2), roll(d, 2)) + jnp.where(
-            at3s, roll(z, -1), jnp.where(at4s, roll(z, 1), 0.0)
-        )
-
-    du_s, du, du_n = [excess(0, SU, r) for r in range(3)]
-    dv_s, dv, dv_n = [excess(1, SV, r) for r in range(3)]
-    dw = beyond(PW, PE, 2, 1) - pack[2, :, 1:9, :]
-    dw = jnp.where(at3s, roll(dw, -1), 0.0)
+    du_s, du, du_n = [excess(0, SU4, r) for r in range(3)]
+    dv_s, dv, dv_n = [excess(1, SV4, r) for r in range(3)]
+    dw = by4.beyond(PW, PE, 2, 1) - pack[2, :, 1:9, :]
+    dw = jnp.where(by4.west, roll(dw, -1), 0.0)
     run = dw
-    for shift in (8, 16, 32, 64):
-        run = run + jnp.where(lanes >= shift, roll(run, shift), 0.0)
-    whole = jnp.broadcast_to(run[:, :, 8 * LC - 5 : 8 * LC - 4], run.shape)
+    for shift in (4, 8, 16, 32, 64):
+        run = run + jnp.where(by4.lanes >= shift, roll(run, shift), 0.0)
+    whole = jnp.broadcast_to(run[:, :, 4 * LM - 3 : 4 * LM - 2], run.shape)
     above = [zero]
-    for c in range(NC - 1):
+    for c in range(NM - 1):
         above.append(above[-1] + whole[c])
     run = run + jnp.stack(above)
-    EU[...] = jnp.where(at3s, f4[None] * roll(dv + dv_s, -1) - run + 0.5 * dw, 0.0) - (
+    EU[...] = jnp.where(by4.west, f4[None] * roll(dv + dv_s, -1) - run + 0.5 * dw, 0.0) - (
         DT * NU
-    ) * edge_far(du, du_n + du_s)
-    EV[...] = jnp.where(at4s, -f4[None] * roll(du + du_n, 1), 0.0) - (DT * NU) * edge_far(
+    ) * by4.far(du, du_n + du_s)
+    EV[...] = jnp.where(by4.east, -f4[None] * roll(du + du_n, 1), 0.0) - (DT * NU) * by4.far(
         dv, dv_n + dv_s
     )
 
     def momentum(c, carry):
-        cum_e, cum_n, sum_u0, sum_v0, sum_u, sum_v = carry
-        base = (c * LC).astype(jnp.float32)
+        cum, cum_n, sum_u0, sum_v0, sum_u, sum_v = carry
+        base = (c * LM).astype(jnp.float32)
         edge_u, edge_v = EU[c], EV[c]
         cu0, cv0 = CU[8:16, :] - base, CV[8:16, :] - base
-        held_u = held_v = zero
-        for i in range(LC):
-            k = c * LC + i
+        for i in range(LM):
+            k = c * LM + i
             dz = thickness(base, i)
             uss, us, u, un, unn = [X[0, k, r : r + 8, :] for r in range(6, 11)]
             vss, vs, v, vn, vnn = [X[1, k, r : r + 8, :] for r in range(6, 11)]
             w, wn = WX[k, 0:8, :], WX[k, 1:9, :]
-            step_e = roll(w, -1) - w
+            cum = cum + w
+            load = cum - 0.5 * w
             step_n = wn - w
-            cum_e = cum_e + step_e
             cum_n = cum_n + step_n
-            uu = u + un
-            vv = v + vs
-            uu = uu + roll(uu, 1)
-            vv = vv + roll(vv, -1)
-            yu, yv = un + us, vn + vs
+            cross_u = f4 * (v + vs)
+            cross_v = f4 * (u + un)
+            yu, yv = (DT * NU) * (un + us), (DT * NU) * (vn + vs)
+            au, av = (DT * NU) * u, (DT * NU) * v
+            zu, zv = 8.0 * au - 2.0 * yu, 8.0 * av - 2.0 * yv
             u1 = (
                 centre_uv * u
-                + f4 * vv
-                - (cum_e - 0.5 * step_e)
-                - (DT * NU) * (far(u, yu, unn + uss) - 8.0 * yu)
-                + jnp.where(edge4, unpacked(edge_u, i), 0.0)
+                + 8.0 * yu
+                - (DT * NU) * (unn + uss)
+                + (cross_u + load)
+                + roll((zu - roll(au, -1)) + (cross_u - load), -1)
+                + roll(zu - roll(au, 1), 1)
+                + jnp.where(edge4, unpacked(edge_u, i, 4), 0.0)
             )
             v1 = (
                 centre_uv * v
-                - f4 * uu
+                + 8.0 * yv
+                - (DT * NU) * (vnn + vss)
+                - cross_v
                 - (cum_n - 0.5 * step_n)
-                - (DT * NU) * (far(v, yv, vnn + vss) - 8.0 * yv)
-                + jnp.where(edge4, unpacked(edge_v, i), 0.0)
+                + roll(zv - roll(av, -1), -1)
+                + roll((zv - roll(av, 1)) - cross_v, 1)
+                + jnp.where(edge4, unpacked(edge_v, i, 4), 0.0)
             )
             u1 = jnp.where(cu0 > i, u1, 0.0)
             v1 = jnp.where(cv0 > i, v1, 0.0)
@@ -411,40 +441,36 @@
             sum_v = sum_v + v1 * dz
             U1B[k] = u1
             V1X[k, 8:16, :] = v1
-            held_u = jnp.where(slot == i, packed(u1, i), held_u)
-            held_v = jnp.where(slot == i, packed(v1, i), held_v)
+        return cum, cum_n, sum_u0, sum_v0, sum_u, sum_v
+
+    sums = lax.fori_loop(0, NM, momentum, (zero,) * 6)[2:]
+
+    for n in range(4):
+        F2[n, 1, 8:16, :] = sums[n]
+    spread(G_SUM, F2, AROUND)
+
+    @pl.loop(0, NC)
+    def _(c):
+        held_u = held_v = zero
+        for i in range(LC):
+            k = c * LC + i
+            held_u = jnp.where(slot == i, packed(U1B[k], i), held_u)
+            held_v = jnp.where(slot == i, packed(V1X[k, 8:16, :], i), held_v)
         pack1[0, c] = held_u
         pack1[1, c] = held_v
-        return cum_e, cum_n, sum_u0, sum_v0, sum_u, sum_v
-
-    sums = lax.fori_loop(0, NC, momentum, (zero,) * 6)[2:]
-
-    for n in range(4):
-        F2[n, 1, 8:16, :] = sums[n]
-    for dx, dy in AROUND:
-        send(
-            G_SUM,
-            F2.at[:, 1, pl.ds(8, 8), :],
-            F2.at[:, 1 - dx, pl.ds(8 * (1 - dy), 8), :],
-            dx,
-            dy,
-        )
+
     for dx in (1, -1):
         side = P1W if dx > 0 else P1E
-        send(G_SIDE1, pack1, side.at[:, :, pl.ds(1, 8), :], dx, 0)
-        send(G_CORNER1, pack1.at[1, :, pl.ds(7, 1), :], side.at[1, :, pl.ds(0, 1), :], dx, 1)
-    send(G_V1, V1X.at[:, pl.ds(15, 1), :], V1X.at[:, pl.ds(7, 1), :], 0, 1)
+        send(G_B, pack1, side.at[:, :, pl.ds(1, 8), :], dx, 0)
+        send(G_B, pack1.at[1, :, pl.ds(7, 1), :], side.at[1, :, pl.ds(0, 1), :], dx, 1)
+    send(G_B, V1X.at[:, pl.ds(15, 1), :], V1X.at[:, pl.ds(7, 1), :], 0, 1)
 
     left(G_2D, size_2d)
-    left(G_W, size_w)
-    left(G_SIDE, size_side)
-    left(G_CORNER, size_corner)
-    left(G_POLE, size_pole)
     left(G_TS, size_ts)
     received(G_TS, size_ts)
 
     for f in range(2):
-        HC[f] = if_wet(SC, 0, 1, beyond(PW, PE, 3 + f, 1))
+        HC[f] = by8.if_wet(SC, 0, 1, by8.beyond(TW, TE, f, 1))
 
     @pl.loop(0, NC)
     def _(c):
@@ -534,26 +560,24 @@
     DP[2] = in_slots(DV[1, 7:15, :], (126, 127, 0, 1))
     DP[3] = jnp.broadcast_to(du[:, LANES - 1 :], du.shape)
 
-    received(G_SIDE1, size_side1)
-    received(G_CORNER1, size_corner1)
-    received(G_V1, size_v1)
+    received(G_B, size_b)
     half = 0.5 * DTT
 
-    edge_u = if_wet(SU, 0, 1, beyond(P1W, P1E, 0, 1) + DP[0][None]) * half
-    edge_v = if_wet(SV, 0, 1, beyond(P1W, P1E, 1, 1) + DP[1][None]) * half
-    edge_vs = if_wet(SV, 0, 0, beyond(P1W, P1E, 1, 0) + DP[2][None]) * half
-    last_u = if_wet(SU, 1, 1, pack1[0] + DP[3][None]) * half
+    edge_u = by8.if_wet(SU, 0, 1, by8.beyond(P1W, P1E, 0, 1) + DP[0][None]) * half
+    edge_v = by8.if_wet(SV, 0, 1, by8.beyond(P1W, P1E, 1, 1) + DP[1][None]) * half
+    edge_vs = by8.if_wet(SV, 0, 0, by8.beyond(P1W, P1E, 1, 0) + DP[2][None]) * half
+    last_u = by8.if_wet(SU, 1, 1, pack1[0] + DP[3][None]) * half
     for f in range(2):
-        south = if_wet(SC, 0, 0, beyond(PW, PE, 3 + f, 0))
+        south = by8.if_wet(SC, 0, 0, by8.beyond(TW, TE, f, 0))
         here = HC[f]
-        north = if_wet(SC, 0, 2, beyond(PW, PE, 3 + f, 2))
-        inner = if_wet(SC, 1, 1, pack[3 + f, :, 1:9, :])
-        flux = edge_u * (here + roll(jnp.where(at4s, inner, here), -1))
+        north = by8.if_wet(SC, 0, 2, by8.beyond(TW, TE, f, 2))
+        inner = by8.if_wet(SC, 1, 1, pack_ts[f, :, 1:9, :])
+        flux = edge_u * (here + roll(jnp.where(by8.east, inner, here), -1))
         flux_last = last_u * (inner + roll(here, -1))
-        flux_west = roll(jnp.where(at3s, flux_last, flux), 1)
+        flux_west = roll(jnp.where(by8.west, flux_last, flux), 1)
         a = here - ((flux - flux_west) + (edge_v * (here + north) - edge_vs * (south + here)))
         FW[f] = flux
-        AO[f] = if_wet(SC, 0, 1, a)
+        AO[f] = by8.if_wet(SC, 0, 1, a)
 
     def send_rows(c, up):
         src, dst, dy, group = (14, 6, 1, G_UP) if up else (8, 16, -1, G_DOWN)
@@ -606,30 +630,26 @@
 
     @pl.when(has_north)
     def _():
-        send(G_UP1, AD.at[:, :, pl.ds(8, 1), :], AD.at[:, :, pl.ds(0, 1), :], 0, 1)
+        send(G_UP, AD.at[:, :, pl.ds(8, 1), :], AD.at[:, :, pl.ds(0, 1), :], 0, 1)
 
     @pl.when(has_south)
     def _():
-        send(G_DOWN1, AD.at[:, :, pl.ds(1, 1), :], AD.at[:, :, pl.ds(9, 1), :], 0, -1)
+        send(G_DOWN, AD.at[:, :, pl.ds(1, 1), :], AD.at[:, :, pl.ds(9, 1), :], 0, -1)
 
     left(G_SUM, size_sum)
-    left(G_SIDE1, size_side1)
-    left(G_CORNER1, size_corner1)
-    left(G_V1, size_v1)
+    left(G_B, size_b)
 
     @pl.when(has_south)
     def _():
-        received(G_UP, size_a)
-        received(G_UP1, size_ad)
+        received(G_UP, size_c)
 
     @pl.when(has_north)
     def _():
-        received(G_DOWN, size_a)
-        received(G_DOWN1, size_ad)
+        received(G_DOWN, size_c)
 
     for f in range(2):
         south, here, north = [AD[f, :, r : r + 8, :] for r in range(3)]
-        EM[f] = KAPPA * edge_far(here, south + north)
+        EM[f] = KAPPA * by8.far(here, south + north)
 
     @pl.loop(0, NC)
     def _(c):
@@ -650,13 +670,11 @@
 
     @pl.when(has_north)
     def _():
-        left(G_UP, size_a)
-        left(G_UP1, size_ad)
+        left(G_UP, size_c)
 
     @pl.when(has_south)
     def _():
-        left(G_DOWN, size_a)
-        left(G_DOWN1, size_ad)
+        left(G_DOWN, size_c)
 
 
 def write_out(*refs):
@@ -693,9 +711,14 @@
             vmem(2, 24, LANES),
             vmem(2, 24, LANES),
             vmem(2, 24, LANES),
-            vmem(5, NC, 16, LANES),
-            vmem(5, NC, 16, LANES),
-            vmem(5, NC, 16, LANES),
+            vmem(2, 24, LANES),
+            vmem(2, 24, LANES),
+            vmem(3, NM, 16, LANES),
+            vmem(3, NM, 16, LANES),
+            vmem(3, NM, 16, LANES),
+            vmem(2, NC, 16, LANES),
+            vmem(2, NC, 16, LANES),
+            vmem(2, NC, 16, LANES),
             vmem(4, 3, 24, LANES),
             vmem(2, 24, LANES),
             vmem(4, ROWS, LANES),
@@ -706,14 +729,14 @@
             vmem(2, NC, 16, LANES),
             vmem(2, K, 24, LANES),
             vmem(2, NC, 16, LANES),
-            vmem(NC, ROWS, LANES),
-            vmem(NC, ROWS, LANES),
+            vmem(NM, ROWS, LANES),
+            vmem(NM, ROWS, LANES),
             vmem(2, NC, ROWS, LANES),
             vmem(2, K, ROWS, LANES),
             vmem(2, NC, ROWS, LANES),
             vmem(2, NC, ROWS, LANES),
             vmem(2, NC, ROWS, LANES),
-            pltpu.SemaphoreType.DMA((7,)),
+            pltpu.SemaphoreType.DMA((2,)),
             pltpu.SemaphoreType.DMA((GROUPS,)),
             pltpu.SemaphoreType.DMA((GROUPS,)),
         ],

time: 34.1 us -> 32 us (0.938)
  Pallas kernels: 33.3 us -> 31.2 us
    pallas_call x1, Pallas kernels: 32.3 us -> 30.2 us  [per_device(): pl.pallas_call(functools.partial(kernel, nx, ny), out_shape=tuple((pltpu....]
where the time goes in v4:
time: 32 us; the launch traced here: 31.9 us
  Pallas kernels  31.2 us (98%)
  between operations  0.64 us (2%)
    pallas_call x1, Pallas kernels, per_device(): pl.pallas_call(functools.partial(kernel, nx, ny), out_shape=tuple((pltpu....  30.2 us
    pallas_call x1, Pallas kernels, per_device(): pl.pallas_call(write_out, out_shape=outs, in_specs=[pl.BlockSpec(memory_s...  1.07 us

profile of v4, /device:TPU:1, one launch (start us, length us, event | category | flops | bytes accessed | tf_op | source)
XLA Modules:
  0.0 31.9 jit_solution(15493354781630934025)
XLA Ops:
  0.6 30.2 %shard_map.110 = (f32[75,8,128]{2,1,0:T(8,128)S(1)}, f32[75,8,128]{2,1,0:T(8,128)S(1)}, f32[75,8,128]{2,1,0:T(8,128)S(1)}, f32[75,8,128]{2,1,0:T(8,128)S(1)}, f32[8,128]{1,0:T(8,128)S(1)}) custom-call(f32[75,8,128]{2,1,0:T(8,128)} %t_in.1, f32[75,8,128]{2,1,0:T(8,128)} %s_in.1, f32[75,8,128]{2,1,0:T(8,128)} %u_in.1, f32[75,8,128]{2,1,0:T(8,128)} %v_in.1, ...), custom_call_target="tpu_custom_call" | custom-call | tf_op jit(solution)/shard_map/pallas_call | solution.py:697
  30.8 1.1 %shard_map.111 = (f32[75,8,128]{2,1,0:T(8,128)}, f32[75,8,128]{2,1,0:T(8,128)}, f32[75,8,128]{2,1,0:T(8,128)}, f32[75,8,128]{2,1,0:T(8,128)}, f32[8,128]{1,0:T(8,128)}) custom-call(f32[75,8,128]{2,1,0:T(8,128)S(1)} %get-tuple-element.10.refs_0_, f32[75,8,128]{2,1,0:T(8,128)S(1)} %get-tuple-element.11.refs_1_, f32[75,8,128]{2,1,0:T(8,128)S(1)} %get-tuple-element.12.refs_2_, ...), custom_call_target="tpu_custom_call" | custom-call | tf_op jit(solution)/shard_map/pallas_call | solution.py:747

commit v5 on v4

--- a/solution.py
+++ b/solution.py
@@ -45,7 +45,7 @@
     VN,
     HN,
     X,
-    WX,
+    PX,
     D2,
     flag_v,
     bottom_v,
@@ -77,6 +77,7 @@
     EV,
     HC,
     CE,
+    CN,
     FW,
     AO,
     EM,
@@ -122,6 +123,7 @@
     slot = lax.div(lane, 8).astype(jnp.float32)
     row = lax.broadcasted_iota(jnp.int32, (ROWS, LANES), 0)
     first, last = lane == 0, lane == LANES - 1
+    half = 0.5 * DTT
     edge4 = jnp.logical_or(lane < 2, lane >= LANES - 2)
     slot4 = lax.div(lane, 4).astype(jnp.float32)
     has_south, has_north = gy > 0, gy < ny - 1
@@ -184,8 +186,7 @@
     def thickness(base, i):
         return 0.5 / K + (base + (i + 0.5)) * (1.0 / (K * K))
 
-    @pl.loop(0, NM)
-    def _(c):
+    def press(c, cum):
         base = (c * LM).astype(jnp.float32)
         depth = D2[0, 1, 8:16, :] - base
         held = [zero] * 3
@@ -193,11 +194,16 @@
             k = c * LM + i
             u, v, t, s = [X[f, k, 8:16, :] for f in range(4)]
             w = jnp.where(depth > i, weight(t, s, DT * thickness(base, i)), 0.0)
-            WX[k, 0:8, :] = w
-            for n, x in enumerate((u, v, w)):
+            cum = cum + w
+            load = cum - 0.5 * w
+            PX[k, 0:8, :] = load
+            for n, x in enumerate((u, v, load)):
                 held[n] = jnp.where(slot4 == i, packed(x, i, 4), held[n])
         for n in range(3):
             pack[n, c, 1:9, :] = held[n]
+        return cum
+
+    lax.fori_loop(0, NM, press, zero)
 
     pl.semaphore_wait(barrier, len(AROUND))
 
@@ -237,7 +243,7 @@
     for dy in (1, -1):
         src, dst = (8, 0) if dy > 0 else (1, 9)
         send(G_A, pack.at[uv, :, pl.ds(src, 1), :], pack.at[uv, :, pl.ds(dst, 1), :], 0, dy)
-    send(G_A, WX.at[:, pl.ds(0, 1), :], WX.at[:, pl.ds(8, 1), :], 0, -1)
+    send(G_A, PX.at[:, pl.ds(0, 1), :], PX.at[:, pl.ds(8, 1), :], 0, -1)
 
     @pl.loop(0, NC)
     def _(c):
@@ -302,17 +308,9 @@
     CC[...] = col[0]
     CU[...] = cu[0]
     CV[...] = cv[0]
-    edge_col = [
-        jnp.where(inside, x, 0.0)
-        for x in (jnp.where(slot24 < 4, D2[2, 0], D2[2, 2]), D2[2, 1])
-    ]
-    edge_cu = [jnp.minimum(a, b) for a, b in zip(edge_col, ring_east(*edge_col, slot24 == 4))]
     for n in range(2):
         SU4[n] = in_slots(cu[1 - n], (126, 127, 0, 1), 4)
         SV4[n] = in_slots(cv[1 - n], (126, 127, 0, 1), 4)
-        SC[n] = edge_col[n]
-        SU[n] = edge_cu[n]
-        SV[n] = jnp.minimum(edge_col[n], north24(edge_col[n]))
 
     at_wall = jnp.where(
         jnp.logical_or(
@@ -342,10 +340,6 @@
                 X[f, k, 6:14, :] = a
                 X[f, k, 10:18, :] = b
 
-    def far(a, y, yy):
-        z = 2.0 * y - 8.0 * a
-        return yy + roll(z + roll(a, -1), -1) + roll(z + roll(a, 1), 1)
-
     class Slots:
         def __init__(self, count, width):
             shape = (count, ROWS, LANES)
@@ -377,17 +371,8 @@
 
     du_s, du, du_n = [excess(0, SU4, r) for r in range(3)]
     dv_s, dv, dv_n = [excess(1, SV4, r) for r in range(3)]
-    dw = by4.beyond(PW, PE, 2, 1) - pack[2, :, 1:9, :]
-    dw = jnp.where(by4.west, roll(dw, -1), 0.0)
-    run = dw
-    for shift in (4, 8, 16, 32, 64):
-        run = run + jnp.where(by4.lanes >= shift, roll(run, shift), 0.0)
-    whole = jnp.broadcast_to(run[:, :, 4 * LM - 3 : 4 * LM - 2], run.shape)
-    above = [zero]
-    for c in range(NM - 1):
-        above.append(above[-1] + whole[c])
-    run = run + jnp.stack(above)
-    EU[...] = jnp.where(by4.west, f4[None] * roll(dv + dv_s, -1) - run + 0.5 * dw, 0.0) - (
+    dp = by4.beyond(PW, PE, 2, 1) - pack[2, :, 1:9, :]
+    EU[...] = jnp.where(by4.west, roll(f4[None] * (dv + dv_s) - dp, -1), 0.0) - (
         DT * NU
     ) * by4.far(du, du_n + du_s)
     EV[...] = jnp.where(by4.east, -f4[None] * roll(du + du_n, 1), 0.0) - (DT * NU) * by4.far(
@@ -395,7 +380,7 @@
     )
 
     def momentum(c, carry):
-        cum, cum_n, sum_u0, sum_v0, sum_u, sum_v = carry
+        sum_u0, sum_v0, sum_u, sum_v = carry
         base = (c * LM).astype(jnp.float32)
         edge_u, edge_v = EU[c], EV[c]
         cu0, cv0 = CU[8:16, :] - base, CV[8:16, :] - base
@@ -404,11 +389,7 @@
             dz = thickness(base, i)
             uss, us, u, un, unn = [X[0, k, r : r + 8, :] for r in range(6, 11)]
             vss, vs, v, vn, vnn = [X[1, k, r : r + 8, :] for r in range(6, 11)]
-            w, wn = WX[k, 0:8, :], WX[k, 1:9, :]
-            cum = cum + w
-            load = cum - 0.5 * w
-            step_n = wn - w
-            cum_n = cum_n + step_n
+            load, load_n = PX[k, 0:8, :], PX[k, 1:9, :]
             cross_u = f4 * (v + vs)
             cross_v = f4 * (u + un)
             yu, yv = (DT * NU) * (un + us), (DT * NU) * (vn + vs)
@@ -419,8 +400,8 @@
                 + 8.0 * yu
                 - (DT * NU) * (unn + uss)
                 + (cross_u + load)
-                + roll((zu - roll(au, -1)) + (cross_u - load), -1)
-                + roll(zu - roll(au, 1), 1)
+                + (roll(zu + (cross_u - load), -1) + roll(zu, 1))
+                - (roll(au, -2) + roll(au, 2))
                 + jnp.where(edge4, unpacked(edge_u, i, 4), 0.0)
             )
             v1 = (
@@ -428,9 +409,9 @@
                 + 8.0 * yv
                 - (DT * NU) * (vnn + vss)
                 - cross_v
-                - (cum_n - 0.5 * step_n)
-                + roll(zv - roll(av, -1), -1)
-                + roll((zv - roll(av, 1)) - cross_v, 1)
+                - (load_n - load)
+                + (roll(zv, -1) + roll(zv - cross_v, 1))
+                - (roll(av, -2) + roll(av, 2))
                 + jnp.where(edge4, unpacked(edge_v, i, 4), 0.0)
             )
             u1 = jnp.where(cu0 > i, u1, 0.0)
@@ -441,9 +422,9 @@
             sum_v = sum_v + v1 * dz
             U1B[k] = u1
             V1X[k, 8:16, :] = v1
-        return cum, cum_n, sum_u0, sum_v0, sum_u, sum_v
-
-    sums = lax.fori_loop(0, NM, momentum, (zero,) * 6)[2:]
+        return sum_u0, sum_v0, sum_u, sum_v
+
+    sums = lax.fori_loop(0, NM, momentum, (zero,) * 4)
 
     for n in range(4):
         F2[n, 1, 8:16, :] = sums[n]
@@ -468,6 +449,16 @@
     left(G_2D, size_2d)
     left(G_TS, size_ts)
     received(G_TS, size_ts)
+
+    edge_col = [
+        jnp.where(inside, x, 0.0)
+        for x in (jnp.where(slot24 < 4, D2[2, 0], D2[2, 2]), D2[2, 1])
+    ]
+    edge_cu = [jnp.minimum(a, b) for a, b in zip(edge_col, ring_east(*edge_col, slot24 == 4))]
+    for n in range(2):
+        SC[n] = edge_col[n]
+        SU[n] = edge_cu[n]
+        SV[n] = jnp.minimum(edge_col[n], north24(edge_col[n]))
 
     for f in range(2):
         HC[f] = by8.if_wet(SC, 0, 1, by8.beyond(TW, TE, f, 1))
@@ -485,7 +476,10 @@
                 north = jnp.where(high > i, X[2 + f, k, 9:17, :], 0.0)
                 X[2 + f, k, 7:15, :] = south
                 X[2 + f, k, 9:17, :] = north
-                CE[f, k] = here + roll(jnp.where(first, unpacked(edge, i), here), -1)
+                east = jnp.where(last, roll(edge, LANES - 5 - 8 * i), roll(here, -1))
+                CE[f, k] = half * (here + east)
+                CN[f, k, 7:15, :] = half * (south + here)
+                CN[f, k, 8:16, :] = half * (here + north)
 
     def both(op, *pairs):
         return [op(*xs) for xs in zip(*pairs)]
@@ -561,8 +555,6 @@
     DP[3] = jnp.broadcast_to(du[:, LANES - 1 :], du.shape)
 
     received(G_B, size_b)
-    half = 0.5 * DTT
-
     edge_u = by8.if_wet(SU, 0, 1, by8.beyond(P1W, P1E, 0, 1) + DP[0][None]) * half
     edge_v = by8.if_wet(SV, 0, 1, by8.beyond(P1W, P1E, 1, 1) + DP[1][None]) * half
     edge_vs = by8.if_wet(SV, 0, 0, by8.beyond(P1W, P1E, 1, 0) + DP[2][None]) * half
@@ -601,18 +593,14 @@
             k = c * LC + i
             u = jnp.where(cu0 > i, U1B[k] + du, 0.0)
             v = jnp.where(cv0 > i, V1X[k, 8:16, :] + dv, 0.0)
-            vs = jnp.where(cvs > i, V1X[k, 7:15, :] + dvs, 0.0) * half
+            vs = jnp.where(cvs > i, V1X[k, 7:15, :] + dvs, 0.0)
             UN[k] = u
             VN[k] = v
-            u = u * half
-            v = v * half
             for f in range(2):
-                south, here, north = [X[2 + f, k, r : r + 8, :] for r in (7, 8, 9)]
-                edge = unpacked(edges[f], i)
                 flux = u * CE[f, k]
-                a = here - (
-                    (flux - roll(jnp.where(last, edge, flux), 1))
-                    + (v * (here + north) - vs * (south + here))
+                flux_west = jnp.where(first, roll(edges[f], LANES - 3 - 8 * i), roll(flux, 1))
+                a = X[2 + f, k, 8:16, :] - (
+                    (flux - flux_west) + (v * CN[f, k, 8:16, :] - vs * CN[f, k, 7:15, :])
                 )
                 a = jnp.where(cc0 > i, a, 0.0)
                 AX[f, k, 8:16, :] = a
@@ -638,6 +626,19 @@
 
     left(G_SUM, size_sum)
     left(G_B, size_b)
+
+    @pl.loop(0, NC)
+    def _(c):
+        for i in range(LC):
+            k = c * LC + i
+            for f, out in ((0, TN), (1, SN)):
+                a = AX[f, k, 8:16, :]
+                b = KAPPA * a
+                out[k] = (
+                    centre_ts * a
+                    + 8.0 * (roll(b, -1) + roll(b, 1))
+                    - (roll(b, -2) + roll(b, 2))
+                )
 
     @pl.when(has_south)
     def _():
@@ -659,11 +660,13 @@
         for i in range(LC):
             k = c * LC + i
             for f, out in ((0, TN), (1, SN)):
-                ss, s, a, n, nn = [AX[f, k, r : r + 8, :] for r in range(6, 11)]
-                y = n + s
+                ss, s, n, nn = [AX[f, k, r : r + 8, :] for r in (6, 7, 9, 10)]
+                y = KAPPA * (n + s)
                 mixed = (
-                    centre_ts * a
-                    - KAPPA * (far(a, y, nn + ss) - 8.0 * y)
+                    out[k]
+                    + 8.0 * y
+                    - 2.0 * (roll(y, -1) + roll(y, 1))
+                    - KAPPA * (nn + ss)
                     - jnp.where(edge4, unpacked(edges[f], i), 0.0)
                 )
                 out[k] = jnp.where(cc0 > i, mixed, 0.0)
@@ -733,6 +736,7 @@
             vmem(NM, ROWS, LANES),
             vmem(2, NC, ROWS, LANES),
             vmem(2, K, ROWS, LANES),
+            vmem(2, K, 16, LANES),
             vmem(2, NC, ROWS, LANES),
             vmem(2, NC, ROWS, LANES),
             vmem(2, NC, ROWS, LANES),

time: 32 us -> 29.7 us (0.928)
  Pallas kernels: 31.2 us -> 29 us
    pallas_call x1, Pallas kernels: 30.2 us -> 27.9 us  [per_device(): pl.pallas_call(functools.partial(kernel, nx, ny), out_shape=tuple((pltpu....]
where the time goes in v5:
time: 29.7 us; the launch traced here: 29.6 us
  Pallas kernels  29 us (98%)
  between operations  0.64 us (2%)
    pallas_call x1, Pallas kernels, per_device(): pl.pallas_call(functools.partial(kernel, nx, ny), out_shape=tuple((pltpu....  27.9 us
    pallas_call x1, Pallas kernels, per_device(): pl.pallas_call(write_out, out_shape=outs, in_specs=[pl.BlockSpec(memory_s...  1.07 us

profile of v5, /device:TPU:1, one launch (start us, length us, event | category | flops | bytes accessed | tf_op | source)
XLA Modules:
  0.0 29.6 jit_solution(11064693221321133685)
XLA Ops:
  0.6 27.9 %shard_map.110 = (f32[75,8,128]{2,1,0:T(8,128)S(1)}, f32[75,8,128]{2,1,0:T(8,128)S(1)}, f32[75,8,128]{2,1,0:T(8,128)S(1)}, f32[75,8,128]{2,1,0:T(8,128)S(1)}, f32[8,128]{1,0:T(8,128)S(1)}) custom-call(f32[75,8,128]{2,1,0:T(8,128)} %t_in.1, f32[75,8,128]{2,1,0:T(8,128)} %s_in.1, f32[75,8,128]{2,1,0:T(8,128)} %u_in.1, f32[75,8,128]{2,1,0:T(8,128)} %v_in.1, ...), custom_call_target="tpu_custom_call" | custom-call | tf_op jit(solution)/shard_map/pallas_call | solution.py:700
  28.5 1.1 %shard_map.111 = (f32[75,8,128]{2,1,0:T(8,128)}, f32[75,8,128]{2,1,0:T(8,128)}, f32[75,8,128]{2,1,0:T(8,128)}, f32[75,8,128]{2,1,0:T(8,128)}, f32[8,128]{1,0:T(8,128)}) custom-call(f32[75,8,128]{2,1,0:T(8,128)S(1)} %get-tuple-element.10.refs_0_, f32[75,8,128]{2,1,0:T(8,128)S(1)} %get-tuple-element.11.refs_1_, f32[75,8,128]{2,1,0:T(8,128)S(1)} %get-tuple-element.12.refs_2_, ...), custom_call_target="tpu_custom_call" | custom-call | tf_op jit(solution)/shard_map/pallas_call | solution.py:751

commit v6 on v5

--- a/solution.py
+++ b/solution.py
@@ -44,12 +44,14 @@
     UN,
     VN,
     HN,
+    AX,
+    EM,
+    CC,
     X,
     PX,
     D2,
     flag_v,
     bottom_v,
-    CC,
     CU,
     CV,
     SC,
@@ -71,7 +73,6 @@
     pack1,
     P1E,
     P1W,
-    AX,
     AD,
     EU,
     EV,
@@ -80,7 +81,7 @@
     CN,
     FW,
     AO,
-    EM,
+    HS,
     load_sem,
     send_sem,
     recv_sem,
@@ -461,7 +462,15 @@
         SV[n] = jnp.minimum(edge_col[n], north24(edge_col[n]))
 
     for f in range(2):
-        HC[f] = by8.if_wet(SC, 0, 1, by8.beyond(TW, TE, f, 1))
+        south, here, north = [
+            by8.if_wet(SC, 0, r, by8.beyond(TW, TE, f, r)) for r in range(3)
+        ]
+        inner = by8.if_wet(SC, 1, 1, pack_ts[f, :, 1:9, :])
+        HC[f] = here
+        HS[f, 0] = half * (here + roll(jnp.where(by8.east, inner, here), -1))
+        HS[f, 1] = half * (inner + roll(here, -1))
+        HS[f, 2] = half * (here + north)
+        HS[f, 3] = half * (south + here)
 
     @pl.loop(0, NC)
     def _(c):
@@ -497,6 +506,8 @@
     ease = both(lambda o: jnp.where(o, DB, 0.0), ocean)
     height = [jnp.where(o, x, 0.0) for o, x in zip(ocean, sides(D2, 1))]
 
+    inverse_u = both(lambda d, o: 1.0 / (d + (1.0 - o)), depth_u, open_u)
+    inverse_v = both(lambda d, o: 1.0 / (d + (1.0 - o)), depth_v, open_v)
     received(G_SUM, size_sum)
     u0, v0, u_all, v_all = [list(sides(F2, f)) for f in range(4)]
     push_u = both(lambda o, a, b: o * ((a - b) * (DB / DT)), open_u, u_all, u0)
@@ -541,11 +552,11 @@
 
     HN[...] = height[0][8:16]
 
-    def shift(r, a, d, o):
-        return (r * (1.0 / SUBSTEPS) - a) / (d + (1.0 - o))
-
-    shift_u = both(shift, run_u, u_all, depth_u, open_u)
-    shift_v = both(shift, run_v, v_all, depth_v, open_v)
+    def shift(r, a, inverse):
+        return (r * (1.0 / SUBSTEPS) - a) * inverse
+
+    shift_u = both(shift, run_u, u_all, inverse_u)
+    shift_v = both(shift, run_v, v_all, inverse_v)
     DV[0] = shift_v[0]
     DV[1] = shift_v[1]
     du, dv, dvs = shift_u[0][8:16], shift_v[0][8:16], DV[0, 7:15, :]
@@ -555,19 +566,14 @@
     DP[3] = jnp.broadcast_to(du[:, LANES - 1 :], du.shape)
 
     received(G_B, size_b)
-    edge_u = by8.if_wet(SU, 0, 1, by8.beyond(P1W, P1E, 0, 1) + DP[0][None]) * half
-    edge_v = by8.if_wet(SV, 0, 1, by8.beyond(P1W, P1E, 1, 1) + DP[1][None]) * half
-    edge_vs = by8.if_wet(SV, 0, 0, by8.beyond(P1W, P1E, 1, 0) + DP[2][None]) * half
-    last_u = by8.if_wet(SU, 1, 1, pack1[0] + DP[3][None]) * half
+    edge_u = by8.if_wet(SU, 0, 1, by8.beyond(P1W, P1E, 0, 1) + DP[0][None])
+    edge_v = by8.if_wet(SV, 0, 1, by8.beyond(P1W, P1E, 1, 1) + DP[1][None])
+    edge_vs = by8.if_wet(SV, 0, 0, by8.beyond(P1W, P1E, 1, 0) + DP[2][None])
+    last_u = by8.if_wet(SU, 1, 1, pack1[0] + DP[3][None])
     for f in range(2):
-        south = by8.if_wet(SC, 0, 0, by8.beyond(TW, TE, f, 0))
-        here = HC[f]
-        north = by8.if_wet(SC, 0, 2, by8.beyond(TW, TE, f, 2))
-        inner = by8.if_wet(SC, 1, 1, pack_ts[f, :, 1:9, :])
-        flux = edge_u * (here + roll(jnp.where(by8.east, inner, here), -1))
-        flux_last = last_u * (inner + roll(here, -1))
-        flux_west = roll(jnp.where(by8.west, flux_last, flux), 1)
-        a = here - ((flux - flux_west) + (edge_v * (here + north) - edge_vs * (south + here)))
+        flux = edge_u * HS[f, 0]
+        flux_west = roll(jnp.where(by8.west, last_u * HS[f, 1], flux), 1)
+        a = HC[f] - ((flux - flux_west) + (edge_v * HS[f, 2] - edge_vs * HS[f, 3]))
         FW[f] = flux
         AO[f] = by8.if_wet(SC, 0, 1, a)
 
@@ -652,40 +658,53 @@
         south, here, north = [AD[f, :, r : r + 8, :] for r in range(3)]
         EM[f] = KAPPA * by8.far(here, south + north)
 
+    @pl.when(has_north)
+    def _():
+        left(G_UP, size_c)
+
+    @pl.when(has_south)
+    def _():
+        left(G_DOWN, size_c)
+
+
+def finish(TN, SN, UN, VN, HN, AX, EM, CC, t_out, s_out, u_out, v_out, h_out, TO, SO, sem):
+    copies = [
+        pltpu.make_async_copy(src, dst, sem.at[n])
+        for n, (src, dst) in enumerate(((UN, u_out), (VN, v_out), (HN, h_out)))
+    ]
+    for copy in copies:
+        copy.start()
+    lane = lax.broadcasted_iota(jnp.int32, (ROWS, LANES), 1)
+    edge4 = jnp.logical_or(lane < 2, lane >= LANES - 2)
+
+    def roll(x, shift):
+        return pltpu.roll(x, shift % LANES, 1)
+
     @pl.loop(0, NC)
     def _(c):
-        base = (c * LC).astype(jnp.float32)
-        cc0 = CC[8:16, :] - base
+        cc0 = CC[8:16, :] - (c * LC).astype(jnp.float32)
         edges = [EM[f, c] for f in range(2)]
         for i in range(LC):
             k = c * LC + i
-            for f, out in ((0, TN), (1, SN)):
+            for f, part, out in ((0, TN, TO), (1, SN, SO)):
                 ss, s, n, nn = [AX[f, k, r : r + 8, :] for r in (6, 7, 9, 10)]
                 y = KAPPA * (n + s)
                 mixed = (
-                    out[k]
+                    part[k]
                     + 8.0 * y
                     - 2.0 * (roll(y, -1) + roll(y, 1))
                     - KAPPA * (nn + ss)
-                    - jnp.where(edge4, unpacked(edges[f], i), 0.0)
+                    - jnp.where(edge4, roll(edges[f], LANES - 4 - 8 * i), 0.0)
                 )
                 out[k] = jnp.where(cc0 > i, mixed, 0.0)
-
-    @pl.when(has_north)
-    def _():
-        left(G_UP, size_c)
-
-    @pl.when(has_south)
-    def _():
-        left(G_DOWN, size_c)
-
-
-def write_out(*refs):
-    copies = [pltpu.make_async_copy(refs[i], refs[5 + i], refs[10].at[i]) for i in range(5)]
-    for copy in copies:
-        copy.start()
+        levels = pl.ds(c * LC, LC)
+        pltpu.make_async_copy(TO.at[levels], t_out.at[levels], sem.at[3]).start()
+        pltpu.make_async_copy(SO.at[levels], s_out.at[levels], sem.at[4]).start()
+
     for copy in copies:
         copy.wait()
+    pltpu.make_async_copy(TO, t_out, sem.at[3]).wait()
+    pltpu.make_async_copy(SO, s_out, sem.at[4]).wait()
 
 
 def per_device(nx, ny, *args):
@@ -699,16 +718,19 @@
     args = [pltpu.with_memory_space_constraint(x, pltpu.HBM) for x in args]
     held = pl.pallas_call(
         functools.partial(kernel, nx, ny),
-        out_shape=tuple(pltpu.VMEM(x.shape, x.dtype) for x in outs),
+        out_shape=tuple(
+            pltpu.VMEM(shape, jnp.float32)
+            for shape in [x.shape for x in outs]
+            + [(2, K, 24, LANES), (2, NC, ROWS, LANES), (24, LANES)]
+        ),
         in_specs=[pl.BlockSpec(memory_space=pltpu.HBM)] * 7,
-        out_specs=[pl.BlockSpec(memory_space=pltpu.VMEM)] * 5,
+        out_specs=[pl.BlockSpec(memory_space=pltpu.VMEM)] * 8,
         scratch_shapes=[
             vmem(4, K, 24, LANES),
             vmem(K, 16, LANES),
             vmem(3, 3, 24, LANES),
             vmem(ROWS, LANES, dtype=jnp.int32),
             vmem(ROWS, LANES, dtype=jnp.int32),
-            vmem(24, LANES),
             vmem(24, LANES),
             vmem(24, LANES),
             vmem(2, 24, LANES),
@@ -730,7 +752,6 @@
             vmem(2, NC, ROWS, LANES),
             vmem(2, NC, 16, LANES),
             vmem(2, NC, 16, LANES),
-            vmem(2, K, 24, LANES),
             vmem(2, NC, 16, LANES),
             vmem(NM, ROWS, LANES),
             vmem(NM, ROWS, LANES),
@@ -739,7 +760,7 @@
             vmem(2, K, 16, LANES),
             vmem(2, NC, ROWS, LANES),
             vmem(2, NC, ROWS, LANES),
-            vmem(2, NC, ROWS, LANES),
+            vmem(2, 4, NC, ROWS, LANES),
             pltpu.SemaphoreType.DMA((2,)),
             pltpu.SemaphoreType.DMA((GROUPS,)),
             pltpu.SemaphoreType.DMA((GROUPS,)),
@@ -749,11 +770,15 @@
         ),
     )(*args)
     return pl.pallas_call(
-        write_out,
+        finish,
         out_shape=outs,
-        in_specs=[pl.BlockSpec(memory_space=pltpu.VMEM)] * 5,
+        in_specs=[pl.BlockSpec(memory_space=pltpu.VMEM)] * 8,
         out_specs=[pl.BlockSpec(memory_space=pltpu.HBM)] * 5,
-        scratch_shapes=[pltpu.SemaphoreType.DMA((5,))],
+        scratch_shapes=[
+            vmem(K, ROWS, LANES),
+            vmem(K, ROWS, LANES),
+            pltpu.SemaphoreType.DMA((5,)),
+        ],
         compiler_params=pltpu.CompilerParams(vmem_limit_bytes=8 * 1024 * 1024),
     )(*held)
 

time: 29.7 us -> 29.3 us (0.987)
  Pallas kernels: 29 us -> 28.5 us
    pallas_call x1, Pallas kernels: 27.9 us -> 27 us  [per_device(): pl.pallas_call(functools.partial(kernel, nx, ny), out_shape=tuple((pltpu....]
    pallas_call x1, Pallas kernels: 1.07 us -> 1.53 us  [per_device(): pl.pallas_call(finish, out_shape=outs, in_specs=[pl.BlockSpec(memory_spac...]
where the time goes in v6:
time: 29.3 us; the launch traced here: 29.2 us
  Pallas kernels  28.5 us (97%)
  between operations  0.64 us (2%)
    pallas_call x1, Pallas kernels, per_device(): pl.pallas_call(functools.partial(kernel, nx, ny), out_shape=tuple((pltpu....  27 us
    pallas_call x1, Pallas kernels, per_device(): pl.pallas_call(finish, out_shape=outs, in_specs=[pl.BlockSpec(memory_spac...  1.53 us

profile of v6, /device:TPU:1, one launch (start us, length us, event | category | flops | bytes accessed | tf_op | source)
XLA Modules:
  0.0 29.2 jit_solution(17095350672548458797)
XLA Ops:
  0.6 27.0 %shard_map.110 = (f32[75,8,128]{2,1,0:T(8,128)S(1)}, f32[75,8,128]{2,1,0:T(8,128)S(1)}, f32[75,8,128]{2,1,0:T(8,128)S(1)}, f32[75,8,128]{2,1,0:T(8,128)S(1)}, f3...) custom-call(f32[75,8,128]{2,1,0:T(8,128)} %t_in.1, ...), custom_call_target="tpu_custom_call" | custom-call | tf_op jit(solution)/shard_map/pallas_call | solution.py:719
  27.6 1.5 %shard_map.111 = (f32[75,8,128]{2,1,0:T(8,128)}, f32[75,8,128]{2,1,0:T(8,128)}, f32[75,8,128]{2,1,0:T(8,128)}, f32[75,8,128]{2,1,0:T(8,128)}, f32[8,128]{1,0:T(8,128)}) custom-call(f32[75,8,128]{2,1,0:T(8,128)S(1)} %get-tuple-element.13.TN, f32[75,8,128]{2,1,0:T(8,128)S(1)} %get-tuple-element.14.SN, f32[75,8,128]{2,1,0:T(8,128)S(1)} %get-tuple-element.15.UN, ...), custom_call_target="tpu_custom_call" | custom-call | tf_op jit(solution)/shard_map/pallas_call | solution.py:772

commit v7 on v6

--- a/solution.py
+++ b/solution.py
@@ -24,7 +24,6 @@
 GRAVITY = 4.0
 DB = DT / SUBSTEPS
 
-AROUND = [(-1, -1), (1, -1), (-1, 1), (1, 1), (-1, 0), (1, 0), (0, -1), (0, 1)]
 GROUPS = 7
 G_2D, G_A, G_TS, G_SUM, G_B, G_UP, G_DOWN = range(GROUPS)
 
@@ -50,6 +49,7 @@
     X,
     PX,
     D2,
+    ET,
     flag_v,
     bottom_v,
     CU,
@@ -57,15 +57,18 @@
     SC,
     SU,
     SV,
-    SU4,
-    SV4,
+    S4,
     pack,
     PE,
     PW,
+    packp,
+    PP,
     pack_ts,
     TE,
     TW,
     F2,
+    FT,
+    FE,
     DV,
     DP,
     U1B,
@@ -74,8 +77,7 @@
     P1E,
     P1W,
     AD,
-    EU,
-    EV,
+    EUV,
     HC,
     CE,
     CN,
@@ -107,9 +109,25 @@
     def left(group, size):
         pltpu.make_async_copy(size, size, send_sem.at[group]).wait()
 
+    has_south, has_north = gy > 0, gy < ny - 1
+
+    def beside(dy):
+        return pl.when(has_north if dy > 0 else has_south)
+
     barrier = pltpu.get_barrier_semaphore()
-    for dx, dy in AROUND:
+
+    def greet(dx, dy):
         pl.semaphore_signal(barrier, inc=1, device_id=device(dx, dy), device_id_type=MESH)
+
+    for dy in (-1, 1):
+
+        @beside(dy)
+        def _():
+            for dx in (-1, 1, 0):
+                greet(dx, dy)
+
+    for dx in (-1, 1):
+        greet(dx, 0)
 
     pltpu.make_async_copy(flag_in, flag_v, load_sem.at[0]).start()
     pltpu.make_async_copy(bottom_in, bottom_v, load_sem.at[0]).start()
@@ -127,7 +145,6 @@
     half = 0.5 * DTT
     edge4 = jnp.logical_or(lane < 2, lane >= LANES - 2)
     slot4 = lax.div(lane, 4).astype(jnp.float32)
-    has_south, has_north = gy > 0, gy < ny - 1
     zero = jnp.zeros((ROWS, LANES), jnp.float32)
 
     def roll(x, shift):
@@ -168,7 +185,7 @@
     loaded(0, AX.at[0, pl.ds(0, 3), pl.ds(8, 8), :])
     own = (flag_v[...] * bottom_v[...]).astype(jnp.float32)
     D2[0, 1, 8:16, :] = own
-    D2[2, 1, 8:16, :] = in_slots(own, (124, 125, 126, 127, 0, 1, 2, 3))
+    ET[...] = jnp.where(jnp.logical_and(lane >= 32, lane < 96), roll(D2[1, 1, 8:16, :], 64), own)
 
     def rows(group, fields, count, dy):
         src, dst = (16 - count, 8 - count) if dy > 0 else (8, 16)
@@ -190,7 +207,7 @@
     def press(c, cum):
         base = (c * LM).astype(jnp.float32)
         depth = D2[0, 1, 8:16, :] - base
-        held = [zero] * 3
+        held = held_p = zero
         for i in range(LM):
             k = c * LM + i
             u, v, t, s = [X[f, k, 8:16, :] for f in range(4)]
@@ -198,53 +215,63 @@
             cum = cum + w
             load = cum - 0.5 * w
             PX[k, 0:8, :] = load
-            for n, x in enumerate((u, v, load)):
-                held[n] = jnp.where(slot4 == i, packed(x, i, 4), held[n])
-        for n in range(3):
-            pack[n, c, 1:9, :] = held[n]
+            held = jnp.where(slot4 == i, packed(u, i, 4), held)
+            held = jnp.where(slot4 == i + 16, packed(v, i + 16, 4), held)
+            held_p = jnp.where(slot4 == i, packed(load, i, 4), held_p)
+        pack[0, c, 1:9, :] = held
+        packp[c] = held_p
         return cum
 
     lax.fori_loop(0, NM, press, zero)
 
-    pl.semaphore_wait(barrier, len(AROUND))
-
-    def corners(group, src, west, east, fields):
+    pl.semaphore_wait(
+        barrier, 2 + 3 * (has_south.astype(jnp.int32) + has_north.astype(jnp.int32))
+    )
+
+    def corners(group, src, west, east, dy):
         for dx in (1, -1):
-            for dy in (1, -1):
-                side = west if dx > 0 else east
-                r_src, r_dst = (8, 0) if dy > 0 else (1, 9)
-                send(
-                    group,
-                    src.at[fields, :, pl.ds(r_src, 1), :],
-                    side.at[fields, :, pl.ds(r_dst, 1), :],
-                    dx,
-                    dy,
-                )
-
-    def spread(group, ref, around):
-        for dx, dy in around:
+            side = west if dx > 0 else east
+            r_src, r_dst = (8, 0) if dy > 0 else (1, 9)
             send(
                 group,
-                ref.at[:, 1, pl.ds(8, 8), :],
-                ref.at[:, 1 - dx, pl.ds(8 * (1 - dy), 8), :],
+                src.at[:, :, pl.ds(r_src, 1), :],
+                side.at[:, :, pl.ds(r_dst, 1), :],
                 dx,
                 dy,
             )
 
-    uv = pl.ds(0, 2)
-    spread(G_2D, D2, AROUND[:4])
-    corners(G_A, pack, PW, PE, uv)
-    spread(G_2D, D2, AROUND[4:6])
+    def edge_tiles(group, edge, aside, dy):
+        for dx in (-1, 1):
+            send(group, edge, aside(1 - dx).at[pl.ds(8 * (1 - dy), 8), :], dx, dy)
+
+    def whole_tiles(group, whole, dy):
+        send(group, whole.at[:, pl.ds(8, 8), :], whole.at[:, pl.ds(8 * (1 - dy), 8), :], 0, dy)
+
+    def edges_2d(dy):
+        edge_tiles(G_2D, ET, lambda n: D2.at[0, n], dy)
+
+    for dy in (-1, 1):
+
+        @beside(dy)
+        def _():
+            edges_2d(dy)
+            corners(G_A, pack, PW, PE, dy)
+
+    edges_2d(0)
     for dx in (1, -1):
         side = PW if dx > 0 else PE
         send(G_A, pack.at[:, :, pl.ds(1, 8), :], side.at[:, :, pl.ds(1, 8), :], dx, 0)
-    spread(G_2D, D2, AROUND[6:])
-    for dy in (1, -1):
-        rows(G_A, uv, 2, dy)
-    for dy in (1, -1):
-        src, dst = (8, 0) if dy > 0 else (1, 9)
-        send(G_A, pack.at[uv, :, pl.ds(src, 1), :], pack.at[uv, :, pl.ds(dst, 1), :], 0, dy)
-    send(G_A, PX.at[:, pl.ds(0, 1), :], PX.at[:, pl.ds(8, 1), :], 0, -1)
+    send(G_A, packp, PP, -1, 0)
+    for dy in (-1, 1):
+
+        @beside(dy)
+        def _():
+            whole_tiles(G_2D, D2.at[:, 1], dy)
+            rows(G_A, pl.ds(0, 2), 2, dy)
+            src, dst = (8, 0) if dy > 0 else (1, 9)
+            send(G_A, pack.at[:, :, pl.ds(src, 1), :], pack.at[:, :, pl.ds(dst, 1), :], 0, dy)
+            if dy < 0:
+                send(G_A, PX.at[:, pl.ds(0, 1), :], PX.at[:, pl.ds(8, 1), :], 0, dy)
 
     @pl.loop(0, NC)
     def _(c):
@@ -258,21 +285,32 @@
     for dx in (1, -1):
         side = TW if dx > 0 else TE
         send(G_TS, pack_ts.at[:, :, pl.ds(1, 8), :], side.at[:, :, pl.ds(1, 8), :], dx, 0)
-    corners(G_TS, pack_ts, TW, TE, uv)
-    for dy in (1, -1):
-        rows(G_TS, pl.ds(2, 2), 1, dy)
+    for dy in (-1, 1):
+
+        @beside(dy)
+        def _():
+            corners(G_TS, pack_ts, TW, TE, dy)
+            rows(G_TS, pl.ds(2, 2), 1, dy)
 
     def size(levels, count):
         return X.at[0, pl.ds(0, levels), pl.ds(0, count), :]
 
-    size_2d = size(24, 8)
-    size_a = size(K, 13)
-    size_ts = size(50, 10)
-    size_sum = size(32, 8)
-    size_b = size(49, 5)
+    def by_walls(wait, group, inner, southmost, northmost):
+        @pl.when(jnp.logical_and(has_south, has_north))
+        def _():
+            wait(group, size(*inner))
+
+        @pl.when(jnp.logical_not(has_south))
+        def _():
+            wait(group, size(*southmost))
+
+        @pl.when(jnp.logical_not(has_north))
+        def _():
+            wait(group, size(*northmost))
+
     size_c = size(62, 5)
 
-    received(G_2D, size_2d)
+    by_walls(received, G_2D, (10, 8), (6, 8), (6, 8))
     row24 = lax.broadcasted_iota(jnp.int32, (24, LANES), 0)
     lane24 = lax.broadcasted_iota(jnp.int32, (24, LANES), 1)
     slot24 = lax.rem(lane24, 8)
@@ -299,10 +337,8 @@
     def south24(x):
         return pltpu.roll(x, 1, 0)
 
-    def sides(ref, f):
-        return ref[f, 1], jnp.where(lane24 < 64, ref[f, 2], ref[f, 0])
-
-    col = [jnp.where(inside, x, 0.0) for x in sides(D2, 0)]
+    edges = jnp.where(lax.rem(lane24, 64) < 32, D2[0, 2], D2[0, 0])
+    col = [jnp.where(inside, x, 0.0) for x in (D2[0, 1], edges)]
     ocean = [x > 0.0 for x in col]
     cu = [jnp.minimum(a, b) for a, b in zip(col, ring_east(*col))]
     cv = [jnp.minimum(a, north24(a)) for a in col]
@@ -310,8 +346,11 @@
     CU[...] = cu[0]
     CV[...] = cv[0]
     for n in range(2):
-        SU4[n] = in_slots(cu[1 - n], (126, 127, 0, 1), 4)
-        SV4[n] = in_slots(cv[1 - n], (126, 127, 0, 1), 4)
+        S4[n] = jnp.where(
+            lane24 < 64,
+            in_slots(cu[1 - n], (126, 127, 0, 1), 4),
+            in_slots(cv[1 - n], (126, 127, 0, 1), 4),
+        )
 
     at_wall = jnp.where(
         jnp.logical_or(
@@ -326,8 +365,8 @@
     centre_uv = 1.0 - (DT * NU) * at_wall
     centre_ts = 1.0 - KAPPA * at_wall
 
-    received(G_A, size_a)
-    left(G_A, size_a)
+    by_walls(received, G_A, (K, 11), (51, 10), (29, 15))
+    by_walls(left, G_A, (K, 11), (29, 15), (51, 10))
 
     @pl.loop(0, NC)
     def _(c):
@@ -342,12 +381,14 @@
                 X[f, k, 10:18, :] = b
 
     class Slots:
-        def __init__(self, count, width):
+        def __init__(self, count, width, span):
             shape = (count, ROWS, LANES)
             self.lanes = lax.broadcasted_iota(jnp.int32, shape, 2)
             self.place = lax.rem(self.lanes, width)
             tile = lax.broadcasted_iota(jnp.int32, shape, 0)
-            self.level = (lax.div(self.lanes, width) + tile * (K // count)).astype(jnp.float32)
+            self.level = (lax.div(lax.rem(self.lanes, span), width) + tile * (K // count)).astype(
+                jnp.float32
+            )
             self.west, self.east = self.place == width // 2 - 1, self.place == width // 2
             self.western = self.place < width // 2
 
@@ -363,27 +404,33 @@
                 self.west, roll(z, -1), jnp.where(self.east, roll(z, 1), 0.0)
             )
 
-    by4, by8 = Slots(NM, 4), Slots(NC, 8)
-
-    def excess(f, depths, r):
-        return by4.if_wet(depths, 0, r, by4.beyond(PW, PE, f, r)) - by4.if_wet(
-            depths, 1, r, pack[f, :, r : r + 8, :]
-        )
-
-    du_s, du, du_n = [excess(0, SU4, r) for r in range(3)]
-    dv_s, dv, dv_n = [excess(1, SV4, r) for r in range(3)]
-    dp = by4.beyond(PW, PE, 2, 1) - pack[2, :, 1:9, :]
-    EU[...] = jnp.where(by4.west, roll(f4[None] * (dv + dv_s) - dp, -1), 0.0) - (
-        DT * NU
-    ) * by4.far(du, du_n + du_s)
-    EV[...] = jnp.where(by4.east, -f4[None] * roll(du + du_n, 1), 0.0) - (DT * NU) * by4.far(
-        dv, dv_n + dv_s
+    by4, by8 = Slots(NM, 4, 64), Slots(NC, 8, LANES)
+
+    def excess(r):
+        return by4.if_wet(S4, 0, r, by4.beyond(PW, PE, 0, r)) - by4.if_wet(
+            S4, 1, r, pack[0, :, r : r + 8, :]
+        )
+
+    d_s, d, d_n = [excess(r) for r in range(3)]
+    dp = PP[...] - packp[...]
+    u_half = by4.lanes < 64
+    EUV[...] = (
+        jnp.where(
+            jnp.logical_and(by4.west, u_half),
+            f4[None] * roll(d + d_s, -65) - roll(dp, -1),
+            jnp.where(
+                jnp.logical_and(by4.east, jnp.logical_not(u_half)),
+                -f4[None] * roll(d + d_n, 65),
+                0.0,
+            ),
+        )
+        - (DT * NU) * by4.far(d, d_n + d_s)
     )
 
     def momentum(c, carry):
         sum_u0, sum_v0, sum_u, sum_v = carry
         base = (c * LM).astype(jnp.float32)
-        edge_u, edge_v = EU[c], EV[c]
+        edge = EUV[c]
         cu0, cv0 = CU[8:16, :] - base, CV[8:16, :] - base
         for i in range(LM):
             k = c * LM + i
@@ -403,7 +450,7 @@
                 + (cross_u + load)
                 + (roll(zu + (cross_u - load), -1) + roll(zu, 1))
                 - (roll(au, -2) + roll(au, 2))
-                + jnp.where(edge4, unpacked(edge_u, i, 4), 0.0)
+                + jnp.where(edge4, unpacked(edge, i, 4), 0.0)
             )
             v1 = (
                 centre_uv * v
@@ -413,7 +460,7 @@
                 - (load_n - load)
                 + (roll(zv, -1) + roll(zv - cross_v, 1))
                 - (roll(av, -2) + roll(av, 2))
-                + jnp.where(edge4, unpacked(edge_v, i, 4), 0.0)
+                + jnp.where(edge4, unpacked(edge, i + 16, 4), 0.0)
             )
             u1 = jnp.where(cu0 > i, u1, 0.0)
             v1 = jnp.where(cv0 > i, v1, 0.0)
@@ -427,9 +474,25 @@
 
     sums = lax.fori_loop(0, NM, momentum, (zero,) * 4)
 
+    edge = sums[0]
     for n in range(4):
-        F2[n, 1, 8:16, :] = sums[n]
-    spread(G_SUM, F2, AROUND)
+        F2[n, 8:16, :] = sums[n]
+        near = jnp.logical_and(lane >= 32 * n - 16, lane < 32 * n + 16)
+        edge = jnp.where(near, roll(sums[n], 32 * n), edge)
+    FT[...] = edge
+    for dy in (-1, 1):
+
+        @beside(dy)
+        def _():
+            edge_tiles(G_SUM, FT, lambda n: FE.at[n], dy)
+
+    edge_tiles(G_SUM, FT, lambda n: FE.at[n], 0)
+    for dy in (-1, 1):
+
+        @beside(dy)
+        def _():
+            whole_tiles(G_SUM, F2, dy)
+
 
     @pl.loop(0, NC)
     def _(c):
@@ -444,17 +507,19 @@
     for dx in (1, -1):
         side = P1W if dx > 0 else P1E
         send(G_B, pack1, side.at[:, :, pl.ds(1, 8), :], dx, 0)
-        send(G_B, pack1.at[1, :, pl.ds(7, 1), :], side.at[1, :, pl.ds(0, 1), :], dx, 1)
-    send(G_B, V1X.at[:, pl.ds(15, 1), :], V1X.at[:, pl.ds(7, 1), :], 0, 1)
-
-    left(G_2D, size_2d)
-    left(G_TS, size_ts)
-    received(G_TS, size_ts)
-
-    edge_col = [
-        jnp.where(inside, x, 0.0)
-        for x in (jnp.where(slot24 < 4, D2[2, 0], D2[2, 2]), D2[2, 1])
-    ]
+
+    @beside(1)
+    def _():
+        for dx in (1, -1):
+            side = P1W if dx > 0 else P1E
+            send(G_B, pack1.at[1, :, pl.ds(7, 1), :], side.at[1, :, pl.ds(0, 1), :], dx, 1)
+        send(G_B, V1X.at[:, pl.ds(15, 1), :], V1X.at[:, pl.ds(7, 1), :], 0, 1)
+
+    by_walls(left, G_2D, (10, 8), (6, 8), (6, 8))
+    by_walls(left, G_TS, (50, 10), (33, 10), (33, 10))
+    by_walls(received, G_TS, (50, 10), (33, 10), (33, 10))
+
+    edge_col = [in_slots(x, (124, 125, 126, 127, 0, 1, 2, 3)) for x in (col[1], col[0])]
     edge_cu = [jnp.minimum(a, b) for a, b in zip(edge_col, ring_east(*edge_col, slot24 == 4))]
     for n in range(2):
         SC[n] = edge_col[n]
@@ -504,16 +569,17 @@
     pull_v = both(lambda o, d: o * d * (DB * GRAVITY), open_v, depth_v)
     pull_w = ring_west(*pull_u)
     ease = both(lambda o: jnp.where(o, DB, 0.0), ocean)
-    height = [jnp.where(o, x, 0.0) for o, x in zip(ocean, sides(D2, 1))]
+    height = [jnp.where(o, x, 0.0) for o, x in zip(ocean, (D2[1, 1], roll(edges, 64)))]
 
     inverse_u = both(lambda d, o: 1.0 / (d + (1.0 - o)), depth_u, open_u)
     inverse_v = both(lambda d, o: 1.0 / (d + (1.0 - o)), depth_v, open_v)
-    received(G_SUM, size_sum)
-    u0, v0, u_all, v_all = [list(sides(F2, f)) for f in range(4)]
-    push_u = both(lambda o, a, b: o * ((a - b) * (DB / DT)), open_u, u_all, u0)
-    push_v = both(lambda o, a, b: o * ((a - b) * (DB / DT)), open_v, v_all, v0)
-    trans_u = both(lambda o, a: o * a, open_u, u0)
-    trans_v = both(lambda o, a: o * a, open_v, v0)
+    by_walls(received, G_SUM, (14, 8), (8, 8), (8, 8))
+    edges = jnp.where(lax.rem(lane24, 32) < 16, FE[2], FE[0])
+    u0, v0, u_all, v_all = [[F2[n], roll(edges, -32 * n)] for n in range(4)]
+    push_u = both(lambda o, a, b: jnp.where(o > 0.0, (a - b) * (DB / DT), 0.0), open_u, u_all, u0)
+    push_v = both(lambda o, a, b: jnp.where(o > 0.0, (a - b) * (DB / DT), 0.0), open_v, v_all, v0)
+    trans_u = both(lambda o, a: jnp.where(o > 0.0, a, 0.0), open_u, u0)
+    trans_v = both(lambda o, a: jnp.where(o > 0.0, a, 0.0), open_v, v0)
     run_u = [jnp.zeros((24, LANES), jnp.float32)] * 2
     run_v = run_u
 
@@ -565,7 +631,7 @@
     DP[2] = in_slots(DV[1, 7:15, :], (126, 127, 0, 1))
     DP[3] = jnp.broadcast_to(du[:, LANES - 1 :], du.shape)
 
-    received(G_B, size_b)
+    by_walls(received, G_B, (49, 5), (20, 8), (49, 5))
     edge_u = by8.if_wet(SU, 0, 1, by8.beyond(P1W, P1E, 0, 1) + DP[0][None])
     edge_v = by8.if_wet(SV, 0, 1, by8.beyond(P1W, P1E, 1, 1) + DP[1][None])
     edge_vs = by8.if_wet(SV, 0, 0, by8.beyond(P1W, P1E, 1, 0) + DP[2][None])
@@ -630,8 +696,8 @@
     def _():
         send(G_DOWN, AD.at[:, :, pl.ds(1, 1), :], AD.at[:, :, pl.ds(9, 1), :], 0, -1)
 
-    left(G_SUM, size_sum)
-    left(G_B, size_b)
+    by_walls(left, G_SUM, (14, 8), (8, 8), (8, 8))
+    by_walls(left, G_B, (49, 5), (49, 5), (20, 8))
 
     @pl.loop(0, NC)
     def _(c):
@@ -728,7 +794,8 @@
         scratch_shapes=[
             vmem(4, K, 24, LANES),
             vmem(K, 16, LANES),
-            vmem(3, 3, 24, LANES),
+            vmem(2, 3, 24, LANES),
+            vmem(ROWS, LANES),
             vmem(ROWS, LANES, dtype=jnp.int32),
             vmem(ROWS, LANES, dtype=jnp.int32),
             vmem(24, LANES),
@@ -737,14 +804,17 @@
             vmem(2, 24, LANES),
             vmem(2, 24, LANES),
             vmem(2, 24, LANES),
-            vmem(2, 24, LANES),
-            vmem(3, NM, 16, LANES),
-            vmem(3, NM, 16, LANES),
-            vmem(3, NM, 16, LANES),
+            vmem(1, NM, 16, LANES),
+            vmem(1, NM, 16, LANES),
+            vmem(1, NM, 16, LANES),
+            vmem(NM, ROWS, LANES),
+            vmem(NM, ROWS, LANES),
             vmem(2, NC, 16, LANES),
             vmem(2, NC, 16, LANES),
             vmem(2, NC, 16, LANES),
-            vmem(4, 3, 24, LANES),
+            vmem(4, 24, LANES),
+            vmem(ROWS, LANES),
+            vmem(3, 24, LANES),
             vmem(2, 24, LANES),
             vmem(4, ROWS, LANES),
             vmem(K, ROWS, LANES),
@@ -753,7 +823,6 @@
             vmem(2, NC, 16, LANES),
             vmem(2, NC, 16, LANES),
             vmem(2, NC, 16, LANES),
-            vmem(NM, ROWS, LANES),
             vmem(NM, ROWS, LANES),
             vmem(2, NC, ROWS, LANES),
             vmem(2, K, ROWS, LANES),

time: 29.3 us -> 27.2 us (0.928)
  the two profiles are of different devices: /device:TPU:1 before, /device:TPU:97 now
where the time goes in v7:
time: 27.2 us; the launch traced here: 27.1 us
  Pallas kernels  26.5 us (97%)
  between operations  0.64 us (2%)
    pallas_call x1, Pallas kernels, per_device(): pl.pallas_call(functools.partial(kernel, nx, ny), out_shape=tuple((pltpu....  24.9 us
    pallas_call x1, Pallas kernels, per_device(): pl.pallas_call(finish, out_shape=outs, in_specs=[pl.BlockSpec(memory_spac...  1.53 us

profile of v7, /device:TPU:97, one launch (start us, length us, event | category | flops | bytes accessed | tf_op | source)
XLA Modules:
  0.0 27.1 jit_solution(13905010664191734273)
XLA Ops:
  0.6 24.9 %shard_map.110 = (f32[75,8,128]{2,1,0:T(8,128)S(1)}, f32[75,8,128]{2,1,0:T(8,128)S(1)}, f32[75,8,128]{2,1,0:T(8,128)S(1)}, f32[75,8,128]{2,1,0:T(8,128)S(1)}, f3...) custom-call(f32[75,8,128]{2,1,0:T(8,128)} %t_in.1, ...), custom_call_target="tpu_custom_call" | custom-call | tf_op jit(solution)/shard_map/pallas_call | solution.py:785
  25.6 1.5 %shard_map.111 = (f32[75,8,128]{2,1,0:T(8,128)}, f32[75,8,128]{2,1,0:T(8,128)}, f32[75,8,128]{2,1,0:T(8,128)}, f32[75,8,128]{2,1,0:T(8,128)}, f32[8,128]{1,0:T(8,128)}) custom-call(f32[75,8,128]{2,1,0:T(8,128)S(1)} %get-tuple-element.13.TN, f32[75,8,128]{2,1,0:T(8,128)S(1)} %get-tuple-element.14.SN, f32[75,8,128]{2,1,0:T(8,128)S(1)} %get-tuple-element.15.UN, ...), custom_call_target="tpu_custom_call" | custom-call | tf_op jit(solution)/shard_map/pallas_call | solution.py:841

commit v8 on v7

--- a/solution.py
+++ b/solution.py
@@ -24,8 +24,8 @@
 GRAVITY = 4.0
 DB = DT / SUBSTEPS
 
-GROUPS = 7
-G_2D, G_A, G_TS, G_SUM, G_B, G_UP, G_DOWN = range(GROUPS)
+GROUPS = 9
+G_2D, G_A, G_TS, G_SUM, G_B, G_UP, G_DOWN, G_UP_EDGE, G_DOWN_EDGE = range(GROUPS)
 
 
 def kernel(
@@ -76,14 +76,16 @@
     pack1,
     P1E,
     P1W,
+    for_east,
+    for_west,
     AD,
     EUV,
     HC,
     CE,
     CN,
     FW,
-    AO,
     HS,
+    HO,
     load_sem,
     send_sem,
     recv_sem,
@@ -240,6 +242,10 @@
                 dy,
             )
 
+    def pole(group, ref, dy):
+        src, dst = (8, 0) if dy > 0 else (1, 9)
+        send(group, ref.at[:, :, pl.ds(src, 1), :], ref.at[:, :, pl.ds(dst, 1), :], 0, dy)
+
     def edge_tiles(group, edge, aside, dy):
         for dx in (-1, 1):
             send(group, edge, aside(1 - dx).at[pl.ds(8 * (1 - dy), 8), :], dx, dy)
@@ -268,8 +274,7 @@
         def _():
             whole_tiles(G_2D, D2.at[:, 1], dy)
             rows(G_A, pl.ds(0, 2), 2, dy)
-            src, dst = (8, 0) if dy > 0 else (1, 9)
-            send(G_A, pack.at[:, :, pl.ds(src, 1), :], pack.at[:, :, pl.ds(dst, 1), :], 0, dy)
+            pole(G_A, pack, dy)
             if dy < 0:
                 send(G_A, PX.at[:, pl.ds(0, 1), :], PX.at[:, pl.ds(8, 1), :], 0, dy)
 
@@ -291,6 +296,7 @@
         def _():
             corners(G_TS, pack_ts, TW, TE, dy)
             rows(G_TS, pl.ds(2, 2), 1, dy)
+            pole(G_TS, pack_ts, dy)
 
     def size(levels, count):
         return X.at[0, pl.ds(0, levels), pl.ds(0, count), :]
@@ -307,8 +313,6 @@
         @pl.when(jnp.logical_not(has_north))
         def _():
             wait(group, size(*northmost))
-
-    size_c = size(62, 5)
 
     by_walls(received, G_2D, (10, 8), (6, 8), (6, 8))
     row24 = lax.broadcasted_iota(jnp.int32, (24, LANES), 0)
@@ -494,6 +498,10 @@
             whole_tiles(G_SUM, F2, dy)
 
 
+    @beside(1)
+    def _():
+        send(G_B, V1X.at[:, pl.ds(15, 1), :], V1X.at[:, pl.ds(7, 1), :], 0, 1)
+
     @pl.loop(0, NC)
     def _(c):
         held_u = held_v = zero
@@ -501,23 +509,27 @@
             k = c * LC + i
             held_u = jnp.where(slot == i, packed(U1B[k], i), held_u)
             held_v = jnp.where(slot == i, packed(V1X[k, 8:16, :], i), held_v)
-        pack1[0, c] = held_u
-        pack1[1, c] = held_v
-
-    for dx in (1, -1):
-        side = P1W if dx > 0 else P1E
-        send(G_B, pack1, side.at[:, :, pl.ds(1, 8), :], dx, 0)
+        pack1[0, c, 1:9, :] = held_u
+        pack1[1, c, 1:9, :] = held_v
+
+    for_east[...] = jnp.where(by8.western, pack1[0, :, 1:9, :], roll(pack1[1, :, 1:9, :], 4))
+    for_west[...] = jnp.where(by8.western, roll(pack1[0, :, 1:9, :], -4), pack1[1, :, 1:9, :])
 
     @beside(1)
     def _():
-        for dx in (1, -1):
-            side = P1W if dx > 0 else P1E
-            send(G_B, pack1.at[1, :, pl.ds(7, 1), :], side.at[1, :, pl.ds(0, 1), :], dx, 1)
-        send(G_B, V1X.at[:, pl.ds(15, 1), :], V1X.at[:, pl.ds(7, 1), :], 0, 1)
+        for dx, src, dst in ((1, for_east, P1W), (-1, for_west, P1E)):
+            send(G_B, src.at[:, pl.ds(7, 1), :], dst.at[:, pl.ds(0, 1), :], dx, 1)
+
+    for dx, src, dst in ((1, for_east, P1W), (-1, for_west, P1E)):
+        send(G_B, src, dst.at[:, pl.ds(1, 8), :], dx, 0)
+
+    @beside(1)
+    def _():
+        send(G_B, pack1.at[1, :, pl.ds(8, 1), :], pack1.at[1, :, pl.ds(0, 1), :], 0, 1)
 
     by_walls(left, G_2D, (10, 8), (6, 8), (6, 8))
-    by_walls(left, G_TS, (50, 10), (33, 10), (33, 10))
-    by_walls(received, G_TS, (50, 10), (33, 10), (33, 10))
+    by_walls(left, G_TS, (52, 10), (34, 10), (34, 10))
+    by_walls(received, G_TS, (52, 10), (34, 10), (34, 10))
 
     edge_col = [in_slots(x, (124, 125, 126, 127, 0, 1, 2, 3)) for x in (col[1], col[0])]
     edge_cu = [jnp.minimum(a, b) for a, b in zip(edge_col, ring_east(*edge_col, slot24 == 4))]
@@ -530,12 +542,17 @@
         south, here, north = [
             by8.if_wet(SC, 0, r, by8.beyond(TW, TE, f, r)) for r in range(3)
         ]
-        inner = by8.if_wet(SC, 1, 1, pack_ts[f, :, 1:9, :])
+        own_s, own, own_n = [
+            by8.if_wet(SC, 1, r, pack_ts[f, :, r : r + 8, :]) for r in range(3)
+        ]
         HC[f] = here
-        HS[f, 0] = half * (here + roll(jnp.where(by8.east, inner, here), -1))
-        HS[f, 1] = half * (inner + roll(here, -1))
+        HO[f] = own
+        HS[f, 0] = half * (here + roll(jnp.where(by8.east, own, here), -1))
+        HS[f, 1] = half * (own + roll(jnp.where(by8.east, here, own), -1))
         HS[f, 2] = half * (here + north)
         HS[f, 3] = half * (south + here)
+        HS[f, 4] = half * (own + own_n)
+        HS[f, 5] = half * (own_s + own)
 
     @pl.loop(0, NC)
     def _(c):
@@ -629,19 +646,36 @@
     DP[0] = in_slots(shift_u[1][8:16], (125, 126, 127, 0, 1))
     DP[1] = in_slots(DV[1, 8:16, :], (126, 127, 0, 1))
     DP[2] = in_slots(DV[1, 7:15, :], (126, 127, 0, 1))
-    DP[3] = jnp.broadcast_to(du[:, LANES - 1 :], du.shape)
-
-    by_walls(received, G_B, (49, 5), (20, 8), (49, 5))
-    edge_u = by8.if_wet(SU, 0, 1, by8.beyond(P1W, P1E, 0, 1) + DP[0][None])
-    edge_v = by8.if_wet(SV, 0, 1, by8.beyond(P1W, P1E, 1, 1) + DP[1][None])
-    edge_vs = by8.if_wet(SV, 0, 0, by8.beyond(P1W, P1E, 1, 0) + DP[2][None])
-    last_u = by8.if_wet(SU, 1, 1, pack1[0] + DP[3][None])
+    DP[3] = in_slots(du, (125, 126, 127, 0, 1))
+    DP[4] = in_slots(dv, (126, 127, 0, 1))
+    DP[5] = in_slots(dvs, (126, 127, 0, 1))
+
+    by_walls(received, G_B, (17, 10), (10, 8), (17, 10))
+    beyond_u = jnp.where(by8.western, P1W[:, 1:9, :], roll(P1E[:, 1:9, :], 4))
+    beyond_v = jnp.where(by8.western, roll(P1W[:, 1:9, :], -4), P1E[:, 1:9, :])
+    beyond_vs = jnp.where(by8.western, roll(P1W[:, 0:8, :], -4), P1E[:, 0:8, :])
+    edge_u = by8.if_wet(SU, 0, 1, beyond_u + DP[0][None])
+    edge_v = by8.if_wet(SV, 0, 1, beyond_v + DP[1][None])
+    edge_vs = by8.if_wet(SV, 0, 0, beyond_vs + DP[2][None])
+    own_u = by8.if_wet(SU, 1, 1, pack1[0, :, 1:9, :] + DP[3][None])
+    own_v = by8.if_wet(SV, 1, 1, pack1[1, :, 1:9, :] + DP[4][None])
+    own_vs = by8.if_wet(SV, 1, 0, pack1[1, :, 0:8, :] + DP[5][None])
     for f in range(2):
-        flux = edge_u * HS[f, 0]
-        flux_west = roll(jnp.where(by8.west, last_u * HS[f, 1], flux), 1)
+        flux, flux_own = edge_u * HS[f, 0], own_u * HS[f, 1]
+        flux_west = roll(jnp.where(by8.west, flux_own, flux), 1)
+        flux_own_west = roll(jnp.where(by8.west, flux, flux_own), 1)
         a = HC[f] - ((flux - flux_west) + (edge_v * HS[f, 2] - edge_vs * HS[f, 3]))
+        own = HO[f] - ((flux_own - flux_own_west) + (own_v * HS[f, 4] - own_vs * HS[f, 5]))
         FW[f] = flux
-        AO[f] = by8.if_wet(SC, 0, 1, a)
+        AD[f, :, 1:9, :] = by8.if_wet(SC, 0, 1, a) - by8.if_wet(SC, 1, 1, own)
+
+    @beside(1)
+    def _():
+        send(G_UP_EDGE, AD.at[:, :, pl.ds(8, 1), :], AD.at[:, :, pl.ds(0, 1), :], 0, 1)
+
+    @beside(-1)
+    def _():
+        send(G_DOWN_EDGE, AD.at[:, :, pl.ds(1, 1), :], AD.at[:, :, pl.ds(9, 1), :], 0, -1)
 
     def send_rows(c, up):
         src, dst, dy, group = (14, 6, 1, G_UP) if up else (8, 16, -1, G_DOWN)
@@ -660,7 +694,6 @@
         edges = [FW[f, c] for f in range(2)]
         cc0, cu0, cv0 = CC[8:16, :] - base, CU[8:16, :] - base, CV[8:16, :] - base
         cvs = CV[7:15, :] - base
-        held = [zero, zero]
         for i in range(LC):
             k = c * LC + i
             u = jnp.where(cu0 > i, U1B[k] + du, 0.0)
@@ -676,9 +709,6 @@
                 )
                 a = jnp.where(cc0 > i, a, 0.0)
                 AX[f, k, 8:16, :] = a
-                held[f] = jnp.where(slot == i, packed(a, i), held[f])
-        for f in range(2):
-            AD[f, c, 1:9, :] = AO[f, c] - held[f]
 
         @pl.when(has_north)
         def _():
@@ -688,16 +718,8 @@
         def _():
             send_rows(c, False)
 
-    @pl.when(has_north)
-    def _():
-        send(G_UP, AD.at[:, :, pl.ds(8, 1), :], AD.at[:, :, pl.ds(0, 1), :], 0, 1)
-
-    @pl.when(has_south)
-    def _():
-        send(G_DOWN, AD.at[:, :, pl.ds(1, 1), :], AD.at[:, :, pl.ds(9, 1), :], 0, -1)
-
     by_walls(left, G_SUM, (14, 8), (8, 8), (8, 8))
-    by_walls(left, G_B, (49, 5), (49, 5), (20, 8))
+    by_walls(left, G_B, (17, 10), (17, 10), (10, 8))
 
     @pl.loop(0, NC)
     def _(c):
@@ -712,25 +734,32 @@
                     - (roll(b, -2) + roll(b, 2))
                 )
 
-    @pl.when(has_south)
-    def _():
-        received(G_UP, size_c)
-
-    @pl.when(has_north)
-    def _():
-        received(G_DOWN, size_c)
+    edge_row = AD.at[:, :, pl.ds(0, 1), :]
+    two_rows = X.at[pl.ds(0, 2), :, pl.ds(0, 2), :]
+
+    @beside(-1)
+    def _():
+        received(G_UP_EDGE, edge_row)
+
+    @beside(1)
+    def _():
+        received(G_DOWN_EDGE, edge_row)
 
     for f in range(2):
         south, here, north = [AD[f, :, r : r + 8, :] for r in range(3)]
         EM[f] = KAPPA * by8.far(here, south + north)
 
-    @pl.when(has_north)
-    def _():
-        left(G_UP, size_c)
-
-    @pl.when(has_south)
-    def _():
-        left(G_DOWN, size_c)
+    @beside(-1)
+    def _():
+        received(G_UP, two_rows)
+        left(G_DOWN, two_rows)
+        left(G_DOWN_EDGE, edge_row)
+
+    @beside(1)
+    def _():
+        received(G_DOWN, two_rows)
+        left(G_UP, two_rows)
+        left(G_UP_EDGE, edge_row)
 
 
 def finish(TN, SN, UN, VN, HN, AX, EM, CC, t_out, s_out, u_out, v_out, h_out, TO, SO, sem):
@@ -816,20 +845,22 @@
             vmem(ROWS, LANES),
             vmem(3, 24, LANES),
             vmem(2, 24, LANES),
-            vmem(4, ROWS, LANES),
+            vmem(6, ROWS, LANES),
             vmem(K, ROWS, LANES),
             vmem(K, 16, LANES),
-            vmem(2, NC, ROWS, LANES),
             vmem(2, NC, 16, LANES),
-            vmem(2, NC, 16, LANES),
+            vmem(NC, 16, LANES),
+            vmem(NC, 16, LANES),
+            vmem(NC, ROWS, LANES),
+            vmem(NC, ROWS, LANES),
             vmem(2, NC, 16, LANES),
             vmem(NM, ROWS, LANES),
             vmem(2, NC, ROWS, LANES),
             vmem(2, K, ROWS, LANES),
             vmem(2, K, 16, LANES),
             vmem(2, NC, ROWS, LANES),
+            vmem(2, 6, NC, ROWS, LANES),
             vmem(2, NC, ROWS, LANES),
-            vmem(2, 4, NC, ROWS, LANES),
             pltpu.SemaphoreType.DMA((2,)),
             pltpu.SemaphoreType.DMA((GROUPS,)),
             pltpu.SemaphoreType.DMA((GROUPS,)),

time: 27.2 us -> 27 us (level)
  no operation moved by 1% of the time
where the time goes in v8:
time: 27 us; the launch traced here: 26.9 us
  Pallas kernels  26.3 us (97%)
  between operations  0.64 us (2%)
    pallas_call x1, Pallas kernels, per_device(): pl.pallas_call(functools.partial(kernel, nx, ny), out_shape=tuple((pltpu....  24.8 us
    pallas_call x1, Pallas kernels, per_device(): pl.pallas_call(finish, out_shape=outs, in_specs=[pl.BlockSpec(memory_spac...  1.53 us

profile of v8, /device:TPU:97, one launch (start us, length us, event | category | flops | bytes accessed | tf_op | source)
XLA Modules:
  0.0 26.9 jit_solution(16843541360116198830)
XLA Ops:
  0.6 24.8 %shard_map.110 = (f32[75,8,128]{2,1,0:T(8,128)S(1)}, f32[75,8,128]{2,1,0:T(8,128)S(1)}, f32[75,8,128]{2,1,0:T(8,128)S(1)}, f32[75,8,128]{2,1,0:T(8,128)S(1)}, f3...) custom-call(f32[75,8,128]{2,1,0:T(8,128)} %t_in.1, ...), custom_call_target="tpu_custom_call" | custom-call | tf_op jit(solution)/shard_map/pallas_call | solution.py:814
  25.4 1.5 %shard_map.111 = (f32[75,8,128]{2,1,0:T(8,128)}, f32[75,8,128]{2,1,0:T(8,128)}, f32[75,8,128]{2,1,0:T(8,128)}, f32[75,8,128]{2,1,0:T(8,128)}, f32[8,128]{1,0:T(8,128)}) custom-call(f32[75,8,128]{2,1,0:T(8,128)S(1)} %get-tuple-element.13.TN, f32[75,8,128]{2,1,0:T(8,128)S(1)} %get-tuple-element.14.SN, f32[75,8,128]{2,1,0:T(8,128)S(1)} %get-tuple-element.15.UN, ...), custom_call_target="tpu_custom_call" | custom-call | tf_op jit(solution)/shard_map/pallas_call | solution.py:872

commit v9 on v8

--- a/solution.py
+++ b/solution.py
@@ -46,6 +46,7 @@
     AX,
     EM,
     CC,
+    XM,
     X,
     PX,
     D2,
@@ -306,13 +307,15 @@
         def _():
             wait(group, size(*inner))
 
-        @pl.when(jnp.logical_not(has_south))
-        def _():
-            wait(group, size(*southmost))
-
-        @pl.when(jnp.logical_not(has_north))
-        def _():
-            wait(group, size(*northmost))
+        @pl.when(jnp.logical_not(jnp.logical_and(has_south, has_north)))
+        def _():
+            @pl.when(has_north)
+            def _():
+                wait(group, size(*southmost))
+
+            @pl.when(has_south)
+            def _():
+                wait(group, size(*northmost))
 
     by_walls(received, G_2D, (10, 8), (6, 8), (6, 8))
     row24 = lax.broadcasted_iota(jnp.int32, (24, LANES), 0)
@@ -370,7 +373,6 @@
     centre_ts = 1.0 - KAPPA * at_wall
 
     by_walls(received, G_A, (K, 11), (51, 10), (29, 15))
-    by_walls(left, G_A, (K, 11), (29, 15), (51, 10))
 
     @pl.loop(0, NC)
     def _(c):
@@ -381,8 +383,8 @@
                 k = c * LC + i
                 a = jnp.where(low > i, X[f, k, 6:14, :], 0.0)
                 b = jnp.where(high > i, X[f, k, 10:18, :], 0.0)
-                X[f, k, 6:14, :] = a
-                X[f, k, 10:18, :] = b
+                XM[f, k, 6:14, :] = a
+                XM[f, k, 10:18, :] = b
 
     class Slots:
         def __init__(self, count, width, span):
@@ -439,8 +441,8 @@
         for i in range(LM):
             k = c * LM + i
             dz = thickness(base, i)
-            uss, us, u, un, unn = [X[0, k, r : r + 8, :] for r in range(6, 11)]
-            vss, vs, v, vn, vnn = [X[1, k, r : r + 8, :] for r in range(6, 11)]
+            uss, us, u, un, unn = [XM[0, k, r : r + 8, :] for r in range(6, 11)]
+            vss, vs, v, vn, vnn = [XM[1, k, r : r + 8, :] for r in range(6, 11)]
             load, load_n = PX[k, 0:8, :], PX[k, 1:9, :]
             cross_u = f4 * (v + vs)
             cross_v = f4 * (u + un)
@@ -528,6 +530,7 @@
         send(G_B, pack1.at[1, :, pl.ds(8, 1), :], pack1.at[1, :, pl.ds(0, 1), :], 0, 1)
 
     by_walls(left, G_2D, (10, 8), (6, 8), (6, 8))
+    by_walls(left, G_A, (K, 11), (29, 15), (51, 10))
     by_walls(left, G_TS, (52, 10), (34, 10), (34, 10))
     by_walls(received, G_TS, (52, 10), (34, 10), (34, 10))
 
@@ -821,6 +824,7 @@
         in_specs=[pl.BlockSpec(memory_space=pltpu.HBM)] * 7,
         out_specs=[pl.BlockSpec(memory_space=pltpu.VMEM)] * 8,
         scratch_shapes=[
+            vmem(2, K, 24, LANES),
             vmem(4, K, 24, LANES),
             vmem(K, 16, LANES),
             vmem(2, 3, 24, LANES),

time: 27 us -> 27 us (level)
  no operation moved by 1% of the time
where the time goes in v9:
time: 27 us; the launch traced here: 26.9 us
  Pallas kernels  26.3 us (97%)
  between operations  0.64 us (2%)
    pallas_call x1, Pallas kernels, per_device(): pl.pallas_call(functools.partial(kernel, nx, ny), out_shape=tuple((pltpu....  24.8 us
    pallas_call x1, Pallas kernels, per_device(): pl.pallas_call(finish, out_shape=outs, in_specs=[pl.BlockSpec(memory_spac...  1.53 us

profile of v9, /device:TPU:97, one launch (start us, length us, event | category | flops | bytes accessed | tf_op | source)
XLA Modules:
  0.0 26.9 jit_solution(5350121008925790405)
XLA Ops:
  0.6 24.8 %shard_map.110 = (f32[75,8,128]{2,1,0:T(8,128)S(1)}, f32[75,8,128]{2,1,0:T(8,128)S(1)}, f32[75,8,128]{2,1,0:T(8,128)S(1)}, f32[75,8,128]{2,1,0:T(8,128)S(1)}, f3...) custom-call(f32[75,8,128]{2,1,0:T(8,128)} %t_in.1, ...), custom_call_target="tpu_custom_call" | custom-call | tf_op jit(solution)/shard_map/pallas_call | solution.py:817
  25.4 1.5 %shard_map.111 = (f32[75,8,128]{2,1,0:T(8,128)}, f32[75,8,128]{2,1,0:T(8,128)}, f32[75,8,128]{2,1,0:T(8,128)}, f32[75,8,128]{2,1,0:T(8,128)}, f32[8,128]{1,0:T(8,128)}) custom-call(f32[75,8,128]{2,1,0:T(8,128)S(1)} %get-tuple-element.13.TN, f32[75,8,128]{2,1,0:T(8,128)S(1)} %get-tuple-element.14.SN, f32[75,8,128]{2,1,0:T(8,128)S(1)} %get-tuple-element.15.UN, ...), custom_call_target="tpu_custom_call" | custom-call | tf_op jit(solution)/shard_map/pallas_call | solution.py:876

commit v10 on v8

--- a/solution.py
+++ b/solution.py
@@ -256,18 +256,18 @@
     def edges_2d(dy):
         edge_tiles(G_2D, ET, lambda n: D2.at[0, n], dy)
 
-    for dy in (-1, 1):
-
-        @beside(dy)
-        def _():
-            edges_2d(dy)
-            corners(G_A, pack, PW, PE, dy)
-
     edges_2d(0)
     for dx in (1, -1):
         side = PW if dx > 0 else PE
         send(G_A, pack.at[:, :, pl.ds(1, 8), :], side.at[:, :, pl.ds(1, 8), :], dx, 0)
     send(G_A, packp, PP, -1, 0)
+    for dy in (-1, 1):
+
+        @beside(dy)
+        def _():
+            edges_2d(dy)
+            corners(G_A, pack, PW, PE, dy)
+
     for dy in (-1, 1):
 
         @beside(dy)

time: 27 us -> 27 us (level)
  the two profiles are of different devices: /device:TPU:97 before, /device:TPU:1 now
where the time goes in v10:
time: 27 us; the launch traced here: 26.7 us
  Pallas kernels  26.1 us (97%)
  between operations  0.64 us (2%)
    pallas_call x1, Pallas kernels, per_device(): pl.pallas_call(functools.partial(kernel, nx, ny), out_shape=tuple((pltpu....  24.6 us
    pallas_call x1, Pallas kernels, per_device(): pl.pallas_call(finish, out_shape=outs, in_specs=[pl.BlockSpec(memory_spac...  1.53 us

profile of v10, /device:TPU:1, one launch (start us, length us, event | category | flops | bytes accessed | tf_op | source)
XLA Modules:
  0.0 26.7 jit_solution(17954707282887994824)
XLA Ops:
  0.6 24.6 %shard_map.110 = (f32[75,8,128]{2,1,0:T(8,128)S(1)}, f32[75,8,128]{2,1,0:T(8,128)S(1)}, f32[75,8,128]{2,1,0:T(8,128)S(1)}, f32[75,8,128]{2,1,0:T(8,128)S(1)}, f3...) custom-call(f32[75,8,128]{2,1,0:T(8,128)} %t_in.1, ...), custom_call_target="tpu_custom_call" | custom-call | tf_op jit(solution)/shard_map/pallas_call | solution.py:814
  25.2 1.5 %shard_map.111 = (f32[75,8,128]{2,1,0:T(8,128)}, f32[75,8,128]{2,1,0:T(8,128)}, f32[75,8,128]{2,1,0:T(8,128)}, f32[75,8,128]{2,1,0:T(8,128)}, f32[8,128]{1,0:T(8,128)}) custom-call(f32[75,8,128]{2,1,0:T(8,128)S(1)} %get-tuple-element.13.TN, f32[75,8,128]{2,1,0:T(8,128)S(1)} %get-tuple-element.14.SN, f32[75,8,128]{2,1,0:T(8,128)S(1)} %get-tuple-element.15.UN, ...), custom_call_target="tpu_custom_call" | custom-call | tf_op jit(solution)/shard_map/pallas_call | solution.py:872
